TPU v7x, 32 devices: a whole 2x2x4 slice. The times are simulated.
32 devices in a mesh: slide: 4 (over x, core), space: 8 (over z, y).
Axes of the slice: x: 2, y: 2, z: 4, core: 2. Of those that a mesh axis runs over, the one named last changes fastest.
Arguments:
- features: bfloat16 [4, 8, 8, 256, 192], P('slide', 'space'), may hold values from -16 to 16
- dw_kernel: float32 [7, 7, 192], replicated, may hold values from -1.3 to 1.3
- dw_bias: float32 [192], replicated, may hold values from -4 to 4
- ln_gain: float32 [192], replicated, may hold values from 0.5 to 1.5
- ln_bias: float32 [192], replicated, may hold values from -3 to 3
- w_in: bfloat16 [192, 768], replicated, may hold values from -0.4375 to 0.4375
- b_in: float32 [768], replicated, may hold values from -3 to 3
- w_out: bfloat16 [768, 192], replicated, may hold values from -0.21875 to 0.21875
- b_out: float32 [192], replicated, may hold values from -3 to 3
- layer_scale: float32 [192], replicated, may hold values from 0.5 to 1.5
- cotangent: bfloat16 [4, 8, 8, 256, 192], P('slide', 'space'), may hold values from -6 to 6
Outputs:
- block_output: bfloat16 [4, 8, 8, 256, 192], P('slide', 'space')
- grad_input: bfloat16 [4, 8, 8, 256, 192], P('slide', 'space')
- grad_w_in: float32 [192, 768], replicated
- grad_w_out: float32 [768, 192], replicated
- grad_kernel: float32 [7, 7, 192], replicated
All inputs are finite; a program needn't handle non-finite values.
Results may differ from a plain program's by a relative error of at most 0.0068.
Values may be sent and summed in bfloat16 or wider, within the bound.
No kernel may reach another device: no remote copies, remote signals or barrier semaphores. Data moves between devices by JAX's collectives and lax.ppermute only.
A program may use at most 64 MiB of HBM per device.

v0:
```python
import jax
import jax.numpy as jnp
from jax import lax
from jax.experimental import pallas as pl
from jax.experimental.pallas import tpu as pltpu
from jax.sharding import PartitionSpec as P

EPSILON = 1e-06
TAPS = 7
REACH = 3
GROUP = 16
BF16 = jnp.bfloat16
F32 = jnp.float32


def shifted(value, axis, steps):
    count = lax.axis_size(axis)
    initial, last = (max(0, -steps), min(count, count - steps))
    return lax.ppermute(value, axis, [(source, source + steps) for source in range(initial, last)])


def slide_lanes(value, steps):
    if steps == 0:
        return value
    width = value.shape[-1]
    lane = lax.broadcasted_iota(jnp.int32, value.shape, value.ndim - 1)
    moved = pltpu.roll(value, (-steps) % width, value.ndim - 1)
    keep = lane < width - steps if steps > 0 else lane >= -steps
    return jnp.where(keep, moved, jnp.zeros_like(moved))


def conv_row(tall_ref, taps_ref, row):
    _, chans, width = tall_ref.shape
    pieces = []
    for group in range(chans // GROUP):
        window = tall_ref[pl.ds(row, TAPS), group * GROUP : (group + 1) * GROUP, :]
        window = window.reshape(TAPS * GROUP, width)
        parts = jnp.dot(taps_ref[group], window, preferred_element_type=F32)
        total = None
        for tap in range(TAPS):
            part = slide_lanes(parts[tap * GROUP : (tap + 1) * GROUP], tap - REACH)
            total = part if total is None else total + part
        pieces.append(total)
    return jnp.concatenate(pieces, axis=0)


def block_kernel(
    x_ref, above_ref, below_ref, g_ref, taps_ref, vec_ref, bin_ref, win_ref, wint_ref, wout_ref, woutt_ref,
    out_ref, gz_ref, terms_ref,
    tall_ref, normed_ref, act_ref, gout_ref, gh_ref,
    *, scale,
):
    rows, chans, width = x_ref.shape
    hidden_units = win_ref.shape[1]
    tall_ref[0:REACH] = above_ref[...]
    tall_ref[REACH : REACH + rows] = x_ref[...]
    tall_ref[REACH + rows :] = below_ref[...]

    def one_row(row, carry):
        def vec(index):
            return vec_ref[:, index : index + 1]

        mixed = conv_row(tall_ref, taps_ref, row) + vec(0)
        centre = mixed - jnp.mean(mixed, axis=0, keepdims=True)
        inverse = lax.rsqrt(jnp.mean(centre * centre, axis=0, keepdims=True) + EPSILON)
        unit = centre * inverse
        normed = (unit * vec(1) + vec(2)).astype(BF16)
        normed_ref[row] = normed
        gout = (vec(4) * g_ref[row].astype(F32)).astype(BF16)
        gout_ref[row] = gout
        span = 256
        for start in range(0, hidden_units, span):
            part = slice(start, start + span)
            hidden = jnp.dot(wint_ref[part, :], normed, preferred_element_type=F32) + bin_ref[part, :]
            grad_act = jnp.dot(wout_ref[part, :], gout, preferred_element_type=F32)
            cdf = 0.5 * (1.0 + lax.erf(hidden * 0.7071067811865476))
            slope = cdf + hidden * jnp.exp(-0.5 * hidden * hidden) * 0.3989422804014327
            act_ref[row, part, :] = (hidden * cdf).astype(BF16)
            gh_ref[row, part, :] = (grad_act * slope).astype(BF16)
        branch = jnp.dot(woutt_ref[...], act_ref[row], preferred_element_type=F32) + vec(3)
        out_ref[row] = (x_ref[row].astype(F32) + vec(4) * branch).astype(BF16)
        grad_norm = jnp.dot(win_ref[...], gh_ref[row], preferred_element_type=F32) * vec(1)
        grad_mixed = inverse * (
            grad_norm
            - jnp.mean(grad_norm, axis=0, keepdims=True)
            - unit * jnp.mean(grad_norm * unit, axis=0, keepdims=True)
        )
        gz_ref[row] = grad_mixed.astype(BF16)
        return carry

    lax.fori_loop(0, rows, one_row, 0)

    nt = (((1,), (1,)), ((), ()))
    blocks = hidden_units // 128
    for index, (left, right) in enumerate(((normed_ref, gh_ref), (gout_ref, act_ref))):
        for start in range(0, hidden_units, 256):
            total = None
            for row in range(rows):
                term = lax.dot_general(left[row], right[row, start : start + 256, :], nt, preferred_element_type=F32)
                total = term if total is None else total + term
            for lanes in range(2):
                block = start // 128 + lanes
                terms_ref[index, block * chans : (block + 1) * chans, :] = (
                    total[:, lanes * 128 : (lanes + 1) * 128] * scale
                ).astype(BF16)
    taps_at = blocks * chans
    span = TAPS * GROUP
    same = lax.broadcasted_iota(jnp.int32, (span, span), 0) % GROUP == lax.broadcasted_iota(
        jnp.int32, (span, span), 1
    ) % GROUP
    groups = chans // GROUP
    terms_ref[:, taps_at:, :] = jnp.zeros((2, terms_ref.shape[1] - taps_at, 128), BF16)
    for group in range(groups):
        total = None
        for row in range(rows):
            grad = gz_ref[row, group * GROUP : (group + 1) * GROUP, :].astype(F32)
            moved = jnp.concatenate([slide_lanes(grad, REACH - tap) for tap in range(TAPS)], axis=0).astype(BF16)
            window = tall_ref[row : row + TAPS, group * GROUP : (group + 1) * GROUP, :].reshape(span, width)
            term = lax.dot_general(moved, window, nt, preferred_element_type=F32)
            total = term if total is None else total + term
        total = jnp.where(same, total, 0.0) * scale
        summed = jnp.sum(total.reshape(TAPS, GROUP, span), axis=1)
        summed = jnp.concatenate([summed, jnp.zeros((1, span), F32)], axis=0)
        summed = jnp.concatenate([summed, jnp.zeros((8, 128 - span), F32)], axis=1)
        half, place = divmod(group, groups // 2)
        terms_ref[half, taps_at + place * 16 : taps_at + place * 16 + 8, :] = summed.astype(BF16)


def input_kernel(gz_ref, above_ref, below_ref, g_ref, taps_ref, out_ref, tall_ref):
    rows, chans, width = gz_ref.shape
    tall_ref[0:REACH] = above_ref[...]
    tall_ref[REACH : REACH + rows] = gz_ref[...]
    tall_ref[REACH + rows :] = below_ref[...]

    def one_row(row, carry):
        out_ref[row] = (g_ref[row].astype(F32) + conv_row(tall_ref, taps_ref, row)).astype(BF16)
        return carry

    lax.fori_loop(0, rows, one_row, 0)


def final_kernel(sum_ref, win_ref, woutt_ref, taps_ref):
    chans, hidden_units = win_ref.shape
    blocks = hidden_units // 128
    for index, ref in enumerate((win_ref, woutt_ref)):
        for block in range(blocks):
            ref[:, block * 128 : (block + 1) * 128] = sum_ref[index, block * chans : (block + 1) * chans, :].astype(F32)
    groups = chans // GROUP
    for group in range(groups):
        half, place = divmod(group, groups // 2)
        at = blocks * chans + place * 16
        piece = sum_ref[half, at : at + 16, :].astype(F32)[:8]
        for tap in range(TAPS):
            taps_ref[tap, :, group * GROUP : (group + 1) * GROUP] = piece[:TAPS, tap * GROUP : (tap + 1) * GROUP]


def spread(kernel):
    chans = kernel.shape[2]
    groups = chans // GROUP
    by_group = kernel.reshape(TAPS, TAPS, groups, GROUP).transpose(2, 1, 3, 0)
    eye = jnp.eye(GROUP, dtype=F32)
    wide = by_group[..., None] * eye[None, None, :, None, :]
    return wide.reshape(groups, TAPS * GROUP, TAPS * GROUP).astype(BF16)


VMEM_LIMIT = pltpu.CompilerParams(vmem_limit_bytes=48 * 1024 * 1024)


def on_device(
    features, dw_kernel, dw_bias, ln_gain, ln_bias, w_in, b_in, w_out, b_out, layer_scale, cotangent
):
    x = jnp.swapaxes(features[0, 0], 1, 2)
    g = jnp.swapaxes(cotangent[0, 0], 1, 2)
    rows, chans, width = x.shape
    hidden_units = w_in.shape[1]
    above = shifted(x[-REACH:], "space", 1)
    below = shifted(x[:REACH], "space", -1)
    taps = spread(dw_kernel)
    back_taps = spread(dw_kernel[::-1, ::-1])
    vectors = jnp.stack([dw_bias, ln_gain, ln_bias, b_out, layer_scale], axis=1)
    devices = lax.axis_size("slide") * lax.axis_size("space")
    scale = float(devices * rows * width) ** (-0.5)
    chunk = 16
    term_rows = hidden_units // 128 * chans + chans // GROUP * 8
    unit = 16 * (devices // 2)
    term_rows = (term_rows + unit - 1) // unit * unit
    out, gz, terms = pl.pallas_call(
        lambda *refs: block_kernel(*refs, scale=scale),
        out_shape=(
            jax.ShapeDtypeStruct((rows, chans, width), BF16),
            jax.ShapeDtypeStruct((rows, chans, width), BF16),
            jax.ShapeDtypeStruct((2, term_rows, 128), BF16),
        ),
        scratch_shapes=[
            pltpu.VMEM((rows + 2 * REACH, chans, width), BF16),
            pltpu.VMEM((rows, chans, width), BF16),
            pltpu.VMEM((rows, hidden_units, width), BF16),
            pltpu.VMEM((rows, chans, width), BF16),
            pltpu.VMEM((rows, hidden_units, width), BF16),
        ],
        compiler_params=VMEM_LIMIT,
    )(x, above, below, g, taps, vectors, b_in[:, None], w_in, w_in.T, w_out, w_out.T)
    gz_above = shifted(gz[-REACH:], "space", 1)
    gz_below = shifted(gz[:REACH], "space", -1)
    axes = ("slide", "space")
    mine = 2 * term_rows // devices
    parts = lax.all_to_all(terms.reshape(devices, mine, 128), axes, 0, 0, tiled=True)
    own = jnp.sum(parts.astype(F32), axis=0).astype(BF16)
    summed = lax.all_to_all(jnp.broadcast_to(own, (devices, mine, 128)), axes, 0, 0, tiled=True)
    grad_input = pl.pallas_call(
        input_kernel,
        out_shape=jax.ShapeDtypeStruct((rows, chans, width), BF16),
        scratch_shapes=[pltpu.VMEM((rows + 2 * REACH, chans, width), BF16)],
        compiler_params=VMEM_LIMIT,
    )(gz, gz_above, gz_below, g, back_taps)
    grad_w_in, grad_w_out_t, grad_kernel = pl.pallas_call(
        final_kernel,
        out_shape=(
            jax.ShapeDtypeStruct((chans, hidden_units), F32),
            jax.ShapeDtypeStruct((chans, hidden_units), F32),
            jax.ShapeDtypeStruct((TAPS, TAPS, chans), F32),
        ),
        compiler_params=VMEM_LIMIT,
    )(summed.reshape(2, term_rows, 128))
    block_output = jnp.swapaxes(out, 1, 2)[None, None]
    grad_image = jnp.swapaxes(grad_input, 1, 2)[None, None]
    return (block_output, grad_image, grad_w_in, grad_w_out_t.T, grad_kernel)


def solution(mesh):
    placed = P("slide", "space", None, None, None)
    return jax.shard_map(
        on_device,
        mesh=mesh,
        in_specs=(placed,) + (P(),) * 9 + (placed,),
        out_specs=(placed, placed, P(), P(), P()),
        check_vma=False,
    )
```

profile of v0, /device:TPU:0, one launch (start us, length us, event | category | flops | bytes accessed | tf_op | source)
XLA Modules:
  0.0 113.8 jit_solution(6037784157345639096)
XLA Ops:
  0.6 1.9 %fusion.2 = (bf16[3,192,256]{2,1,0:T(8,128)(2,1)}, bf16[3,192,256]{2,1,0:T(8,128)(2,1)}) fusion(bf16[8,192,256]{2,1,0:T(8,128)(2,1)} %bitcast.27), kind=kLoop, calls=%fused_computation.5 | loop fusion | bytes 1179648 | tf_op jit(solution)/shard_map/slice | solution.py:177
  2.5 4.9 %collective-permute-start = (bf16[3,192,256]{2,1,0:T(8,128)(2,1)}, bf16[3,192,256]{2,1,0:T(8,128)(2,1)S(1)}, u32[]{:S(2)}, u32[]{:S(2)}) collective-permute-start(bf16[3,192,256]{2,1,0:T(8,128)(2,1)} %get-tuple-element.20), channel_id=1, source_target_pairs={{0,1},{1,2},{2,3},{3,4},{4,5},{5,6},{6,7},{8,9},{9,10},{10,11},{11... | collective-permute-start | bytes 884744 | tf_op jit(solution)/shard_map/ppermute | solution.py:19
  7.4 1.3 %collective-permute-start.1 = (bf16[3,192,256]{2,1,0:T(8,128)(2,1)}, bf16[3,192,256]{2,1,0:T(8,128)(2,1)}, u32[]{:S(2)}, u32[]{:S(2)}) collective-permute-start(bf16[3,192,256]{2,1,0:T(8,128)(2,1)} %get-tuple-element.19), channel_id=1, source_target_pairs={{1,0},{2,1},{3,2},{4,3},{5,4},{6,5},{7,6},{9,8},{10,9},{11,10},{12... | collective-permute-start | bytes 884744 | tf_op jit(solution)/shard_map/ppermute | solution.py:19
  9.6 1.0 reshape.38
  11.3 3.6 %mul.46 = f32[12,7,16,7,16]{4,3,2,1,0:T(8,128)} broadcast(f32[12,7,16,7]{3,2,1,0:T(8,128)S(1)} %copy.35), dimensions={0,1,2,3} | broadcast | bytes 639744 | tf_op jit(solution)/shard_map/mul | solution.py:162
  14.9 4.7 %mul.47 = f32[12,112,112]{2,1,0:T(8,128)} reshape(f32[12,7,16,7,16]{4,3,2,1,0:T(8,128)} %mul.46) | data formatting | bytes 1204224 | tf_op jit(solution)/shard_map/mul | solution.py:162
  20.2 3.6 %mul.40 = f32[12,7,16,7,16]{4,3,2,1,0:T(8,128)} broadcast(f32[12,7,16,7]{3,2,1,0:T(8,128)S(1)} %copy.30), dimensions={0,1,2,3} | broadcast | bytes 639744 | tf_op jit(solution)/shard_map/mul | solution.py:162
  23.9 4.9 %mul.41 = f32[12,112,112]{2,1,0:T(8,128)} reshape(f32[12,7,16,7,16]{4,3,2,1,0:T(8,128)} %mul.40) | data formatting | bytes 1204224 | tf_op jit(solution)/shard_map/mul | solution.py:162
  29.9 0.9 copy.34.refs_9_
  31.0 2.2 %multiply_convert_fusion = (bf16[12,112,112]{2,1,0:T(8,128)(2,1)}, bf16[12,112,112]{2,1,0:T(8,128)(2,1)S(1)}) fusion(f32[12,112,112]{2,1,0:T(8,128)} %mul.47, f32[112,112]{1,0:T(8,128)} %mul.43, f32[12,112,112]{2,1,0:T(8,128)} %mul.41), kind=kLoop, calls=%fused_computation | loop fusion | flops 602112 | bytes 1856512 | tf_op jit(solution)/shard_map/convert_element_type | solution.py:163
  33.9 1.0 copy-done.2
  34.9 1.0 copy-done.5
  35.9 1.0 copy-done.7
  36.9 1.0 copy-done.9
  37.8 17.1 %shard_map.146 = (bf16[8,192,256]{2,1,0:T(8,128)(2,1)}, bf16[8,192,256]{2,1,0:T(8,128)(2,1)S(1)}, bf16[2,1280,128]{2,1,0:T(8,128)(2,1)S(1)}) custom-call(bf16[8,192,256]{2,1,0:T(8,128)(2,1)S(1)} %bitcast.28, bf16[3,192,256]{2,1,0:T(8,128)(2,1)S(1)} %copy-done.9, bf16[3,192,256]{2,1,0:T(8,128)(2,1)} %collective-permute-done.1.refs_2_, ...), custom_call_target="tpu_custom_call" | custom-call | tf_op jit(solution)/shard_map/pallas_call | solution.py:187
  54.9 26.6 %all_to_all.10 = bf16[32,80,128]{2,1,0:T(8,128)(2,1)S(1)} all-to-all(bf16[32,80,128]{2,1,0:T(8,128)(2,1)S(1)} %bitcast.31), channel_id=1, replica_groups=mesh['slide'=4,'space'=8] {'slide','space'}, dimensions={0} | all-to-all | bytes 1310720 | tf_op jit(solution)/shard_map/all_to_all | solution.py:207
  81.6 0.9 broadcast_in_dim.19
  82.6 2.6 %all-to-all-start.1 = ((bf16[32,80,128]{2,1,0:T(8,128)(2,1)}), bf16[32,80,128]{2,1,0:T(8,128)(2,1)S(1)}, u32[]{:S(2)}, u32[]{:S(2)}) async-start(bf16[32,80,128]{2,1,0:T(8,128)(2,1)} %broadcast_in_dim.19), calls=%async_computation.1 | async-start | bytes 1310720 | tf_op jit(solution)/shard_map/all_to_all | solution.py:209
  85.3 3.6 %collective-permute-start.2 = (bf16[3,192,256]{2,1,0:T(8,128)(2,1)S(1)}, bf16[3,192,256]{2,1,0:T(8,128)(2,1)S(1)}, u32[]{:S(2)}, u32[]{:S(2)}) collective-permute-start(bf16[3,192,256]{2,1,0:T(8,128)(2,1)S(1)} %get-tuple-element.18), channel_id=1, source_target_pairs={{0,1},{1,2},{2,3},{3,4},{4,5},{5,6},{6,7},{8,9},{9,10},{10,11},{11... | collective-permute-start | bytes 884744 | tf_op jit(solution)/shard_map/ppermute | solution.py:19
  88.8 1.3 %collective-permute-start.3 = (bf16[3,192,256]{2,1,0:T(8,128)(2,1)S(1)}, bf16[3,192,256]{2,1,0:T(8,128)(2,1)S(1)}, u32[]{:S(2)}, u32[]{:S(2)}) collective-permute-start(bf16[3,192,256]{2,1,0:T(8,128)(2,1)S(1)} %get-tuple-element.17), channel_id=1, source_target_pairs={{1,0},{2,1},{3,2},{4,3},{5,4},{6,5},{7,6},{9,8},{10,9},{11,10},{12... | collective-permute-start | bytes 884744 | tf_op jit(solution)/shard_map/ppermute | solution.py:19
  90.1 16.4 %collective-permute-done.2.above_ref = bf16[3,192,256]{2,1,0:T(8,128)(2,1)S(1)} collective-permute-done((bf16[3,192,256]{2,1,0:T(8,128)(2,1)S(1)}, bf16[3,192,256]{2,1,0:T(8,128)(2,1)S(1)}, u32[]{:S(2)}, u32[]{:S(2)}) %collective-permute-start.2) | collective-permute-done | bytes 294944 | tf_op jit(solution)/shard_map/ppermute | solution.py:19
  106.5 1.0 copy-done.3
  107.5 5.2 %shard_map.147 = bf16[8,192,256]{2,1,0:T(8,128)(2,1)} custom-call(bf16[8,192,256]{2,1,0:T(8,128)(2,1)S(1)} %get-tuple-element.12.gz_ref, bf16[3,192,256]{2,1,0:T(8,128)(2,1)S(1)} %collective-permute-done.2.above_ref, bf16[3,192,256]{2,1,0:T(8,128)(2,1)S(1)} %collective-permute-done.3.below_ref, bf16[8,192,256]{2,1,0:T(8,128)(2,1)S(1)} %bitcast.25, ...), custom_call_target="tpu_custom_call" | custom-call | tf_op jit(solution)/shard_map/pallas_call | solution.py:210
  112.7 1.1 shard_map.148
  (44 shorter events, 4.3 us)
Async XLA Ops:
  2.5 30.7 %collective-permute-start = (bf16[3,192,256]{2,1,0:T(8,128)(2,1)}, bf16[3,192,256]{2,1,0:T(8,128)(2,1)S(1)}, u32[]{:S(2)}, u32[]{:S(2)}) collective-permute-start(bf16[3,192,256]{2,1,0:T(8,128)(2,1)} %get-tuple-element.20), channel_id=1, source_target_pairs={{0,1},{1,2},{2,3},{3,4},{4,5},{5,6},{6,7},{8,9},{9,10},{10,11},{11... | collective-permute-start | bytes 884744 | tf_op jit(solution)/shard_map/ppermute | solution.py:19
  7.4 26.5 %collective-permute-start.1 = (bf16[3,192,256]{2,1,0:T(8,128)(2,1)}, bf16[3,192,256]{2,1,0:T(8,128)(2,1)}, u32[]{:S(2)}, u32[]{:S(2)}) collective-permute-start(bf16[3,192,256]{2,1,0:T(8,128)(2,1)} %get-tuple-element.19), channel_id=1, source_target_pairs={{1,0},{2,1},{3,2},{4,3},{5,4},{6,5},{7,6},{9,8},{10,9},{11,10},{12... | collective-permute-start | bytes 884744 | tf_op jit(solution)/shard_map/ppermute | solution.py:19
  20.2 9.4 %copy-start.4 = (bf16[192,768]{1,0:T(8,128)(2,1)S(1)}, bf16[192,768]{1,0:T(8,128)(2,1)}, u32[]{:S(2)}) copy-start(bf16[192,768]{1,0:T(8,128)(2,1)} %refs_7_.1) | copy-start | bytes 884740
  20.2 9.6 %copy-start.10 = (f32[768]{0:T(1024)S(1)}, f32[768]{0:T(1024)}, u32[]{:S(2)}) copy-start(f32[768]{0:T(1024)} %param.17) | copy-start | bytes 9220
  23.8 6.1 %copy-start.6 = (bf16[768,192]{0,1:T(8,128)(2,1)S(1)}, bf16[768,192]{0,1:T(8,128)(2,1)}, u32[]{:S(2)}) copy-start(bf16[768,192]{0,1:T(8,128)(2,1)} %param.18) | copy-start | bytes 884740
  23.8 7.0 %copy-start.11 = (f32[192]{0:T(256)S(1)}, f32[192]{0:T(256)}, u32[]{:S(2)}) copy-start(f32[192]{0:T(256)} %param.13) | copy-start | bytes 2308
  23.8 7.0 %copy-start.12 = (f32[192]{0:T(256)S(1)}, f32[192]{0:T(256)}, u32[]{:S(2)}) copy-start(f32[192]{0:T(256)} %param.14) | copy-start | bytes 2308
  23.8 7.0 %copy-start.13 = (f32[192]{0:T(256)S(1)}, f32[192]{0:T(256)}, u32[]{:S(2)}) copy-start(f32[192]{0:T(256)} %param.15) | copy-start | bytes 2308
  23.8 7.0 %copy-start.14 = (f32[192]{0:T(256)S(1)}, f32[192]{0:T(256)}, u32[]{:S(2)}) copy-start(f32[192]{0:T(256)} %param.19) | copy-start | bytes 2308
  23.8 7.0 %copy-start.15 = (f32[192]{0:T(256)S(1)}, f32[192]{0:T(256)}, u32[]{:S(2)}) copy-start(f32[192]{0:T(256)} %param.20) | copy-start | bytes 2308
  23.8 10.1 %copy-start = (bf16[1,1,8,256,192]{3,4,2,1,0:T(8,128)(2,1)S(1)}, bf16[1,1,8,256,192]{3,4,2,1,0:T(8,128)(2,1)}, u32[]{:S(2)}) copy-start(bf16[1,1,8,256,192]{3,4,2,1,0:T(8,128)(2,1)} %param.21) | copy-start | bytes 2359300
  23.8 10.1 %copy-start.1 = (bf16[1,1,8,256,192]{3,4,2,1,0:T(8,128)(2,1)S(1)}, bf16[1,1,8,256,192]{3,4,2,1,0:T(8,128)(2,1)}, u32[]{:S(2)}) copy-start(bf16[1,1,8,256,192]{3,4,2,1,0:T(8,128)(2,1)} %param.11) | copy-start | bytes 2359300
  33.2 0.7 copy-start.8
  33.9 1.0 copy-start.2
  34.9 1.0 copy-start.5
  35.9 1.0 copy-start.7
  36.8 1.0 copy-start.9
  82.6 30.1 %all-to-all-start.1 = ((bf16[32,80,128]{2,1,0:T(8,128)(2,1)}), bf16[32,80,128]{2,1,0:T(8,128)(2,1)S(1)}, u32[]{:S(2)}, u32[]{:S(2)}) async-start(bf16[32,80,128]{2,1,0:T(8,128)(2,1)} %broadcast_in_dim.19), calls=%async_computation.1 | async-start | bytes 1310720 | tf_op jit(solution)/shard_map/all_to_all | solution.py:209
  85.3 21.3 %collective-permute-start.2 = (bf16[3,192,256]{2,1,0:T(8,128)(2,1)S(1)}, bf16[3,192,256]{2,1,0:T(8,128)(2,1)S(1)}, u32[]{:S(2)}, u32[]{:S(2)}) collective-permute-start(bf16[3,192,256]{2,1,0:T(8,128)(2,1)S(1)} %get-tuple-element.18), channel_id=1, source_target_pairs={{0,1},{1,2},{2,3},{3,4},{4,5},{5,6},{6,7},{8,9},{9,10},{10,11},{11... | collective-permute-start | bytes 884744 | tf_op jit(solution)/shard_map/ppermute | solution.py:19
  88.8 17.7 %collective-permute-start.3 = (bf16[3,192,256]{2,1,0:T(8,128)(2,1)S(1)}, bf16[3,192,256]{2,1,0:T(8,128)(2,1)S(1)}, u32[]{:S(2)}, u32[]{:S(2)}) collective-permute-start(bf16[3,192,256]{2,1,0:T(8,128)(2,1)S(1)} %get-tuple-element.17), channel_id=1, source_target_pairs={{1,0},{2,1},{3,2},{4,3},{5,4},{6,5},{7,6},{9,8},{10,9},{11,10},{12... | collective-permute-start | bytes 884744 | tf_op jit(solution)/shard_map/ppermute | solution.py:19
  106.5 1.0 copy-start.3
where the time goes:
time: 115 us; the launch traced here: 114 us
  local copies, waits for them, and re-layouts  30.6 us (27%)
  blocking collectives  26.6 us (23%)
  Pallas kernels  23.4 us (20%)
  waiting for transfers between devices  16.4 us (14%)
  starting transfers between devices  13.7 us (12%)
  other arithmetic  2.29 us (2%)
    all_to_all x1, blocking collectives, on_device(): lax.all_to_all(terms.reshape(devices, mine, 128), axes, 0, 0, tiled=True)  26.6 us
    mul x6, local copies, waits for them, and re-layouts, spread(): wide = by_group[..., None] * eye[None, None, :, None, :]  17.6 us
    pallas_call x1, Pallas kernels, on_device(): pl.pallas_call(lambda *refs: block_kernel(*refs, scale=scale), out_shape=...  17.1 us
    ppermute x4, waiting for transfers between devices, shifted(): lax.ppermute(value, axis, [(source, source + steps) for source in range(i...  16.4 us
    ppermute x4, starting transfers between devices, shifted(): lax.ppermute(value, axis, [(source, source + steps) for source in range(i...  11 us
    unnamed x34, local copies, waits for them, and re-layouts  6.7 us
    pallas_call x1, Pallas kernels, on_device(): pl.pallas_call(input_kernel, out_shape=jax.ShapeDtypeStruct((rows, chans,...  5.2 us
    all_to_all x1, starting transfers between devices, on_device(): lax.all_to_all(jnp.broadcast_to(own, (devices, mine, 128)), axes, 0, 0, t...  2.61 us
  transfers between devices with their start and end apart: 5, of which 1 were waited for; matrix products, arithmetic and copies ran while one was open for 21% of the time, Pallas kernels for 5%

commit v1 on v0

v1 whole, which is shorter than its diff:
```python
import jax
import jax.numpy as jnp
from jax import lax
from jax.experimental import pallas as pl
from jax.experimental.pallas import tpu as pltpu
from jax.sharding import Mesh
from jax.sharding import PartitionSpec as P

EPSILON = 1e-06
TAPS = 7
REACH = 3
GROUP = 16
BF16 = jnp.bfloat16
F32 = jnp.float32


def shifted(value, axis, steps):
    count = lax.axis_size(axis)
    initial, last = (max(0, -steps), min(count, count - steps))
    return lax.ppermute(value, axis, [(source, source + steps) for source in range(initial, last)])


def slide_lanes(value, steps):
    if steps == 0:
        return value
    width = value.shape[-1]
    lane = lax.broadcasted_iota(jnp.int32, value.shape, value.ndim - 1)
    moved = pltpu.roll(value, (-steps) % width, value.ndim - 1)
    keep = lane < width - steps if steps > 0 else lane >= -steps
    return jnp.where(keep, moved, jnp.zeros_like(moved))


def conv_row(tall_ref, taps_ref, row):
    _, chans, width = tall_ref.shape
    pieces = []
    for group in range(chans // GROUP):
        window = tall_ref[pl.ds(row, TAPS), group * GROUP : (group + 1) * GROUP, :]
        window = window.reshape(TAPS * GROUP, width)
        window = jnp.concatenate([window, window], axis=0)
        parts = jnp.dot(taps_ref[group], window, preferred_element_type=F32)
        total = None
        for tap in range(TAPS):
            part = slide_lanes(parts[tap * GROUP : (tap + 1) * GROUP], tap - REACH)
            total = part if total is None else total + part
        pieces.append(total)
    return jnp.concatenate(pieces, axis=0)


def spread_taps(kernel_ref, taps_ref, flipped):
    chans = kernel_ref.shape[2]
    span = TAPS * GROUP
    same = lax.broadcasted_iota(jnp.int32, (GROUP, span), 0) == lax.broadcasted_iota(
        jnp.int32, (GROUP, span), 1
    ) % GROUP
    for group in range(chans // GROUP):
        lanes = slice(group * GROUP, (group + 1) * GROUP)
        order = [TAPS - 1 - tap if flipped else tap for tap in range(TAPS)]
        across = jnp.concatenate([kernel_ref[tap, :, lanes] for tap in order], axis=1)
        for tap in range(TAPS):
            source = TAPS - 1 - tap if flipped else tap
            wide = jnp.broadcast_to(across[source : source + 1], (GROUP, span))
            wide = jnp.where(same, wide, 0.0)
            high = wide.astype(BF16)
            low = (wide - high.astype(F32)).astype(BF16)
            taps_ref[group, tap * GROUP : (tap + 1) * GROUP, :] = jnp.concatenate([high, low], axis=1)


def one_row(row, tall_ref, g_ref, taps_ref, weights, out_ref, gz_ref, kept):
    vec_ref, bin_ref, win_ref, wint_ref, wout_ref, woutt_ref = weights
    normed_ref, act_ref, gout_ref, gh_ref = kept

    def vec(index):
        return vec_ref[:, index : index + 1]

    hidden_units = win_ref.shape[1]
    mixed = conv_row(tall_ref, taps_ref, row) + vec(0)
    centre = mixed - jnp.mean(mixed, axis=0, keepdims=True)
    inverse = lax.rsqrt(jnp.mean(centre * centre, axis=0, keepdims=True) + EPSILON)
    unit = centre * inverse
    normed = (unit * vec(1) + vec(2)).astype(BF16)
    normed_ref[row] = normed
    gout = (vec(4) * g_ref[row].astype(F32)).astype(BF16)
    gout_ref[row] = gout
    span = 256
    for start in range(0, hidden_units, span):
        part = slice(start, start + span)
        hidden = jnp.dot(wint_ref[part, :], normed, preferred_element_type=F32) + bin_ref[part, :]
        grad_act = jnp.dot(wout_ref[part, :], gout, preferred_element_type=F32)
        cdf = 0.5 * (1.0 + lax.erf(hidden * 0.7071067811865476))
        slope = cdf + hidden * jnp.exp(-0.5 * hidden * hidden) * 0.3989422804014327
        act_ref[row, part, :] = (hidden * cdf).astype(BF16)
        gh_ref[row, part, :] = (grad_act * slope).astype(BF16)
    branch = jnp.dot(woutt_ref[...], act_ref[row], preferred_element_type=F32) + vec(3)
    out_ref[row] = (tall_ref[row + REACH].astype(F32) + vec(4) * branch).astype(BF16)
    grad_norm = jnp.dot(win_ref[...], gh_ref[row], preferred_element_type=F32) * vec(1)
    grad_mixed = inverse * (
        grad_norm
        - jnp.mean(grad_norm, axis=0, keepdims=True)
        - unit * jnp.mean(grad_norm * unit, axis=0, keepdims=True)
    )
    gz_ref[row] = grad_mixed.astype(BF16)


def all_rows(tall_ref, g_ref, taps_ref, weights, out_ref, gz_ref, kept):
    def step(row, carry):
        one_row(row, tall_ref, g_ref, taps_ref, weights, out_ref, gz_ref, kept)
        return carry

    lax.fori_loop(0, out_ref.shape[0], step, 0)


NT = (((1,), (1,)), ((), ()))


def total_of(terms):
    total = terms[0]
    for term in terms[1:]:
        total = total + term
    return total


def weight_terms(kept, start, width, index):
    normed_ref, act_ref, gout_ref, gh_ref = kept
    left, right = ((normed_ref, gh_ref), (gout_ref, act_ref))[index]
    return total_of(
        [
            lax.dot_general(left[row], right[row, start : start + width, :], NT, preferred_element_type=F32)
            for row in range(left.shape[0])
        ]
    )


def tap_terms(tall_ref, gz_ref, group):
    span = TAPS * GROUP
    same = lax.broadcasted_iota(jnp.int32, (span, span), 0) % GROUP == lax.broadcasted_iota(
        jnp.int32, (span, span), 1
    ) % GROUP
    lanes = slice(group * GROUP, (group + 1) * GROUP)
    terms = []
    for row in range(gz_ref.shape[0]):
        grad = gz_ref[row, lanes, :].astype(F32)
        moved = jnp.concatenate([slide_lanes(grad, REACH - tap) for tap in range(TAPS)], axis=0).astype(BF16)
        window = tall_ref[row : row + TAPS, lanes, :].reshape(span, -1)
        terms.append(lax.dot_general(moved, window, NT, preferred_element_type=F32))
    total = jnp.where(same, total_of(terms), 0.0)
    summed = jnp.sum(total.reshape(TAPS, GROUP, span), axis=1)
    return jnp.concatenate([summed, jnp.zeros((1, span), F32)], axis=0)


def inner_kernel(
    x_ref, g_ref, kernel_ref, vec_ref, bin_ref, win_ref, wint_ref, wout_ref, woutt_ref,
    taps_ref, back_ref, out_ref, gz_ref, dwin_ref, dwout_ref, dtaps_ref,
    *kept,
):
    hidden_units = win_ref.shape[1]
    spread_taps(kernel_ref, taps_ref, False)
    spread_taps(kernel_ref, back_ref, True)
    weights = (vec_ref, bin_ref, win_ref, wint_ref, wout_ref, woutt_ref)
    all_rows(x_ref, g_ref.at[pl.ds(REACH, out_ref.shape[0])], taps_ref, weights, out_ref, gz_ref, kept)
    for start in range(0, hidden_units, 256):
        for index, ref in enumerate((dwin_ref, dwout_ref)):
            ref[:, start : start + 256] = weight_terms(kept, start, 256, index)
    for group in range(x_ref.shape[1] // GROUP):
        dtaps_ref[group] = tap_terms(x_ref, gz_ref, group)


def upper_kernel(
    x_ref, above_ref, g_ref, taps_ref, vec_ref, bin_ref, win_ref, wint_ref, wout_ref, woutt_ref,
    dwin_in_ref, dwout_in_ref, dtaps_in_ref,
    out_ref, gz_ref, dwin_ref, dwout_ref, dtaps_ref,
    tall_ref, *kept,
):
    hidden_units = win_ref.shape[1]
    tall_ref[0:REACH] = above_ref[...]
    tall_ref[REACH:] = x_ref[0 : 2 * REACH]
    weights = (vec_ref, bin_ref, win_ref, wint_ref, wout_ref, woutt_ref)
    all_rows(tall_ref, g_ref.at[pl.ds(0, REACH)], taps_ref, weights, out_ref, gz_ref, kept)
    for start in range(0, hidden_units, 256):
        part = slice(start, start + 256)
        for index, (ref, before_ref) in enumerate(((dwin_ref, dwin_in_ref), (dwout_ref, dwout_in_ref))):
            ref[:, part] = weight_terms(kept, start, 256, index) + before_ref[:, part]
    for group in range(x_ref.shape[1] // GROUP):
        dtaps_ref[group] = tap_terms(tall_ref, gz_ref, group) + dtaps_in_ref[group]


def lower_kernel(
    x_ref, below_ref, g_ref, taps_ref, vec_ref, bin_ref, win_ref, wint_ref, wout_ref, woutt_ref,
    out_ref, gz_ref, tall_ref, *kept,
):
    rows = x_ref.shape[0]
    tall_ref[0 : 2 * REACH] = x_ref[rows - 2 * REACH :]
    tall_ref[2 * REACH :] = below_ref[...]
    weights = (vec_ref, bin_ref, win_ref, wint_ref, wout_ref, woutt_ref)
    all_rows(tall_ref, g_ref.at[pl.ds(rows - REACH, REACH)], taps_ref, weights, out_ref, gz_ref, kept)


def terms_kernel(
    core_ref, tall_ref, gz_ref, normed_ref, act_ref, gout_ref, gh_ref, dwin_ref, dwout_ref, dtaps_ref,
    keep_ref, send_ref, halves_ref, *, scale,
):
    chans, hidden_units = dwin_ref.shape
    kept = (normed_ref, act_ref, gout_ref, gh_ref)
    blocks = hidden_units // 128
    for index, ref in enumerate((dwin_ref, dwout_ref)):
        for start in range(0, hidden_units, 256):
            total = (weight_terms(kept, start, 256, index) + ref[:, start : start + 256]) * scale
            for lanes in range(2):
                block = start // 128 + lanes
                halves_ref[index, block * chans : (block + 1) * chans, :] = total[
                    :, lanes * 128 : (lanes + 1) * 128
                ].astype(BF16)
    at = blocks * chans
    groups = chans // GROUP
    halves_ref[:, at:, :] = jnp.zeros((2, halves_ref.shape[1] - at, 128), BF16)
    span = TAPS * GROUP
    for pair in range(groups // 2):
        both = [
            (tap_terms(tall_ref, gz_ref, group) + dtaps_ref[group]) * scale for group in (2 * pair, 2 * pair + 1)
        ]
        both = jnp.concatenate(both, axis=0)
        both = jnp.concatenate([both, jnp.zeros((16, 128 - span), F32)], axis=1)
        half, place = divmod(pair, groups // 4)
        halves_ref[half, at + place * 16 : at + (place + 1) * 16, :] = both.astype(BF16)
    core = core_ref[0]
    keep_ref[...] = halves_ref[core]
    send_ref[...] = halves_ref[1 - core]


def input_kernel(
    out_upper_ref, out_inner_ref, out_lower_ref, gz_upper_ref, gz_inner_ref, gz_lower_ref,
    above_ref, below_ref, g_ref, taps_ref,
    out_ref, grad_ref, tall_ref,
):
    rows = g_ref.shape[0]
    at = 0
    for ref in (above_ref, gz_upper_ref, gz_inner_ref, gz_lower_ref, below_ref):
        tall_ref[at : at + ref.shape[0]] = ref[...]
        at += ref.shape[0]
    at = 0
    for ref in (out_upper_ref, out_inner_ref, out_lower_ref):
        out_ref[at : at + ref.shape[0]] = ref[...]
        at += ref.shape[0]

    def step(row, carry):
        grad_ref[row] = (g_ref[row].astype(F32) + conv_row(tall_ref, taps_ref, row)).astype(BF16)
        return carry

    lax.fori_loop(0, rows, step, 0)


def final_kernel(place_ref, mine_ref, other_ref, win_ref, woutt_ref, taps_ref, all_ref):
    core, quarter = place_ref[0], place_ref[1]
    chans, hidden_units = win_ref.shape
    size = mine_ref.shape[1]
    for turn in range(4):
        at = pl.ds(pl.multiple_of((quarter ^ turn) * size, 16), size)
        all_ref[core, at, :] = mine_ref[turn]
        all_ref[1 - core, at, :] = other_ref[turn]
    blocks = hidden_units // 128
    for index, ref in enumerate((win_ref, woutt_ref)):
        for block in range(blocks):
            ref[:, block * 128 : (block + 1) * 128] = all_ref[index, block * chans : (block + 1) * chans, :].astype(F32)
    groups = chans // GROUP
    for pair in range(groups // 2):
        half, place = divmod(pair, groups // 4)
        at = blocks * chans + place * 16
        both = all_ref[half, at : at + 16, :].astype(F32)
        for side in range(2):
            group = 2 * pair + side
            piece = both[side * 8 : side * 8 + 8]
            for tap in range(TAPS):
                taps_ref[tap, :, group * GROUP : (group + 1) * GROUP] = piece[:TAPS, tap * GROUP : (tap + 1) * GROUP]


def edge_kernel(x_ref, edge_ref, sem, *, start):
    copy = pltpu.make_async_copy(x_ref.at[pl.ds(start, REACH)], edge_ref, sem)
    copy.start()
    copy.wait()


PARAMS = pltpu.CompilerParams(vmem_limit_bytes=20 * 1024 * 1024)
SMALL = pltpu.CompilerParams(vmem_limit_bytes=4 * 1024 * 1024)
IN_VMEM = pl.BlockSpec(memory_space=pltpu.VMEM)
IN_SMEM = pl.BlockSpec(memory_space=pltpu.SMEM)


def swap(value, axis, mask):
    count = lax.axis_size(axis)
    return lax.ppermute(value, axis, [(source, source ^ mask) for source in range(count)])


def added(*terms):
    terms = [term.astype(F32) for term in terms]
    while len(terms) > 1:
        terms = [terms[at] + terms[at + 1] for at in range(0, len(terms), 2)]
    return terms[0].astype(BF16)


def on_device(
    features, dw_kernel, dw_bias, ln_gain, ln_bias, w_in, b_in, w_out, b_out, layer_scale, cotangent
):
    core = lax.axis_index("core").astype(jnp.uint32)
    quarter = (2 * lax.axis_index("x") + lax.axis_index("space") % 2).astype(jnp.uint32)
    turns = [quarter ^ turn for turn in range(4)]
    place = jnp.stack([core, quarter]).astype(jnp.int32)
    features, place, *turns = lax.optimization_barrier((features, place, *turns))
    x = jnp.swapaxes(features[0, 0], 1, 2)
    g = jnp.swapaxes(cotangent[0, 0], 1, 2)
    rows, chans, width = x.shape
    hidden_units = w_in.shape[1]
    strips = lax.axis_size("space")
    narrow = jax.ShapeDtypeStruct((REACH, chans, width), BF16)
    image = jax.ShapeDtypeStruct((rows, chans, width), BF16)

    def edge(start):
        return pl.pallas_call(
            lambda *refs: edge_kernel(*refs, start=start),
            out_shape=narrow,
            in_specs=[pl.BlockSpec(memory_space=pl.ANY)],
            out_specs=IN_VMEM,
            scratch_shapes=[pltpu.SemaphoreType.DMA(())],
            compiler_params=SMALL,
        )(x)

    above = shifted(edge(rows - REACH), "space", 1)
    vectors = jnp.stack([dw_bias, ln_gain, ln_bias, b_out, layer_scale], axis=1)
    weights = (vectors, b_in[:, None], w_in, w_in.T, w_out, w_out.T)
    devices = lax.axis_size("x") * lax.axis_size("core") * strips
    scale = float(devices * rows * width) ** (-0.5)
    groups = chans // GROUP
    span = TAPS * GROUP
    inner = rows - 2 * REACH

    tall = jax.ShapeDtypeStruct((3 * REACH, chans, width), BF16)

    def kept(count):
        small = jax.ShapeDtypeStruct((count, chans, width), BF16)
        large = jax.ShapeDtypeStruct((count, hidden_units, width), BF16)
        return (small, large, small, large)

    def scratch(shapes):
        return [pltpu.VMEM(shape.shape, shape.dtype) for shape in shapes]

    middle = jax.ShapeDtypeStruct((inner, chans, width), BF16)
    spread = jax.ShapeDtypeStruct((groups, span, 2 * span), BF16)
    matrix = jax.ShapeDtypeStruct((chans, hidden_units), F32)
    terms = (matrix, matrix, jax.ShapeDtypeStruct((groups, 8, span), F32))
    taps, back_taps, out_inner, gz_inner, *inner_terms = pl.pallas_call(
        inner_kernel,
        out_shape=(spread, spread, middle, middle, *terms),
        in_specs=[IN_VMEM] * 9,
        out_specs=(IN_VMEM,) * 7,
        scratch_shapes=scratch(kept(inner)),
        compiler_params=PARAMS,
    )(x, g, dw_kernel, *weights)
    above, top, out_inner = lax.optimization_barrier((above, edge(0), out_inner))
    below = shifted(top, "space", -1)
    half_rows = hidden_units // 128 * chans + groups // 2 * 8
    half_rows = (half_rows + 63) // 64 * 64
    half = jax.ShapeDtypeStruct((half_rows, 128), BF16)
    out_upper, gz_upper, *upper_terms = pl.pallas_call(
        upper_kernel,
        out_shape=(narrow, narrow, *terms),
        in_specs=[IN_VMEM] * 13,
        out_specs=(IN_VMEM,) * 5,
        scratch_shapes=scratch((tall, *kept(REACH))),
        compiler_params=PARAMS,
    )(x, above, g, taps, *weights, *inner_terms)
    gz_below = shifted(gz_upper, "space", -1)
    out_lower, gz_lower, *lower_kept = pl.pallas_call(
        lower_kernel,
        out_shape=(narrow, narrow, tall, *kept(REACH)),
        in_specs=[IN_VMEM] * 10,
        out_specs=(IN_VMEM,) * 7,
        compiler_params=PARAMS,
    )(x, below, g, taps, *weights)
    gz_above = shifted(gz_lower, "space", 1)
    keep, send = pl.pallas_call(
        lambda *refs: terms_kernel(*refs, scale=scale),
        out_shape=(half, half),
        in_specs=[IN_SMEM] + [IN_VMEM] * 9,
        out_specs=(IN_VMEM,) * 2,
        scratch_shapes=[pltpu.VMEM((2, half_rows, 128), BF16)],
        compiler_params=PARAMS,
    )(place, lower_kept[0], gz_lower, *lower_kept[1:], *upper_terms)

    summed = added(keep, swap(send, "core", 1)).reshape(4, half_rows // 4, 128)

    def at(turn):
        return lax.dynamic_index_in_dim(summed, turns[turn], 0, keepdims=False)

    def partner(value, turn):
        return swap(value, ("x", "space"), (turn >> 1) * strips | (turn & 1))

    own = added(at(0), *[partner(at(turn), turn) for turn in (1, 2, 3)])
    out, grad_input = pl.pallas_call(
        input_kernel,
        out_shape=(image, image),
        in_specs=[IN_VMEM] * 10,
        out_specs=(IN_VMEM, IN_VMEM),
        scratch_shapes=[pltpu.VMEM((rows + 2 * REACH, chans, width), BF16)],
        compiler_params=PARAMS,
    )(out_upper, out_inner, out_lower, gz_upper, gz_inner, gz_lower, gz_above, gz_below, g, back_taps)
    bit = 2
    while bit < strips:
        masks = (bit, 2 * bit, 3 * bit) if 2 * bit < strips else (bit,)
        own = added(own, *[swap(own, "space", mask) for mask in masks])
        bit *= 4
    own, grad_input = lax.optimization_barrier((own, grad_input))
    mine = jnp.stack([own] + [partner(own, turn) for turn in (1, 2, 3)])
    other = swap(mine, "core", 1)
    grad_w_in, grad_w_out_t, grad_kernel = pl.pallas_call(
        final_kernel,
        out_shape=(matrix, matrix, jax.ShapeDtypeStruct((TAPS, TAPS, chans), F32)),
        in_specs=[IN_SMEM, IN_VMEM, IN_VMEM],
        out_specs=(IN_VMEM,) * 3,
        scratch_shapes=[pltpu.VMEM((2, half_rows, 128), BF16)],
        compiler_params=PARAMS,
    )(place, mine, other)
    block_output = jnp.swapaxes(out, 1, 2)[None, None]
    grad_image = jnp.swapaxes(grad_input, 1, 2)[None, None]
    return (block_output, grad_image, grad_w_in, grad_w_out_t.T, grad_kernel)


def solution(mesh):
    slides, strips = mesh.devices.shape
    split = Mesh(mesh.devices.reshape(slides // 2, 2, strips), ("x", "core", "space"))
    placed = P(("x", "core"), "space", None, None, None)
    return jax.shard_map(
        on_device,
        mesh=split,
        in_specs=(placed,) + (P(),) * 9 + (placed,),
        out_specs=(placed, placed, P(), P(), P()),
        check_vma=False,
    )
```

time: 115 us -> 72.6 us (0.63)
  local copies, waits for them, and re-layouts: 30.6 us -> 3.18 us
  blocking collectives: 26.6 us -> 0 us
  starting transfers between devices: 13.7 us -> 25.1 us
  Pallas kernels: 23.4 us -> 27.1 us
  other arithmetic: 2.29 us -> 0.3 us
    all_to_all x1 -> x0, blocking collectives: 26.6 us -> none  [on_device(): lax.all_to_all(terms.reshape(devices, mine, 128), axes, 0, 0, tiled=True)]
    mul x6 -> x0, local copies, waits for them, and re-layouts: 17.6 us -> none  [spread(): wide = by_group[..., None] * eye[None, None, :, None, :]]
    ppermute x0 -> x11, starting transfers between devices: none -> 12.3 us  [swap(): lax.ppermute(value, axis, [(source, source ^ mask) for source in range(co...]
    ppermute x4, waiting for transfers between devices: 16.4 us -> 8.21 us  [shifted(): lax.ppermute(value, axis, [(source, source + steps) for source in range(i...]
    ppermute x0 -> x11, waiting for transfers between devices: none -> 7.49 us  [swap(): lax.ppermute(value, axis, [(source, source ^ mask) for source in range(co...]
    unnamed x34 -> x30, local copies, waits for them, and re-layouts: 6.7 us -> 2.85 us
    pallas_call x3 -> x8, Pallas kernels: 23.4 us -> 27.1 us  [the longest x1 7 us: on_device(): pl.pallas_call(upper_kernel, out_shape=(narrow, narrow, *terms), in_specs...]
    all_to_all x1 -> x0, starting transfers between devices: 2.61 us -> none  [on_device(): lax.all_to_all(jnp.broadcast_to(own, (devices, mine, 128)), axes, 0, 0, t...]
  transfers between devices with their start and end apart: 5 -> 15, of which waited for: 1 -> 7; matrix products, arithmetic and copies ran while one was open for 21% -> 1% of each run, Pallas kernels for 5% -> 25%
where the time goes in v1:
time: 72.6 us; the launch traced here: 72.3 us
  Pallas kernels  27.1 us (37%)
  starting transfers between devices  25.1 us (35%)
  waiting for transfers between devices  15.7 us (22%)
  local copies, waits for them, and re-layouts  3.18 us (4%)
  between operations  0.96 us (1%)
    ppermute x4, starting transfers between devices, shifted(): lax.ppermute(value, axis, [(source, source + steps) for source in range(i...  12.9 us
    ppermute x11, starting transfers between devices, swap(): lax.ppermute(value, axis, [(source, source ^ mask) for source in range(co...  12.3 us
    ppermute x4, waiting for transfers between devices, shifted(): lax.ppermute(value, axis, [(source, source + steps) for source in range(i...  8.21 us
    ppermute x11, waiting for transfers between devices, swap(): lax.ppermute(value, axis, [(source, source ^ mask) for source in range(co...  7.49 us
    pallas_call x1, Pallas kernels, on_device(): pl.pallas_call(upper_kernel, out_shape=(narrow, narrow, *terms), in_specs...  7 us
    pallas_call x1, Pallas kernels, on_device(): pl.pallas_call(input_kernel, out_shape=(image, image), in_specs=[IN_VMEM]...  5.56 us
    pallas_call x1, Pallas kernels, on_device(): pl.pallas_call(inner_kernel, out_shape=(spread, spread, middle, middle, *...  5.43 us
    pallas_call x1, Pallas kernels, on_device(): pl.pallas_call(lower_kernel, out_shape=(narrow, narrow, tall, *kept(REACH...  4.49 us
  transfers between devices with their start and end apart: 15, of which 7 were waited for; matrix products, arithmetic and copies ran while one was open for 1% of the time, Pallas kernels for 25%

profile of v1, /device:TPU:0, one launch (start us, length us, event | category | flops | bytes accessed | tf_op | source)
XLA Modules:
  0.0 72.3 jit_solution(11600516264224546256)
XLA Ops:
  0.8 1.1 %copy-done = bf16[1,1,8,256,192]{3,4,2,1,0:T(8,128)(2,1)S(1)} copy-done((bf16[1,1,8,256,192]{3,4,2,1,0:T(8,128)(2,1)S(1)}, bf16[1,1,8,256,192]{3,4,2,1,0:T(8,128)(2,1)}, u32[]{:S(2)}) %copy-start) | copy-done | bytes 786456
  1.9 0.8 %shard_map.146 = bf16[3,192,256]{2,1,0:T(8,128)(2,1)} custom-call(bf16[8,192,256]{2,1,0:T(8,128)(2,1)S(1)} %bitcast.36), custom_call_target="tpu_custom_call" | custom-call | tf_op jit(solution)/shard_map/pallas_call | solution.py:316
  2.7 5.7 %collective-permute-start = (bf16[3,192,256]{2,1,0:T(8,128)(2,1)}, bf16[3,192,256]{2,1,0:T(8,128)(2,1)}, u32[]{:S(2)}, u32[]{:S(2)}) collective-permute-start(bf16[3,192,256]{2,1,0:T(8,128)(2,1)} %shard_map.146), channel_id=1, source_target_pairs={{0,1},{1,2},{2,3},{3,4},{4,5},{5,6},{6,7},{8,9},{9,10},{10,11},{11... | collective-permute-start | bytes 884744 | tf_op jit(solution)/shard_map/ppermute | solution.py:20
  8.5 0.7 copy-done.5
  10.6 5.4 %shard_map.148 = (bf16[12,112,224]{2,1,0:T(8,128)(2,1)S(1)}, bf16[12,112,224]{2,1,0:T(8,128)(2,1)S(1)}, bf16[2,192,256]{2,1,0:T(8,128)(2,1)S(1)}, bf16[2,192,256...) custom-call(bf16[8,192,256]{2,1,0:T(8,128)(2,1)S(1)} %bitcast.38, ...), custom_call_target="tpu_custom_call" | custom-call | tf_op jit(solution)/shard_map/pallas_call | solution.py:348
  16.1 1.3 %collective-permute-start.1 = (bf16[3,192,256]{2,1,0:T(8,128)(2,1)S(1)}, bf16[3,192,256]{2,1,0:T(8,128)(2,1)S(1)}, u32[]{:S(2)}, u32[]{:S(2)}) collective-permute-start(bf16[3,192,256]{2,1,0:T(8,128)(2,1)S(1)} %copy-done.6), channel_id=1, source_target_pairs={{1,0},{2,1},{3,2},{4,3},{5,4},{6,5},{7,6},{9,8},{10,9},{11,10},{12... | collective-permute-start | bytes 884744 | tf_op jit(solution)/shard_map/ppermute | solution.py:20
  17.4 7.0 %shard_map.149 = (bf16[3,192,256]{2,1,0:T(8,128)(2,1)S(1)}, bf16[3,192,256]{2,1,0:T(8,128)(2,1)S(1)}, f32[192,768]{1,0:T(8,128)S(1)}, f32[192,768]{1,0:T(8,128)S(1)}, f32[12,8,112]{2,1,0:T(8,128)S(1)}) custom-call(bf16[8,192,256]{2,1,0:T(8,128)(2,1)S(1)} %bitcast.39, bf16[3,192,256]{2,1,0:T(8,128)(2,1)} %collective-permute-done.above_ref, ...), custom_call_target="tpu_custom_call" | custom-call | tf_op jit(solution)/shard_map/pallas_call | solution.py:361
  24.4 2.1 %collective-permute-done.1.below_ref = bf16[3,192,256]{2,1,0:T(8,128)(2,1)S(1)} collective-permute-done((bf16[3,192,256]{2,1,0:T(8,128)(2,1)S(1)}, bf16[3,192,256]{2,1,0:T(8,128)(2,1)S(1)}, u32[]{:S(2)}, u32[]{:S(2)}) %collective-permute-start.1) | collective-permute-done | bytes 294944 | tf_op jit(solution)/shard_map/ppermute | solution.py:20
  26.4 4.5 %shard_map.150 = (bf16[3,192,256]{2,1,0:T(8,128)(2,1)S(1)}, bf16[3,192,256]{2,1,0:T(8,128)(2,1)S(1)}, bf16[9,192,256]{2,1,0:T(8,128)(2,1)S(1)}, bf16[3,192,256]{...) custom-call(bf16[8,192,256]{2,1,0:T(8,128)(2,1)S(1)} %bitcast.40, ...), custom_call_target="tpu_custom_call" | custom-call | tf_op jit(solution)/shard_map/pallas_call | solution.py:370
  30.9 2.1 %shard_map.152 = (bf16[1216,128]{1,0:T(8,128)(2,1)S(1)}, bf16[1216,128]{1,0:T(8,128)(2,1)S(1)}) custom-call(s32[2]{0:T(128)S(1)} %add_convert_fusion.2.refs_0_.place_ref, bf16[9,192,256]{2,1,0:T(8,128)(2,1)S(1)} %get-tuple-element.59.refs_1_, bf16[3,192,256]{2,1,0:T(8,128)(2,1)S(1)} %get-tuple-element.55.gz_lower_ref.refs_2_, ...), custom_call_target="tpu_custom_call" | custom-call | tf_op jit(solution)/shard_map/pallas_call | solution.py:378
  33.1 1.6 %collective-permute-done.4 = bf16[1216,128]{1,0:T(8,128)(2,1)S(1)} collective-permute-done((bf16[1216,128]{1,0:T(8,128)(2,1)S(1)}, bf16[1216,128]{1,0:T(8,128)(2,1)S(1)}, u32[]{:S(2)}, u32[]{:S(2)}) %collective-permute-start.4) | collective-permute-done | bytes 311328 | tf_op jit(solution)/shard_map/ppermute | solution.py:289
  34.8 2.7 %collective-permute-start.7 = (bf16[304,128]{1,0:T(8,128)(2,1)S(1)}, bf16[304,128]{1,0:T(8,128)(2,1)S(1)}, u32[]{:S(2)}, u32[]{:S(2)}) collective-permute-start(bf16[304,128]{1,0:T(8,128)(2,1)S(1)} %get-tuple-element.80), channel_id=1, source_target_pairs={{0,17},{1,16},{2,19},{3,18},{4,21},{5,20},{6,23},{7,22},{16,1},{17... | collective-permute-start | bytes 233480 | tf_op jit(solution)/shard_map/ppermute | solution.py:289
  38.4 1.3 %collective-permute-start.3 = (bf16[3,192,256]{2,1,0:T(8,128)(2,1)S(1)}, bf16[3,192,256]{2,1,0:T(8,128)(2,1)S(1)}, u32[]{:S(2)}, u32[]{:S(2)}) collective-permute-start(bf16[3,192,256]{2,1,0:T(8,128)(2,1)S(1)} %get-tuple-element.53.gz_upper_ref), channel_id=1, source_target_pairs={{1,0},{2,1},{3,2},{4,3},{5,4},{6,5},{7,6},{9,8},{10,9},{11,10},{12... | collective-permute-start | bytes 884744 | tf_op jit(solution)/shard_map/ppermute | solution.py:20
  39.7 4.6 %collective-permute-start.2 = (bf16[3,192,256]{2,1,0:T(8,128)(2,1)S(1)}, bf16[3,192,256]{2,1,0:T(8,128)(2,1)S(1)}, u32[]{:S(2)}, u32[]{:S(2)}) collective-permute-start(bf16[3,192,256]{2,1,0:T(8,128)(2,1)S(1)} %get-tuple-element.55.gz_lower_ref.refs_2_), channel_id=1, source_target_pairs={{0,1},{1,2},{2,3},{3,4},{4,5},{5,6},{6,7},{8,9},{9,10},{10,11},{11... | collective-permute-start | bytes 884744 | tf_op jit(solution)/shard_map/ppermute | solution.py:20
  44.3 3.2 %collective-permute-start.10 = (bf16[304,128]{1,0:T(8,128)(2,1)S(1)}, bf16[304,128]{1,0:T(8,128)(2,1)S(1)}, u32[]{:S(2)}, u32[]{:S(2)}) collective-permute-start(bf16[304,128]{1,0:T(8,128)(2,1)S(1)} %fusion.1), channel_id=1, source_target_pairs={{0,6},{1,7},{2,4},{3,5},{4,2},{5,3},{6,0},{7,1},{8,14},{9,15},{10,... | collective-permute-start | bytes 233480 | tf_op jit(solution)/shard_map/ppermute | solution.py:289
  47.6 1.2 %collective-permute-start.8 = (bf16[304,128]{1,0:T(8,128)(2,1)S(1)}, bf16[304,128]{1,0:T(8,128)(2,1)S(1)}, u32[]{:S(2)}, u32[]{:S(2)}) collective-permute-start(bf16[304,128]{1,0:T(8,128)(2,1)S(1)} %fusion.1), channel_id=1, source_target_pairs={{0,2},{1,3},{2,0},{3,1},{4,6},{5,7},{6,4},{7,5},{8,10},{9,11},{10,... | collective-permute-start | bytes 233480 | tf_op jit(solution)/shard_map/ppermute | solution.py:289
  48.8 6.1 %collective-permute-done.2.above_ref = bf16[3,192,256]{2,1,0:T(8,128)(2,1)S(1)} collective-permute-done((bf16[3,192,256]{2,1,0:T(8,128)(2,1)S(1)}, bf16[3,192,256]{2,1,0:T(8,128)(2,1)S(1)}, u32[]{:S(2)}, u32[]{:S(2)}) %collective-permute-start.2) | collective-permute-done | bytes 294944 | tf_op jit(solution)/shard_map/ppermute | solution.py:20
  54.9 5.6 %shard_map.151 = (bf16[8,192,256]{2,1,0:T(8,128)(2,1)}, bf16[8,192,256]{2,1,0:T(8,128)(2,1)}) custom-call(bf16[3,192,256]{2,1,0:T(8,128)(2,1)S(1)} %get-tuple-element.49.out_upper_ref, bf16[2,192,256]{2,1,0:T(8,128)(2,1)S(1)} %get-tuple-element.50.out_inner_ref, bf16[3,192,256]{2,1,0:T(8,128)(2,1)S(1)} %get-tuple-element.52.out_lower_ref, ...), custom_call_target="tpu_custom_call" | custom-call | tf_op jit(solution)/shard_map/pallas_call | solution.py:396
  60.6 3.5 %collective-permute-start.13 = (bf16[304,128]{1,0:T(8,128)(2,1)S(1)}, bf16[304,128]{1,0:T(8,128)(2,1)S(1)}, u32[]{:S(2)}, u32[]{:S(2)}) collective-permute-start(bf16[304,128]{1,0:T(8,128)(2,1)S(1)} %add_convert_fusion.1), channel_id=1, source_target_pairs={{0,17},{1,16},{2,19},{3,18},{4,21},{5,20},{6,23},{7,22},{16,1},{17... | collective-permute-start | bytes 233480 | tf_op jit(solution)/shard_map/ppermute | solution.py:289
  64.0 0.5 collective-permute-start.12
  64.7 2.5 %collective-permute-done.13 = bf16[304,128]{1,0:T(8,128)(2,1)S(1)} collective-permute-done((bf16[304,128]{1,0:T(8,128)(2,1)S(1)}, bf16[304,128]{1,0:T(8,128)(2,1)S(1)}, u32[]{:S(2)}, u32[]{:S(2)}) %collective-permute-start.13) | collective-permute-done | bytes 77856 | tf_op jit(solution)/shard_map/ppermute | solution.py:289
  67.2 1.4 %collective-permute-done.12 = bf16[304,128]{1,0:T(8,128)(2,1)S(1)} collective-permute-done((bf16[304,128]{1,0:T(8,128)(2,1)S(1)}, bf16[304,128]{1,0:T(8,128)(2,1)S(1)}, u32[]{:S(2)}, u32[]{:S(2)}) %collective-permute-start.12) | collective-permute-done | bytes 77856 | tf_op jit(solution)/shard_map/ppermute | solution.py:289
  69.1 1.6 %collective-permute-done.14.other_ref = bf16[4,304,128]{2,1,0:T(8,128)(2,1)S(1)} collective-permute-done((bf16[4,304,128]{2,1,0:T(8,128)(2,1)S(1)}, bf16[4,304,128]{2,1,0:T(8,128)(2,1)S(1)}, u32[]{:S(2)}, u32[]{:S(2)}) %collective-permute-start.14) | collective-permute-done | bytes 311328 | tf_op jit(solution)/shard_map/ppermute | solution.py:289
  70.7 1.7 %shard_map.153 = (f32[192,768]{1,0:T(8,128)}, f32[192,768]{1,0:T(8,128)}, f32[7,7,192]{2,1,0:T(8,128)}) custom-call(s32[2]{0:T(128)S(1)} %add_convert_fusion.2.refs_0_.place_ref, bf16[4,304,128]{2,1,0:T(8,128)(2,1)S(1)} %pad_maximum_fusion.mine_ref, bf16[4,304,128]{2,1,0:T(8,128)(2,1)S(1)} %collective-permute-done.14.other_ref), custom_call_target="tpu_custom_call" | custom-call | tf_op jit(solution)/shard_map/pallas_call | solution.py:412
  (53 shorter events, 3.2 us)
Async XLA Ops:
  0.6 8.6 %copy-start.9 = (f32[192]{0:T(256)S(1)}, f32[192]{0:T(256)}, u32[]{:S(2)}) copy-start(f32[192]{0:T(256)} %param.13) | copy-start | bytes 2308
  0.6 8.6 %copy-start.10 = (f32[192]{0:T(256)S(1)}, f32[192]{0:T(256)}, u32[]{:S(2)}) copy-start(f32[192]{0:T(256)} %param.14) | copy-start | bytes 2308
  0.7 8.6 %copy-start.11 = (f32[192]{0:T(256)S(1)}, f32[192]{0:T(256)}, u32[]{:S(2)}) copy-start(f32[192]{0:T(256)} %param.15) | copy-start | bytes 2308
  0.7 8.6 %copy-start.12 = (f32[192]{0:T(256)S(1)}, f32[192]{0:T(256)}, u32[]{:S(2)}) copy-start(f32[192]{0:T(256)} %param.19) | copy-start | bytes 2308
  0.7 8.6 %copy-start.13 = (f32[192]{0:T(256)S(1)}, f32[192]{0:T(256)}, u32[]{:S(2)}) copy-start(f32[192]{0:T(256)} %param.20) | copy-start | bytes 2308
  0.7 8.8 %copy-start.8 = (f32[768]{0:T(1024)S(1)}, f32[768]{0:T(1024)}, u32[]{:S(2)}) copy-start(f32[768]{0:T(1024)} %param.17) | copy-start | bytes 9220
  1.9 7.7 %copy-start.3 = (bf16[192,768]{1,0:T(8,128)(2,1)S(1)}, bf16[192,768]{1,0:T(8,128)(2,1)}, u32[]{:S(2)}) copy-start(bf16[192,768]{1,0:T(8,128)(2,1)} %win_ref.5) | copy-start | bytes 884740
  2.7 7.1 %copy-start.4 = (bf16[768,192]{0,1:T(8,128)(2,1)S(1)}, bf16[768,192]{0,1:T(8,128)(2,1)}, u32[]{:S(2)}) copy-start(bf16[768,192]{0,1:T(8,128)(2,1)} %param.18) | copy-start | bytes 884740
  2.7 13.3 %collective-permute-start = (bf16[3,192,256]{2,1,0:T(8,128)(2,1)}, bf16[3,192,256]{2,1,0:T(8,128)(2,1)}, u32[]{:S(2)}, u32[]{:S(2)}) collective-permute-start(bf16[3,192,256]{2,1,0:T(8,128)(2,1)} %shard_map.146), channel_id=1, source_target_pairs={{0,1},{1,2},{2,3},{3,4},{4,5},{5,6},{6,7},{8,9},{9,10},{10,11},{11... | collective-permute-start | bytes 884744 | tf_op jit(solution)/shard_map/ppermute | solution.py:20
  10.6 5.5 %copy-start.6 = (bf16[3,192,256]{2,1,0:T(8,128)(2,1)S(1)}, bf16[3,192,256]{2,1,0:T(8,128)(2,1)}, u32[]{:S(2)}) copy-start(bf16[3,192,256]{2,1,0:T(8,128)(2,1)} %copy-done.5) | copy-start | bytes 884740
  16.1 10.4 %collective-permute-start.1 = (bf16[3,192,256]{2,1,0:T(8,128)(2,1)S(1)}, bf16[3,192,256]{2,1,0:T(8,128)(2,1)S(1)}, u32[]{:S(2)}, u32[]{:S(2)}) collective-permute-start(bf16[3,192,256]{2,1,0:T(8,128)(2,1)S(1)} %copy-done.6), channel_id=1, source_target_pairs={{1,0},{2,1},{3,2},{4,3},{5,4},{6,5},{7,6},{9,8},{10,9},{11,10},{12... | collective-permute-start | bytes 884744 | tf_op jit(solution)/shard_map/ppermute | solution.py:20
  33.0 1.7 %collective-permute-start.4 = (bf16[1216,128]{1,0:T(8,128)(2,1)S(1)}, bf16[1216,128]{1,0:T(8,128)(2,1)S(1)}, u32[]{:S(2)}, u32[]{:S(2)}) collective-permute-start(bf16[1216,128]{1,0:T(8,128)(2,1)S(1)} %get-tuple-element.68), channel_id=1, source_target_pairs={{0,8},{8,0},{1,9},{9,1},{2,10},{10,2},{3,11},{11,3},{4,12},{12,4},... | collective-permute-start | bytes 933896 | tf_op jit(solution)/shard_map/ppermute | solution.py:289
  34.8 9.4 %collective-permute-start.7 = (bf16[304,128]{1,0:T(8,128)(2,1)S(1)}, bf16[304,128]{1,0:T(8,128)(2,1)S(1)}, u32[]{:S(2)}, u32[]{:S(2)}) collective-permute-start(bf16[304,128]{1,0:T(8,128)(2,1)S(1)} %get-tuple-element.80), channel_id=1, source_target_pairs={{0,17},{1,16},{2,19},{3,18},{4,21},{5,20},{6,23},{7,22},{16,1},{17... | collective-permute-start | bytes 233480 | tf_op jit(solution)/shard_map/ppermute | solution.py:289
  37.5 6.7 %collective-permute-start.6 = (bf16[304,128]{1,0:T(8,128)(2,1)S(1)}, bf16[304,128]{1,0:T(8,128)(2,1)S(1)}, u32[]{:S(2)}, u32[]{:S(2)}) collective-permute-start(bf16[304,128]{1,0:T(8,128)(2,1)S(1)} %get-tuple-element.81), channel_id=1, source_target_pairs={{0,16},{1,17},{2,18},{3,19},{4,20},{5,21},{6,22},{7,23},{16,0},{17... | collective-permute-start | bytes 233480 | tf_op jit(solution)/shard_map/ppermute | solution.py:289
  38.1 6.2 %collective-permute-start.5 = (bf16[304,128]{1,0:T(8,128)(2,1)S(1)}, bf16[304,128]{1,0:T(8,128)(2,1)S(1)}, u32[]{:S(2)}, u32[]{:S(2)}) collective-permute-start(bf16[304,128]{1,0:T(8,128)(2,1)S(1)} %get-tuple-element.79), channel_id=1, source_target_pairs={{0,1},{1,0},{2,3},{3,2},{4,5},{5,4},{6,7},{7,6},{16,17},{17,16},{1... | collective-permute-start | bytes 233480 | tf_op jit(solution)/shard_map/ppermute | solution.py:289
  38.4 10.4 %collective-permute-start.3 = (bf16[3,192,256]{2,1,0:T(8,128)(2,1)S(1)}, bf16[3,192,256]{2,1,0:T(8,128)(2,1)S(1)}, u32[]{:S(2)}, u32[]{:S(2)}) collective-permute-start(bf16[3,192,256]{2,1,0:T(8,128)(2,1)S(1)} %get-tuple-element.53.gz_upper_ref), channel_id=1, source_target_pairs={{1,0},{2,1},{3,2},{4,3},{5,4},{6,5},{7,6},{9,8},{10,9},{11,10},{12... | collective-permute-start | bytes 884744 | tf_op jit(solution)/shard_map/ppermute | solution.py:20
  39.7 15.3 %collective-permute-start.2 = (bf16[3,192,256]{2,1,0:T(8,128)(2,1)S(1)}, bf16[3,192,256]{2,1,0:T(8,128)(2,1)S(1)}, u32[]{:S(2)}, u32[]{:S(2)}) collective-permute-start(bf16[3,192,256]{2,1,0:T(8,128)(2,1)S(1)} %get-tuple-element.55.gz_lower_ref.refs_2_), channel_id=1, source_target_pairs={{0,1},{1,2},{2,3},{3,4},{4,5},{5,6},{6,7},{8,9},{9,10},{10,11},{11... | collective-permute-start | bytes 884744 | tf_op jit(solution)/shard_map/ppermute | solution.py:20
  44.3 16.2 %collective-permute-start.10 = (bf16[304,128]{1,0:T(8,128)(2,1)S(1)}, bf16[304,128]{1,0:T(8,128)(2,1)S(1)}, u32[]{:S(2)}, u32[]{:S(2)}) collective-permute-start(bf16[304,128]{1,0:T(8,128)(2,1)S(1)} %fusion.1), channel_id=1, source_target_pairs={{0,6},{1,7},{2,4},{3,5},{4,2},{5,3},{6,0},{7,1},{8,14},{9,15},{10,... | collective-permute-start | bytes 233480 | tf_op jit(solution)/shard_map/ppermute | solution.py:289
  47.6 12.9 %collective-permute-start.9 = (bf16[304,128]{1,0:T(8,128)(2,1)S(1)}, bf16[304,128]{1,0:T(8,128)(2,1)S(1)}, u32[]{:S(2)}, u32[]{:S(2)}) collective-permute-start(bf16[304,128]{1,0:T(8,128)(2,1)S(1)} %fusion.1), channel_id=1, source_target_pairs={{0,4},{1,5},{2,6},{3,7},{4,0},{5,1},{6,2},{7,3},{8,12},{9,13},{10,... | collective-permute-start | bytes 233480 | tf_op jit(solution)/shard_map/ppermute | solution.py:289
  47.6 12.9 %collective-permute-start.8 = (bf16[304,128]{1,0:T(8,128)(2,1)S(1)}, bf16[304,128]{1,0:T(8,128)(2,1)S(1)}, u32[]{:S(2)}, u32[]{:S(2)}) collective-permute-start(bf16[304,128]{1,0:T(8,128)(2,1)S(1)} %fusion.1), channel_id=1, source_target_pairs={{0,2},{1,3},{2,0},{3,1},{4,6},{5,7},{6,4},{7,5},{8,10},{9,11},{10,... | collective-permute-start | bytes 233480 | tf_op jit(solution)/shard_map/ppermute | solution.py:289
  60.6 6.6 %collective-permute-start.13 = (bf16[304,128]{1,0:T(8,128)(2,1)S(1)}, bf16[304,128]{1,0:T(8,128)(2,1)S(1)}, u32[]{:S(2)}, u32[]{:S(2)}) collective-permute-start(bf16[304,128]{1,0:T(8,128)(2,1)S(1)} %add_convert_fusion.1), channel_id=1, source_target_pairs={{0,17},{1,16},{2,19},{3,18},{4,21},{5,20},{6,23},{7,22},{16,1},{17... | collective-permute-start | bytes 233480 | tf_op jit(solution)/shard_map/ppermute | solution.py:289
  64.0 4.6 %collective-permute-start.12 = (bf16[304,128]{1,0:T(8,128)(2,1)S(1)}, bf16[304,128]{1,0:T(8,128)(2,1)S(1)}, u32[]{:S(2)}, u32[]{:S(2)}) collective-permute-start(bf16[304,128]{1,0:T(8,128)(2,1)S(1)} %add_convert_fusion.1), channel_id=1, source_target_pairs={{0,16},{1,17},{2,18},{3,19},{4,20},{5,21},{6,22},{7,23},{16,0},{17... | collective-permute-start | bytes 233480 | tf_op jit(solution)/shard_map/ppermute | solution.py:289
  64.6 4.4 %collective-permute-start.11 = (bf16[304,128]{1,0:T(8,128)(2,1)S(1)}, bf16[304,128]{1,0:T(8,128)(2,1)S(1)}, u32[]{:S(2)}, u32[]{:S(2)}) collective-permute-start(bf16[304,128]{1,0:T(8,128)(2,1)S(1)} %add_convert_fusion.1), channel_id=1, source_target_pairs={{0,1},{1,0},{2,3},{3,2},{4,5},{5,4},{6,7},{7,6},{16,17},{17,16},{1... | collective-permute-start | bytes 233480 | tf_op jit(solution)/shard_map/ppermute | solution.py:289
  69.0 1.7 %collective-permute-start.14 = (bf16[4,304,128]{2,1,0:T(8,128)(2,1)S(1)}, bf16[4,304,128]{2,1,0:T(8,128)(2,1)S(1)}, u32[]{:S(2)}, u32[]{:S(2)}) collective-permute-start(bf16[4,304,128]{2,1,0:T(8,128)(2,1)S(1)} %pad_maximum_fusion.mine_ref), channel_id=1, source_target_pairs={{0,8},{8,0},{1,9},{9,1},{2,10},{10,2},{3,11},{11,3},{4,12},{12,4},... | collective-permute-start | bytes 933896 | tf_op jit(solution)/shard_map/ppermute | solution.py:289
  (5 other events, 5.7 us)

commit v2 on v1

--- a/solution.py
+++ b/solution.py
@@ -228,12 +228,12 @@
 
 def input_kernel(
     out_upper_ref, out_inner_ref, out_lower_ref, gz_upper_ref, gz_inner_ref, gz_lower_ref,
-    above_ref, below_ref, g_ref, taps_ref,
+    below_ref, g_ref, taps_ref,
     out_ref, grad_ref, tall_ref,
 ):
     rows = g_ref.shape[0]
     at = 0
-    for ref in (above_ref, gz_upper_ref, gz_inner_ref, gz_lower_ref, below_ref):
+    for ref in (gz_upper_ref, gz_inner_ref, gz_lower_ref, below_ref):
         tall_ref[at : at + ref.shape[0]] = ref[...]
         at += ref.shape[0]
     at = 0
@@ -242,10 +242,31 @@
         at += ref.shape[0]
 
     def step(row, carry):
-        grad_ref[row] = (g_ref[row].astype(F32) + conv_row(tall_ref, taps_ref, row)).astype(BF16)
+        at = row + REACH
+        grad_ref[at] = (g_ref[at].astype(F32) + conv_row(tall_ref, taps_ref, row)).astype(BF16)
         return carry
 
-    lax.fori_loop(0, rows, step, 0)
+    lax.fori_loop(0, rows - REACH, step, 0)
+
+
+def input_upper_kernel(
+    above_ref, gz_upper_ref, gz_inner_ref, gz_lower_ref, g_ref, taps_ref, rest_ref,
+    grad_ref, tall_ref, part_ref, sem,
+):
+    tall_ref[0:REACH] = above_ref[...]
+    tall_ref[REACH : 2 * REACH] = gz_upper_ref[...]
+    inner = gz_inner_ref.shape[0]
+    for at in range(REACH):
+        tall_ref[2 * REACH + at] = gz_inner_ref[at] if at < inner else gz_lower_ref[at - inner]
+
+    def step(row, carry):
+        part_ref[row] = (g_ref[row].astype(F32) + conv_row(tall_ref, taps_ref, row)).astype(BF16)
+        return carry
+
+    lax.fori_loop(0, REACH, step, 0)
+    copy = pltpu.make_async_copy(part_ref, grad_ref.at[pl.ds(0, REACH)], sem)
+    copy.start()
+    copy.wait()
 
 
 def final_kernel(place_ref, mine_ref, other_ref, win_ref, woutt_ref, taps_ref, all_ref):
@@ -383,6 +404,7 @@
         scratch_shapes=[pltpu.VMEM((2, half_rows, 128), BF16)],
         compiler_params=PARAMS,
     )(place, lower_kept[0], gz_lower, *lower_kept[1:], *upper_terms)
+    keep, send, gz_below = lax.optimization_barrier((keep, send, gz_below))
 
     summed = added(keep, swap(send, "core", 1)).reshape(4, half_rows // 4, 128)
 
@@ -393,21 +415,35 @@
         return swap(value, ("x", "space"), (turn >> 1) * strips | (turn & 1))
 
     own = added(at(0), *[partner(at(turn), turn) for turn in (1, 2, 3)])
-    out, grad_input = pl.pallas_call(
+    out, grad_rest = pl.pallas_call(
         input_kernel,
         out_shape=(image, image),
-        in_specs=[IN_VMEM] * 10,
+        in_specs=[IN_VMEM] * 9,
         out_specs=(IN_VMEM, IN_VMEM),
-        scratch_shapes=[pltpu.VMEM((rows + 2 * REACH, chans, width), BF16)],
-        compiler_params=PARAMS,
-    )(out_upper, out_inner, out_lower, gz_upper, gz_inner, gz_lower, gz_above, gz_below, g, back_taps)
+        scratch_shapes=[pltpu.VMEM((rows + REACH, chans, width), BF16)],
+        compiler_params=PARAMS,
+    )(out_upper, out_inner, out_lower, gz_upper, gz_inner, gz_lower, gz_below, g, back_taps)
+    own, grad_rest = lax.optimization_barrier((own, grad_rest))
     bit = 2
     while bit < strips:
         masks = (bit, 2 * bit, 3 * bit) if 2 * bit < strips else (bit,)
         own = added(own, *[swap(own, "space", mask) for mask in masks])
         bit *= 4
-    own, grad_input = lax.optimization_barrier((own, grad_input))
     mine = jnp.stack([own] + [partner(own, turn) for turn in (1, 2, 3)])
+    grad_input = pl.pallas_call(
+        input_upper_kernel,
+        out_shape=image,
+        in_specs=[IN_VMEM] * 6 + [pl.BlockSpec(memory_space=pl.ANY)],
+        out_specs=pl.BlockSpec(memory_space=pl.ANY),
+        scratch_shapes=[
+            pltpu.VMEM((3 * REACH, chans, width), BF16),
+            pltpu.VMEM((REACH, chans, width), BF16),
+            pltpu.SemaphoreType.DMA(()),
+        ],
+        input_output_aliases={6: 0},
+        compiler_params=PARAMS,
+    )(gz_above, gz_upper, gz_inner, gz_lower, g, back_taps, grad_rest)
+    mine, grad_input = lax.optimization_barrier((mine, grad_input))
     other = swap(mine, "core", 1)
     grad_w_in, grad_w_out_t, grad_kernel = pl.pallas_call(
         final_kernel,

time: 72.6 us -> 67.9 us (0.935)
  waiting for transfers between devices: 15.7 us -> 10.6 us
  starting transfers between devices: 25.1 us -> 24.1 us
    ppermute x4, waiting for transfers between devices: 8.21 us -> 5.42 us  [shifted(): lax.ppermute(value, axis, [(source, source + steps) for source in range(i...]
    pallas_call x0 -> x1, Pallas kernels: none -> 2.42 us  [on_device(): pl.pallas_call(input_upper_kernel, out_shape=image, in_specs=[IN_VMEM] *...]
    ppermute x11, waiting for transfers between devices: 7.49 us -> 5.17 us  [swap(): lax.ppermute(value, axis, [(source, source ^ mask) for source in range(co...]
    pallas_call x1, Pallas kernels: 5.56 us -> 3.9 us  [on_device(): pl.pallas_call(input_kernel, out_shape=(image, image), in_specs=[IN_VMEM]...]
    ppermute x4, starting transfers between devices: 12.9 us -> 11.8 us  [shifted(): lax.ppermute(value, axis, [(source, source + steps) for source in range(i...]
  transfers between devices with their start and end apart: 15 -> 15, of which waited for: 7 -> 7; matrix products, arithmetic and copies ran while one was open for 1% -> 1% of each run, Pallas kernels for 25% -> 38%
where the time goes in v2:
time: 67.9 us; the launch traced here: 67 us
  Pallas kernels  27.8 us (41%)
  starting transfers between devices  24.1 us (35%)
  waiting for transfers between devices  10.6 us (16%)
  local copies, waits for them, and re-layouts  3.18 us (5%)
  between operations  0.97 us (1%)
    ppermute x11, starting transfers between devices, swap(): lax.ppermute(value, axis, [(source, source ^ mask) for source in range(co...  12.4 us
    ppermute x4, starting transfers between devices, shifted(): lax.ppermute(value, axis, [(source, source + steps) for source in range(i...  11.8 us
    pallas_call x1, Pallas kernels, on_device(): pl.pallas_call(upper_kernel, out_shape=(narrow, narrow, *terms), in_specs...  7 us
    pallas_call x1, Pallas kernels, on_device(): pl.pallas_call(inner_kernel, out_shape=(spread, spread, middle, middle, *...  5.43 us
    ppermute x4, waiting for transfers between devices, shifted(): lax.ppermute(value, axis, [(source, source + steps) for source in range(i...  5.42 us
    ppermute x11, waiting for transfers between devices, swap(): lax.ppermute(value, axis, [(source, source ^ mask) for source in range(co...  5.17 us
    pallas_call x1, Pallas kernels, on_device(): pl.pallas_call(lower_kernel, out_shape=(narrow, narrow, tall, *kept(REACH...  4.5 us
    pallas_call x1, Pallas kernels, on_device(): pl.pallas_call(input_kernel, out_shape=(image, image), in_specs=[IN_VMEM]...  3.9 us
  transfers between devices with their start and end apart: 15, of which 7 were waited for; matrix products, arithmetic and copies ran while one was open for 1% of the time, Pallas kernels for 38%

profile of v2, /device:TPU:0, one launch (start us, length us, event | category | flops | bytes accessed | tf_op | source)
XLA Modules:
  0.0 67.0 jit_solution(432936279594738908)
XLA Ops:
  0.8 1.1 %copy-done = bf16[1,1,8,256,192]{3,4,2,1,0:T(8,128)(2,1)S(1)} copy-done((bf16[1,1,8,256,192]{3,4,2,1,0:T(8,128)(2,1)S(1)}, bf16[1,1,8,256,192]{3,4,2,1,0:T(8,128)(2,1)}, u32[]{:S(2)}) %copy-start) | copy-done | bytes 786456
  1.9 0.8 %shard_map.146 = bf16[3,192,256]{2,1,0:T(8,128)(2,1)} custom-call(bf16[8,192,256]{2,1,0:T(8,128)(2,1)S(1)} %bitcast.36), custom_call_target="tpu_custom_call" | custom-call | tf_op jit(solution)/shard_map/pallas_call | solution.py:337
  2.7 5.7 %collective-permute-start = (bf16[3,192,256]{2,1,0:T(8,128)(2,1)}, bf16[3,192,256]{2,1,0:T(8,128)(2,1)}, u32[]{:S(2)}, u32[]{:S(2)}) collective-permute-start(bf16[3,192,256]{2,1,0:T(8,128)(2,1)} %shard_map.146), channel_id=1, source_target_pairs={{0,1},{1,2},{2,3},{3,4},{4,5},{5,6},{6,7},{8,9},{9,10},{10,11},{11... | collective-permute-start | bytes 884744 | tf_op jit(solution)/shard_map/ppermute | solution.py:20
  8.5 0.7 %copy-done.5 = bf16[3,192,256]{2,1,0:T(8,128)(2,1)} copy-done((bf16[3,192,256]{2,1,0:T(8,128)(2,1)}, bf16[3,192,256]{2,1,0:T(8,128)(2,1)S(1)}, u32[]{:S(2)}) %copy-start.5) | copy-done | bytes 294936
  10.6 5.4 %shard_map.148 = (bf16[12,112,224]{2,1,0:T(8,128)(2,1)S(1)}, bf16[12,112,224]{2,1,0:T(8,128)(2,1)S(1)}, bf16[2,192,256]{2,1,0:T(8,128)(2,1)S(1)}, bf16[2,192,256...) custom-call(bf16[8,192,256]{2,1,0:T(8,128)(2,1)S(1)} %bitcast.38, ...), custom_call_target="tpu_custom_call" | custom-call | tf_op jit(solution)/shard_map/pallas_call | solution.py:369
  16.1 1.3 %collective-permute-start.1 = (bf16[3,192,256]{2,1,0:T(8,128)(2,1)S(1)}, bf16[3,192,256]{2,1,0:T(8,128)(2,1)S(1)}, u32[]{:S(2)}, u32[]{:S(2)}) collective-permute-start(bf16[3,192,256]{2,1,0:T(8,128)(2,1)S(1)} %copy-done.6), channel_id=1, source_target_pairs={{1,0},{2,1},{3,2},{4,3},{5,4},{6,5},{7,6},{9,8},{10,9},{11,10},{12... | collective-permute-start | bytes 884744 | tf_op jit(solution)/shard_map/ppermute | solution.py:20
  17.4 7.0 %shard_map.149 = (bf16[3,192,256]{2,1,0:T(8,128)(2,1)S(1)}, bf16[3,192,256]{2,1,0:T(8,128)(2,1)S(1)}, f32[192,768]{1,0:T(8,128)S(1)}, f32[192,768]{1,0:T(8,128)S(1)}, f32[12,8,112]{2,1,0:T(8,128)S(1)}) custom-call(bf16[8,192,256]{2,1,0:T(8,128)(2,1)S(1)} %bitcast.39, bf16[3,192,256]{2,1,0:T(8,128)(2,1)} %collective-permute-done.above_ref, ...), custom_call_target="tpu_custom_call" | custom-call | tf_op jit(solution)/shard_map/pallas_call | solution.py:382
  24.4 1.3 %collective-permute-start.2 = (bf16[3,192,256]{2,1,0:T(8,128)(2,1)S(1)}, bf16[3,192,256]{2,1,0:T(8,128)(2,1)S(1)}, u32[]{:S(2)}, u32[]{:S(2)}) collective-permute-start(bf16[3,192,256]{2,1,0:T(8,128)(2,1)S(1)} %get-tuple-element.58.gz_upper_ref), channel_id=1, source_target_pairs={{1,0},{2,1},{3,2},{4,3},{5,4},{6,5},{7,6},{9,8},{10,9},{11,10},{12... | collective-permute-start | bytes 884744 | tf_op jit(solution)/shard_map/ppermute | solution.py:20
  25.7 0.8 %collective-permute-done.1.below_ref = bf16[3,192,256]{2,1,0:T(8,128)(2,1)S(1)} collective-permute-done((bf16[3,192,256]{2,1,0:T(8,128)(2,1)S(1)}, bf16[3,192,256]{2,1,0:T(8,128)(2,1)S(1)}, u32[]{:S(2)}, u32[]{:S(2)}) %collective-permute-start.1) | collective-permute-done | bytes 294944 | tf_op jit(solution)/shard_map/ppermute | solution.py:20
  26.4 4.5 %shard_map.150 = (bf16[3,192,256]{2,1,0:T(8,128)(2,1)S(1)}, bf16[3,192,256]{2,1,0:T(8,128)(2,1)S(1)}, bf16[9,192,256]{2,1,0:T(8,128)(2,1)S(1)}, bf16[3,192,256]{...) custom-call(bf16[8,192,256]{2,1,0:T(8,128)(2,1)S(1)} %bitcast.40, ...), custom_call_target="tpu_custom_call" | custom-call | tf_op jit(solution)/shard_map/pallas_call | solution.py:391
  30.9 2.1 %shard_map.151 = (bf16[1216,128]{1,0:T(8,128)(2,1)S(1)}, bf16[1216,128]{1,0:T(8,128)(2,1)S(1)}) custom-call(s32[2]{0:T(128)S(1)} %add_convert_fusion.2.refs_0_.place_ref, bf16[9,192,256]{2,1,0:T(8,128)(2,1)S(1)} %get-tuple-element.62.refs_1_, bf16[3,192,256]{2,1,0:T(8,128)(2,1)S(1)} %get-tuple-element.60.refs_2_.gz_lower_ref, ...), custom_call_target="tpu_custom_call" | custom-call | tf_op jit(solution)/shard_map/pallas_call | solution.py:399
  33.1 2.3 %collective-permute-done.2.below_ref = bf16[3,192,256]{2,1,0:T(8,128)(2,1)S(1)} collective-permute-done((bf16[3,192,256]{2,1,0:T(8,128)(2,1)S(1)}, bf16[3,192,256]{2,1,0:T(8,128)(2,1)S(1)}, u32[]{:S(2)}, u32[]{:S(2)}) %collective-permute-start.2) | collective-permute-done | bytes 294944 | tf_op jit(solution)/shard_map/ppermute | solution.py:20
  35.4 1.6 %collective-permute-done.3 = bf16[1216,128]{1,0:T(8,128)(2,1)S(1)} collective-permute-done((bf16[1216,128]{1,0:T(8,128)(2,1)S(1)}, bf16[1216,128]{1,0:T(8,128)(2,1)S(1)}, u32[]{:S(2)}, u32[]{:S(2)}) %collective-permute-start.3) | collective-permute-done | bytes 311328 | tf_op jit(solution)/shard_map/ppermute | solution.py:310
  37.1 3.6 %collective-permute-start.6 = (bf16[304,128]{1,0:T(8,128)(2,1)S(1)}, bf16[304,128]{1,0:T(8,128)(2,1)S(1)}, u32[]{:S(2)}, u32[]{:S(2)}) collective-permute-start(bf16[304,128]{1,0:T(8,128)(2,1)S(1)} %get-tuple-element.90), channel_id=1, source_target_pairs={{0,17},{1,16},{2,19},{3,18},{4,21},{5,20},{6,23},{7,22},{16,1},{17... | collective-permute-start | bytes 233480 | tf_op jit(solution)/shard_map/ppermute | solution.py:310
  41.4 3.9 %shard_map.152 = (bf16[8,192,256]{2,1,0:T(8,128)(2,1)}, bf16[8,192,256]{2,1,0:T(8,128)(2,1)}) custom-call(bf16[3,192,256]{2,1,0:T(8,128)(2,1)S(1)} %get-tuple-element.54.out_upper_ref, bf16[2,192,256]{2,1,0:T(8,128)(2,1)S(1)} %get-tuple-element.55.out_inner_ref, bf16[3,192,256]{2,1,0:T(8,128)(2,1)S(1)} %get-tuple-element.57.out_lower_ref, ...), custom_call_target="tpu_custom_call" | custom-call | tf_op jit(solution)/shard_map/pallas_call | solution.py:418
  45.7 3.0 %collective-permute-start.9 = (bf16[304,128]{1,0:T(8,128)(2,1)S(1)}, bf16[304,128]{1,0:T(8,128)(2,1)S(1)}, u32[]{:S(2)}, u32[]{:S(2)}) collective-permute-start(bf16[304,128]{1,0:T(8,128)(2,1)S(1)} %fusion.1), channel_id=1, source_target_pairs={{0,6},{1,7},{2,4},{3,5},{4,2},{5,3},{6,0},{7,1},{8,14},{9,15},{10,... | collective-permute-start | bytes 233480 | tf_op jit(solution)/shard_map/ppermute | solution.py:310
  48.7 1.5 %collective-permute-start.7 = (bf16[304,128]{1,0:T(8,128)(2,1)S(1)}, bf16[304,128]{1,0:T(8,128)(2,1)S(1)}, u32[]{:S(2)}, u32[]{:S(2)}) collective-permute-start(bf16[304,128]{1,0:T(8,128)(2,1)S(1)} %fusion.1), channel_id=1, source_target_pairs={{0,2},{1,3},{2,0},{3,1},{4,6},{5,7},{6,4},{7,5},{8,10},{9,11},{10,... | collective-permute-start | bytes 233480 | tf_op jit(solution)/shard_map/ppermute | solution.py:310
  50.2 3.5 %collective-permute-start.13 = (bf16[3,192,256]{2,1,0:T(8,128)(2,1)S(1)}, bf16[3,192,256]{2,1,0:T(8,128)(2,1)S(1)}, u32[]{:S(2)}, u32[]{:S(2)}) collective-permute-start(bf16[3,192,256]{2,1,0:T(8,128)(2,1)S(1)} %get-tuple-element.60.refs_2_.gz_lower_ref), channel_id=1, source_target_pairs={{0,1},{1,2},{2,3},{3,4},{4,5},{5,6},{6,7},{8,9},{9,10},{10,11},{11... | collective-permute-start | bytes 884744 | tf_op jit(solution)/shard_map/ppermute | solution.py:20
  53.6 1.6 %collective-permute-done.8 = bf16[304,128]{1,0:T(8,128)(2,1)S(1)} collective-permute-done((bf16[304,128]{1,0:T(8,128)(2,1)S(1)}, bf16[304,128]{1,0:T(8,128)(2,1)S(1)}, u32[]{:S(2)}, u32[]{:S(2)}) %collective-permute-start.8) | collective-permute-done | bytes 77856 | tf_op jit(solution)/shard_map/ppermute | solution.py:310
  55.3 2.7 %collective-permute-start.12 = (bf16[304,128]{1,0:T(8,128)(2,1)S(1)}, bf16[304,128]{1,0:T(8,128)(2,1)S(1)}, u32[]{:S(2)}, u32[]{:S(2)}) collective-permute-start(bf16[304,128]{1,0:T(8,128)(2,1)S(1)} %add_convert_fusion.1), channel_id=1, source_target_pairs={{0,17},{1,16},{2,19},{3,18},{4,21},{5,20},{6,23},{7,22},{16,1},{17... | collective-permute-start | bytes 233480 | tf_op jit(solution)/shard_map/ppermute | solution.py:310
  58.8 2.3 %collective-permute-done.13.above_ref = bf16[3,192,256]{2,1,0:T(8,128)(2,1)S(1)} collective-permute-done((bf16[3,192,256]{2,1,0:T(8,128)(2,1)S(1)}, bf16[3,192,256]{2,1,0:T(8,128)(2,1)S(1)}, u32[]{:S(2)}, u32[]{:S(2)}) %collective-permute-start.13) | collective-permute-done | bytes 294944 | tf_op jit(solution)/shard_map/ppermute | solution.py:20
  61.2 2.4 %shard_map.153 = bf16[8,192,256]{2,1,0:T(8,128)(2,1)} custom-call(bf16[3,192,256]{2,1,0:T(8,128)(2,1)S(1)} %collective-permute-done.13.above_ref, bf16[3,192,256]{2,1,0:T(8,128)(2,1)S(1)} %get-tuple-element.58.gz_upper_ref, bf16[2,192,256]{2,1,0:T(8,128)(2,1)S(1)} %get-tuple-element.59.gz_inner_ref, ...), custom_call_target="tpu_custom_call", output_to_operand_aliasing={{}: (6, {})} | custom-call | tf_op jit(solution)/shard_map/pallas_call | solution.py:433
  63.7 1.6 %collective-permute-done.14.other_ref = bf16[4,304,128]{2,1,0:T(8,128)(2,1)S(1)} collective-permute-done((bf16[4,304,128]{2,1,0:T(8,128)(2,1)S(1)}, bf16[4,304,128]{2,1,0:T(8,128)(2,1)S(1)}, u32[]{:S(2)}, u32[]{:S(2)}) %collective-permute-start.14) | collective-permute-done | bytes 311328 | tf_op jit(solution)/shard_map/ppermute | solution.py:310
  65.3 1.7 %shard_map.154 = (f32[192,768]{1,0:T(8,128)}, f32[192,768]{1,0:T(8,128)}, f32[7,7,192]{2,1,0:T(8,128)}) custom-call(s32[2]{0:T(128)S(1)} %add_convert_fusion.2.refs_0_.place_ref, bf16[4,304,128]{2,1,0:T(8,128)(2,1)S(1)} %pad_maximum_fusion.mine_ref, bf16[4,304,128]{2,1,0:T(8,128)(2,1)S(1)} %collective-permute-done.14.other_ref), custom_call_target="tpu_custom_call" | custom-call | tf_op jit(solution)/shard_map/pallas_call | solution.py:448
  (54 shorter events, 3.6 us)
Async XLA Ops:
  0.6 8.6 %copy-start.9 = (f32[192]{0:T(256)S(1)}, f32[192]{0:T(256)}, u32[]{:S(2)}) copy-start(f32[192]{0:T(256)} %param.13) | copy-start | bytes 2308
  0.6 8.6 %copy-start.10 = (f32[192]{0:T(256)S(1)}, f32[192]{0:T(256)}, u32[]{:S(2)}) copy-start(f32[192]{0:T(256)} %param.14) | copy-start | bytes 2308
  0.7 8.6 %copy-start.11 = (f32[192]{0:T(256)S(1)}, f32[192]{0:T(256)}, u32[]{:S(2)}) copy-start(f32[192]{0:T(256)} %param.15) | copy-start | bytes 2308
  0.7 8.6 %copy-start.12 = (f32[192]{0:T(256)S(1)}, f32[192]{0:T(256)}, u32[]{:S(2)}) copy-start(f32[192]{0:T(256)} %param.19) | copy-start | bytes 2308
  0.7 8.6 %copy-start.13 = (f32[192]{0:T(256)S(1)}, f32[192]{0:T(256)}, u32[]{:S(2)}) copy-start(f32[192]{0:T(256)} %param.20) | copy-start | bytes 2308
  0.7 8.8 %copy-start.8 = (f32[768]{0:T(1024)S(1)}, f32[768]{0:T(1024)}, u32[]{:S(2)}) copy-start(f32[768]{0:T(1024)} %param.17) | copy-start | bytes 9220
  1.9 7.7 %copy-start.3 = (bf16[192,768]{1,0:T(8,128)(2,1)S(1)}, bf16[192,768]{1,0:T(8,128)(2,1)}, u32[]{:S(2)}) copy-start(bf16[192,768]{1,0:T(8,128)(2,1)} %win_ref.5) | copy-start | bytes 884740
  2.7 7.1 %copy-start.4 = (bf16[768,192]{0,1:T(8,128)(2,1)S(1)}, bf16[768,192]{0,1:T(8,128)(2,1)}, u32[]{:S(2)}) copy-start(bf16[768,192]{0,1:T(8,128)(2,1)} %param.18) | copy-start | bytes 884740
  2.7 13.3 %collective-permute-start = (bf16[3,192,256]{2,1,0:T(8,128)(2,1)}, bf16[3,192,256]{2,1,0:T(8,128)(2,1)}, u32[]{:S(2)}, u32[]{:S(2)}) collective-permute-start(bf16[3,192,256]{2,1,0:T(8,128)(2,1)} %shard_map.146), channel_id=1, source_target_pairs={{0,1},{1,2},{2,3},{3,4},{4,5},{5,6},{6,7},{8,9},{9,10},{10,11},{11... | collective-permute-start | bytes 884744 | tf_op jit(solution)/shard_map/ppermute | solution.py:20
  10.6 5.5 %copy-start.6 = (bf16[3,192,256]{2,1,0:T(8,128)(2,1)S(1)}, bf16[3,192,256]{2,1,0:T(8,128)(2,1)}, u32[]{:S(2)}) copy-start(bf16[3,192,256]{2,1,0:T(8,128)(2,1)} %copy-done.5) | copy-start | bytes 884740
  16.1 10.4 %collective-permute-start.1 = (bf16[3,192,256]{2,1,0:T(8,128)(2,1)S(1)}, bf16[3,192,256]{2,1,0:T(8,128)(2,1)S(1)}, u32[]{:S(2)}, u32[]{:S(2)}) collective-permute-start(bf16[3,192,256]{2,1,0:T(8,128)(2,1)S(1)} %copy-done.6), channel_id=1, source_target_pairs={{1,0},{2,1},{3,2},{4,3},{5,4},{6,5},{7,6},{9,8},{10,9},{11,10},{12... | collective-permute-start | bytes 884744 | tf_op jit(solution)/shard_map/ppermute | solution.py:20
  24.4 11.0 %collective-permute-start.2 = (bf16[3,192,256]{2,1,0:T(8,128)(2,1)S(1)}, bf16[3,192,256]{2,1,0:T(8,128)(2,1)S(1)}, u32[]{:S(2)}, u32[]{:S(2)}) collective-permute-start(bf16[3,192,256]{2,1,0:T(8,128)(2,1)S(1)} %get-tuple-element.58.gz_upper_ref), channel_id=1, source_target_pairs={{1,0},{2,1},{3,2},{4,3},{5,4},{6,5},{7,6},{9,8},{10,9},{11,10},{12... | collective-permute-start | bytes 884744 | tf_op jit(solution)/shard_map/ppermute | solution.py:20
  35.4 1.6 %collective-permute-start.3 = (bf16[1216,128]{1,0:T(8,128)(2,1)S(1)}, bf16[1216,128]{1,0:T(8,128)(2,1)S(1)}, u32[]{:S(2)}, u32[]{:S(2)}) collective-permute-start(bf16[1216,128]{1,0:T(8,128)(2,1)S(1)} %get-tuple-element.76), channel_id=1, source_target_pairs={{0,8},{8,0},{1,9},{9,1},{2,10},{10,2},{3,11},{11,3},{4,12},{12,4},... | collective-permute-start | bytes 933896 | tf_op jit(solution)/shard_map/ppermute | solution.py:310
  37.1 8.2 %collective-permute-start.6 = (bf16[304,128]{1,0:T(8,128)(2,1)S(1)}, bf16[304,128]{1,0:T(8,128)(2,1)S(1)}, u32[]{:S(2)}, u32[]{:S(2)}) collective-permute-start(bf16[304,128]{1,0:T(8,128)(2,1)S(1)} %get-tuple-element.90), channel_id=1, source_target_pairs={{0,17},{1,16},{2,19},{3,18},{4,21},{5,20},{6,23},{7,22},{16,1},{17... | collective-permute-start | bytes 233480 | tf_op jit(solution)/shard_map/ppermute | solution.py:310
  40.7 4.6 %collective-permute-start.5 = (bf16[304,128]{1,0:T(8,128)(2,1)S(1)}, bf16[304,128]{1,0:T(8,128)(2,1)S(1)}, u32[]{:S(2)}, u32[]{:S(2)}) collective-permute-start(bf16[304,128]{1,0:T(8,128)(2,1)S(1)} %get-tuple-element.91), channel_id=1, source_target_pairs={{0,16},{1,17},{2,18},{3,19},{4,20},{5,21},{6,22},{7,23},{16,0},{17... | collective-permute-start | bytes 233480 | tf_op jit(solution)/shard_map/ppermute | solution.py:310
  41.3 4.4 %collective-permute-start.4 = (bf16[304,128]{1,0:T(8,128)(2,1)S(1)}, bf16[304,128]{1,0:T(8,128)(2,1)S(1)}, u32[]{:S(2)}, u32[]{:S(2)}) collective-permute-start(bf16[304,128]{1,0:T(8,128)(2,1)S(1)} %get-tuple-element.89), channel_id=1, source_target_pairs={{0,1},{1,0},{2,3},{3,2},{4,5},{5,4},{6,7},{7,6},{16,17},{17,16},{1... | collective-permute-start | bytes 233480 | tf_op jit(solution)/shard_map/ppermute | solution.py:310
  45.7 7.9 %collective-permute-start.9 = (bf16[304,128]{1,0:T(8,128)(2,1)S(1)}, bf16[304,128]{1,0:T(8,128)(2,1)S(1)}, u32[]{:S(2)}, u32[]{:S(2)}) collective-permute-start(bf16[304,128]{1,0:T(8,128)(2,1)S(1)} %fusion.1), channel_id=1, source_target_pairs={{0,6},{1,7},{2,4},{3,5},{4,2},{5,3},{6,0},{7,1},{8,14},{9,15},{10,... | collective-permute-start | bytes 233480 | tf_op jit(solution)/shard_map/ppermute | solution.py:310
  48.7 6.5 %collective-permute-start.8 = (bf16[304,128]{1,0:T(8,128)(2,1)S(1)}, bf16[304,128]{1,0:T(8,128)(2,1)S(1)}, u32[]{:S(2)}, u32[]{:S(2)}) collective-permute-start(bf16[304,128]{1,0:T(8,128)(2,1)S(1)} %fusion.1), channel_id=1, source_target_pairs={{0,4},{1,5},{2,6},{3,7},{4,0},{5,1},{6,2},{7,3},{8,12},{9,13},{10,... | collective-permute-start | bytes 233480 | tf_op jit(solution)/shard_map/ppermute | solution.py:310
  48.7 6.5 %collective-permute-start.7 = (bf16[304,128]{1,0:T(8,128)(2,1)S(1)}, bf16[304,128]{1,0:T(8,128)(2,1)S(1)}, u32[]{:S(2)}, u32[]{:S(2)}) collective-permute-start(bf16[304,128]{1,0:T(8,128)(2,1)S(1)} %fusion.1), channel_id=1, source_target_pairs={{0,2},{1,3},{2,0},{3,1},{4,6},{5,7},{6,4},{7,5},{8,10},{9,11},{10,... | collective-permute-start | bytes 233480 | tf_op jit(solution)/shard_map/ppermute | solution.py:310
  50.2 11.0 %collective-permute-start.13 = (bf16[3,192,256]{2,1,0:T(8,128)(2,1)S(1)}, bf16[3,192,256]{2,1,0:T(8,128)(2,1)S(1)}, u32[]{:S(2)}, u32[]{:S(2)}) collective-permute-start(bf16[3,192,256]{2,1,0:T(8,128)(2,1)S(1)} %get-tuple-element.60.refs_2_.gz_lower_ref), channel_id=1, source_target_pairs={{0,1},{1,2},{2,3},{3,4},{4,5},{5,6},{6,7},{8,9},{9,10},{10,11},{11... | collective-permute-start | bytes 884744 | tf_op jit(solution)/shard_map/ppermute | solution.py:20
  55.3 8.3 %collective-permute-start.12 = (bf16[304,128]{1,0:T(8,128)(2,1)S(1)}, bf16[304,128]{1,0:T(8,128)(2,1)S(1)}, u32[]{:S(2)}, u32[]{:S(2)}) collective-permute-start(bf16[304,128]{1,0:T(8,128)(2,1)S(1)} %add_convert_fusion.1), channel_id=1, source_target_pairs={{0,17},{1,16},{2,19},{3,18},{4,21},{5,20},{6,23},{7,22},{16,1},{17... | collective-permute-start | bytes 233480 | tf_op jit(solution)/shard_map/ppermute | solution.py:310
  58.0 5.6 %collective-permute-start.11 = (bf16[304,128]{1,0:T(8,128)(2,1)S(1)}, bf16[304,128]{1,0:T(8,128)(2,1)S(1)}, u32[]{:S(2)}, u32[]{:S(2)}) collective-permute-start(bf16[304,128]{1,0:T(8,128)(2,1)S(1)} %add_convert_fusion.1), channel_id=1, source_target_pairs={{0,16},{1,17},{2,18},{3,19},{4,20},{5,21},{6,22},{7,23},{16,0},{17... | collective-permute-start | bytes 233480 | tf_op jit(solution)/shard_map/ppermute | solution.py:310
  58.6 5.0 %collective-permute-start.10 = (bf16[304,128]{1,0:T(8,128)(2,1)S(1)}, bf16[304,128]{1,0:T(8,128)(2,1)S(1)}, u32[]{:S(2)}, u32[]{:S(2)}) collective-permute-start(bf16[304,128]{1,0:T(8,128)(2,1)S(1)} %add_convert_fusion.1), channel_id=1, source_target_pairs={{0,1},{1,0},{2,3},{3,2},{4,5},{5,4},{6,7},{7,6},{16,17},{17,16},{1... | collective-permute-start | bytes 233480 | tf_op jit(solution)/shard_map/ppermute | solution.py:310
  63.7 1.7 %collective-permute-start.14 = (bf16[4,304,128]{2,1,0:T(8,128)(2,1)S(1)}, bf16[4,304,128]{2,1,0:T(8,128)(2,1)S(1)}, u32[]{:S(2)}, u32[]{:S(2)}) collective-permute-start(bf16[4,304,128]{2,1,0:T(8,128)(2,1)S(1)} %pad_maximum_fusion.mine_ref), channel_id=1, source_target_pairs={{0,8},{8,0},{1,9},{9,1},{2,10},{10,2},{3,11},{11,3},{4,12},{12,4},... | collective-permute-start | bytes 933896 | tf_op jit(solution)/shard_map/ppermute | solution.py:310
  (5 other events, 5.7 us)

commit v3 on v2

--- a/solution.py
+++ b/solution.py
@@ -12,12 +12,6 @@
 GROUP = 16
 BF16 = jnp.bfloat16
 F32 = jnp.float32
-
-
-def shifted(value, axis, steps):
-    count = lax.axis_size(axis)
-    initial, last = (max(0, -steps), min(count, count - steps))
-    return lax.ppermute(value, axis, [(source, source + steps) for source in range(initial, last)])
 
 
 def slide_lanes(value, steps):
@@ -69,8 +63,10 @@
     vec_ref, bin_ref, win_ref, wint_ref, wout_ref, woutt_ref = weights
     normed_ref, act_ref, gout_ref, gh_ref = kept
 
+    width = g_ref.shape[2]
+
     def vec(index):
-        return vec_ref[:, index : index + 1]
+        return across(vec_ref[index], width)
 
     hidden_units = win_ref.shape[1]
     mixed = conv_row(tall_ref, taps_ref, row) + vec(0)
@@ -84,7 +80,7 @@
     span = 256
     for start in range(0, hidden_units, span):
         part = slice(start, start + span)
-        hidden = jnp.dot(wint_ref[part, :], normed, preferred_element_type=F32) + bin_ref[part, :]
+        hidden = jnp.dot(wint_ref[part, :], normed, preferred_element_type=F32) + across(bin_ref[part, :], width)
         grad_act = jnp.dot(wout_ref[part, :], gout, preferred_element_type=F32)
         cdf = 0.5 * (1.0 + lax.erf(hidden * 0.7071067811865476))
         slope = cdf + hidden * jnp.exp(-0.5 * hidden * hidden) * 0.3989422804014327
@@ -147,14 +143,37 @@
     return jnp.concatenate([summed, jnp.zeros((1, span), F32)], axis=0)
 
 
-def inner_kernel(
-    x_ref, g_ref, kernel_ref, vec_ref, bin_ref, win_ref, wint_ref, wout_ref, woutt_ref,
-    taps_ref, back_ref, out_ref, gz_ref, dwin_ref, dwout_ref, dtaps_ref,
-    *kept,
-):
-    hidden_units = win_ref.shape[1]
+def prepare_kernel(
+    kernel_ref, win_ref, woutt_ref, bin_in_ref, *refs
+):
+    count = len(refs) - 6
+    vectors, (taps_ref, back_ref, vec_ref, bin_ref, wint_ref, wout_ref) = refs[:count], refs[count:]
     spread_taps(kernel_ref, taps_ref, False)
     spread_taps(kernel_ref, back_ref, True)
+    for source, target in ((win_ref, wint_ref), (woutt_ref, wout_ref)):
+        target[...] = source[...].T
+    chans = vec_ref.shape[1]
+    for index, ref in enumerate(vectors):
+        row = jnp.concatenate([ref[...], jnp.zeros((1, -chans % 128), F32)], axis=1)
+        for start in range(0, chans, 128):
+            size = min(128, chans - start)
+            square = jnp.broadcast_to(row[:, start : start + 128], (128, 128)).T
+            vec_ref[index, start : start + size, :] = square[:size]
+    for index in range(bin_in_ref.shape[0]):
+        square = jnp.broadcast_to(bin_in_ref[index : index + 1, :], (128, 128))
+        bin_ref[index * 128 : (index + 1) * 128, :] = square.T
+
+
+def across(value, width):
+    return jnp.concatenate([value] * (width // 128), axis=1)
+
+
+def inner_kernel(
+    x_ref, g_ref, taps_ref, vec_ref, bin_ref, win_ref, wint_ref, wout_ref, woutt_ref,
+    out_ref, gz_ref, dwin_ref, dwout_ref, dtaps_ref,
+    *kept,
+):
+    hidden_units = win_ref.shape[1]
     weights = (vec_ref, bin_ref, win_ref, wint_ref, wout_ref, woutt_ref)
     all_rows(x_ref, g_ref.at[pl.ds(REACH, out_ref.shape[0])], taps_ref, weights, out_ref, gz_ref, kept)
     for start in range(0, hidden_units, 256):
@@ -164,17 +183,24 @@
         dtaps_ref[group] = tap_terms(x_ref, gz_ref, group)
 
 
-def upper_kernel(
-    x_ref, above_ref, g_ref, taps_ref, vec_ref, bin_ref, win_ref, wint_ref, wout_ref, woutt_ref,
+def with_halo(x_ref, halo_ref, tall_ref, low):
+    shared = 2 * REACH
+    tall_ref[pl.ds(shared * low, REACH)] = halo_ref[...]
+    tall_ref[pl.ds(REACH * (1 - low), shared)] = x_ref[pl.ds((x_ref.shape[0] - shared) * low, shared)]
+
+
+def first_kernel(
+    place_ref, x_ref, halo_ref, g_ref, taps_ref, vec_ref, bin_ref, win_ref, wint_ref, wout_ref, woutt_ref,
     dwin_in_ref, dwout_in_ref, dtaps_in_ref,
     out_ref, gz_ref, dwin_ref, dwout_ref, dtaps_ref,
     tall_ref, *kept,
 ):
     hidden_units = win_ref.shape[1]
-    tall_ref[0:REACH] = above_ref[...]
-    tall_ref[REACH:] = x_ref[0 : 2 * REACH]
+    low = place_ref[2]
+    with_halo(x_ref, halo_ref, tall_ref, low)
     weights = (vec_ref, bin_ref, win_ref, wint_ref, wout_ref, woutt_ref)
-    all_rows(tall_ref, g_ref.at[pl.ds(0, REACH)], taps_ref, weights, out_ref, gz_ref, kept)
+    rows = g_ref.at[pl.ds((x_ref.shape[0] - REACH) * low, REACH)]
+    all_rows(tall_ref, rows, taps_ref, weights, out_ref, gz_ref, kept)
     for start in range(0, hidden_units, 256):
         part = slice(start, start + 256)
         for index, (ref, before_ref) in enumerate(((dwin_ref, dwin_in_ref), (dwout_ref, dwout_in_ref))):
@@ -183,15 +209,15 @@
         dtaps_ref[group] = tap_terms(tall_ref, gz_ref, group) + dtaps_in_ref[group]
 
 
-def lower_kernel(
-    x_ref, below_ref, g_ref, taps_ref, vec_ref, bin_ref, win_ref, wint_ref, wout_ref, woutt_ref,
+def second_kernel(
+    place_ref, x_ref, halo_ref, g_ref, taps_ref, vec_ref, bin_ref, win_ref, wint_ref, wout_ref, woutt_ref,
     out_ref, gz_ref, tall_ref, *kept,
 ):
-    rows = x_ref.shape[0]
-    tall_ref[0 : 2 * REACH] = x_ref[rows - 2 * REACH :]
-    tall_ref[2 * REACH :] = below_ref[...]
+    low = 1 - place_ref[2]
+    with_halo(x_ref, halo_ref, tall_ref, low)
     weights = (vec_ref, bin_ref, win_ref, wint_ref, wout_ref, woutt_ref)
-    all_rows(tall_ref, g_ref.at[pl.ds(rows - REACH, REACH)], taps_ref, weights, out_ref, gz_ref, kept)
+    rows = g_ref.at[pl.ds((x_ref.shape[0] - REACH) * low, REACH)]
+    all_rows(tall_ref, rows, taps_ref, weights, out_ref, gz_ref, kept)
 
 
 def terms_kernel(
@@ -227,44 +253,49 @@
 
 
 def input_kernel(
-    out_upper_ref, out_inner_ref, out_lower_ref, gz_upper_ref, gz_inner_ref, gz_lower_ref,
-    below_ref, g_ref, taps_ref,
+    place_ref, out_first_ref, out_inner_ref, out_second_ref, gz_first_ref, gz_inner_ref, gz_second_ref,
+    halo_ref, g_ref, taps_ref,
     out_ref, grad_ref, tall_ref,
 ):
+    low = place_ref[2]
     rows = g_ref.shape[0]
-    at = 0
-    for ref in (gz_upper_ref, gz_inner_ref, gz_lower_ref, below_ref):
-        tall_ref[at : at + ref.shape[0]] = ref[...]
-        at += ref.shape[0]
-    at = 0
-    for ref in (out_upper_ref, out_inner_ref, out_lower_ref):
-        out_ref[at : at + ref.shape[0]] = ref[...]
-        at += ref.shape[0]
+    inner = rows - 2 * REACH
+    tall_ref[pl.ds(rows * (1 - low), REACH)] = gz_second_ref[...]
+    tall_ref[pl.ds(REACH * (2 - low), inner)] = gz_inner_ref[...]
+    tall_ref[pl.ds(REACH + inner * low, REACH)] = gz_first_ref[...]
+    tall_ref[pl.ds(rows * low, REACH)] = halo_ref[...]
+    out_ref[REACH : REACH + inner] = out_inner_ref[...]
+    out_ref[pl.ds((rows - REACH) * low, REACH)] = out_first_ref[...]
+    out_ref[pl.ds((rows - REACH) * (1 - low), REACH)] = out_second_ref[...]
 
     def step(row, carry):
-        at = row + REACH
+        at = row + REACH * low
         grad_ref[at] = (g_ref[at].astype(F32) + conv_row(tall_ref, taps_ref, row)).astype(BF16)
         return carry
 
     lax.fori_loop(0, rows - REACH, step, 0)
 
 
-def input_upper_kernel(
-    above_ref, gz_upper_ref, gz_inner_ref, gz_lower_ref, g_ref, taps_ref, rest_ref,
+def input_rest_kernel(
+    place_ref, halo_ref, gz_first_ref, gz_inner_ref, gz_second_ref, g_ref, taps_ref, rest_ref,
     grad_ref, tall_ref, part_ref, sem,
 ):
-    tall_ref[0:REACH] = above_ref[...]
-    tall_ref[REACH : 2 * REACH] = gz_upper_ref[...]
-    inner = gz_inner_ref.shape[0]
-    for at in range(REACH):
-        tall_ref[2 * REACH + at] = gz_inner_ref[at] if at < inner else gz_lower_ref[at - inner]
+    low = 1 - place_ref[2]
+    rows = g_ref.shape[0]
+    inner = rows - 2 * REACH
+    near = REACH - inner
+    tall_ref[pl.ds(2 * REACH * low, REACH)] = halo_ref[...]
+    tall_ref[REACH : 2 * REACH] = gz_second_ref[...]
+    tall_ref[pl.ds(2 * REACH * (1 - low) + near * low, inner)] = gz_inner_ref[...]
+    tall_ref[pl.ds((2 * REACH + inner) * (1 - low), near)] = gz_first_ref[pl.ds((REACH - near) * low, near)]
+    first = (rows - REACH) * low
 
     def step(row, carry):
-        part_ref[row] = (g_ref[row].astype(F32) + conv_row(tall_ref, taps_ref, row)).astype(BF16)
+        part_ref[row] = (g_ref[first + row].astype(F32) + conv_row(tall_ref, taps_ref, row)).astype(BF16)
         return carry
 
     lax.fori_loop(0, REACH, step, 0)
-    copy = pltpu.make_async_copy(part_ref, grad_ref.at[pl.ds(0, REACH)], sem)
+    copy = pltpu.make_async_copy(part_ref, grad_ref.at[pl.ds(first, REACH)], sem)
     copy.start()
     copy.wait()
 
@@ -293,14 +324,13 @@
                 taps_ref[tap, :, group * GROUP : (group + 1) * GROUP] = piece[:TAPS, tap * GROUP : (tap + 1) * GROUP]
 
 
-def edge_kernel(x_ref, edge_ref, sem, *, start):
-    copy = pltpu.make_async_copy(x_ref.at[pl.ds(start, REACH)], edge_ref, sem)
-    copy.start()
-    copy.wait()
+def edge_kernel(place_ref, x_ref, edge_ref, *, first):
+    low = place_ref[2] if first else 1 - place_ref[2]
+    edge_ref[...] = x_ref[pl.ds((x_ref.shape[0] - REACH) * low, REACH)]
 
 
 PARAMS = pltpu.CompilerParams(vmem_limit_bytes=20 * 1024 * 1024)
-SMALL = pltpu.CompilerParams(vmem_limit_bytes=4 * 1024 * 1024)
+SMALL = pltpu.CompilerParams(vmem_limit_bytes=8 * 1024 * 1024)
 IN_VMEM = pl.BlockSpec(memory_space=pltpu.VMEM)
 IN_SMEM = pl.BlockSpec(memory_space=pltpu.SMEM)
 
@@ -323,7 +353,8 @@
     core = lax.axis_index("core").astype(jnp.uint32)
     quarter = (2 * lax.axis_index("x") + lax.axis_index("space") % 2).astype(jnp.uint32)
     turns = [quarter ^ turn for turn in range(4)]
-    place = jnp.stack([core, quarter]).astype(jnp.int32)
+    even = (1 - lax.axis_index("space") % 2).astype(jnp.uint32)
+    place = jnp.stack([core, quarter, even]).astype(jnp.int32)
     features, place, *turns = lax.optimization_barrier((features, place, *turns))
     x = jnp.swapaxes(features[0, 0], 1, 2)
     g = jnp.swapaxes(cotangent[0, 0], 1, 2)
@@ -333,19 +364,23 @@
     narrow = jax.ShapeDtypeStruct((REACH, chans, width), BF16)
     image = jax.ShapeDtypeStruct((rows, chans, width), BF16)
 
-    def edge(start):
+    def edge(first):
         return pl.pallas_call(
-            lambda *refs: edge_kernel(*refs, start=start),
+            lambda *refs: edge_kernel(*refs, first=first),
             out_shape=narrow,
-            in_specs=[pl.BlockSpec(memory_space=pl.ANY)],
+            in_specs=[IN_SMEM, IN_VMEM],
             out_specs=IN_VMEM,
-            scratch_shapes=[pltpu.SemaphoreType.DMA(())],
             compiler_params=SMALL,
-        )(x)
-
-    above = shifted(edge(rows - REACH), "space", 1)
-    vectors = jnp.stack([dw_bias, ln_gain, ln_bias, b_out, layer_scale], axis=1)
-    weights = (vectors, b_in[:, None], w_in, w_in.T, w_out, w_out.T)
+        )(place, x)
+
+    def first_swap(value):
+        return swap(value, "space", 1)
+
+    def second_swap(value):
+        pairs = [(low, low + 1) for low in range(1, strips - 1, 2)]
+        return lax.ppermute(value, "space", pairs + [(high, low) for low, high in pairs])
+
+    first_halo = first_swap(edge(True))
     devices = lax.axis_size("x") * lax.axis_size("core") * strips
     scale = float(devices * rows * width) ** (-0.5)
     groups = chans // GROUP
@@ -366,36 +401,48 @@
     spread = jax.ShapeDtypeStruct((groups, span, 2 * span), BF16)
     matrix = jax.ShapeDtypeStruct((chans, hidden_units), F32)
     terms = (matrix, matrix, jax.ShapeDtypeStruct((groups, 8, span), F32))
-    taps, back_taps, out_inner, gz_inner, *inner_terms = pl.pallas_call(
+    vectors = (dw_bias, ln_gain, ln_bias, b_out, layer_scale)
+    across_lanes = jax.ShapeDtypeStruct((len(vectors), chans, 128), F32)
+    hidden_lanes = jax.ShapeDtypeStruct((hidden_units, 128), F32)
+    turned = jax.ShapeDtypeStruct((hidden_units, chans), BF16)
+    taps, back_taps, vectors, bias, w_in_t, w_out_turned = pl.pallas_call(
+        prepare_kernel,
+        out_shape=(spread, spread, across_lanes, hidden_lanes, turned, turned),
+        in_specs=[IN_VMEM] * (4 + len(vectors)),
+        out_specs=(IN_VMEM,) * 6,
+        compiler_params=SMALL,
+    )(dw_kernel, w_in, w_out.T, b_in.reshape(-1, 128), *[vector[None] for vector in vectors])
+    weights = (vectors, bias, w_in, w_in_t, w_out_turned, w_out.T)
+    second_edge, taps = lax.optimization_barrier((edge(False), taps))
+    second_halo = second_swap(second_edge)
+    out_inner, gz_inner, *inner_terms = pl.pallas_call(
         inner_kernel,
-        out_shape=(spread, spread, middle, middle, *terms),
+        out_shape=(middle, middle, *terms),
         in_specs=[IN_VMEM] * 9,
-        out_specs=(IN_VMEM,) * 7,
+        out_specs=(IN_VMEM,) * 5,
         scratch_shapes=scratch(kept(inner)),
         compiler_params=PARAMS,
-    )(x, g, dw_kernel, *weights)
-    above, top, out_inner = lax.optimization_barrier((above, edge(0), out_inner))
-    below = shifted(top, "space", -1)
+    )(x, g, taps, *weights)
     half_rows = hidden_units // 128 * chans + groups // 2 * 8
     half_rows = (half_rows + 63) // 64 * 64
     half = jax.ShapeDtypeStruct((half_rows, 128), BF16)
-    out_upper, gz_upper, *upper_terms = pl.pallas_call(
-        upper_kernel,
+    out_first, gz_first, *first_terms = pl.pallas_call(
+        first_kernel,
         out_shape=(narrow, narrow, *terms),
-        in_specs=[IN_VMEM] * 13,
+        in_specs=[IN_SMEM] + [IN_VMEM] * 13,
         out_specs=(IN_VMEM,) * 5,
         scratch_shapes=scratch((tall, *kept(REACH))),
         compiler_params=PARAMS,
-    )(x, above, g, taps, *weights, *inner_terms)
-    gz_below = shifted(gz_upper, "space", -1)
-    out_lower, gz_lower, *lower_kept = pl.pallas_call(
-        lower_kernel,
+    )(place, x, first_halo, g, taps, *weights, *inner_terms)
+    gz_first_halo = first_swap(gz_first)
+    out_second, gz_second, *second_kept = pl.pallas_call(
+        second_kernel,
         out_shape=(narrow, narrow, tall, *kept(REACH)),
-        in_specs=[IN_VMEM] * 10,
+        in_specs=[IN_SMEM] + [IN_VMEM] * 10,
         out_specs=(IN_VMEM,) * 7,
         compiler_params=PARAMS,
-    )(x, below, g, taps, *weights)
-    gz_above = shifted(gz_lower, "space", 1)
+    )(place, x, second_halo, g, taps, *weights)
+    gz_second_halo = second_swap(gz_second)
     keep, send = pl.pallas_call(
         lambda *refs: terms_kernel(*refs, scale=scale),
         out_shape=(half, half),
@@ -403,8 +450,8 @@
         out_specs=(IN_VMEM,) * 2,
         scratch_shapes=[pltpu.VMEM((2, half_rows, 128), BF16)],
         compiler_params=PARAMS,
-    )(place, lower_kept[0], gz_lower, *lower_kept[1:], *upper_terms)
-    keep, send, gz_below = lax.optimization_barrier((keep, send, gz_below))
+    )(place, second_kept[0], gz_second, *second_kept[1:], *first_terms)
+    keep, send, gz_first_halo = lax.optimization_barrier((keep, send, gz_first_halo))
 
     summed = added(keep, swap(send, "core", 1)).reshape(4, half_rows // 4, 128)
 
@@ -418,31 +465,31 @@
     out, grad_rest = pl.pallas_call(
         input_kernel,
         out_shape=(image, image),
-        in_specs=[IN_VMEM] * 9,
+        in_specs=[IN_SMEM] + [IN_VMEM] * 9,
         out_specs=(IN_VMEM, IN_VMEM),
         scratch_shapes=[pltpu.VMEM((rows + REACH, chans, width), BF16)],
         compiler_params=PARAMS,
-    )(out_upper, out_inner, out_lower, gz_upper, gz_inner, gz_lower, gz_below, g, back_taps)
-    own, grad_rest = lax.optimization_barrier((own, grad_rest))
+    )(place, out_first, out_inner, out_second, gz_first, gz_inner, gz_second, gz_first_halo, g, back_taps)
     bit = 2
     while bit < strips:
         masks = (bit, 2 * bit, 3 * bit) if 2 * bit < strips else (bit,)
         own = added(own, *[swap(own, "space", mask) for mask in masks])
         bit *= 4
+    own, grad_rest = lax.optimization_barrier((own, grad_rest))
     mine = jnp.stack([own] + [partner(own, turn) for turn in (1, 2, 3)])
     grad_input = pl.pallas_call(
-        input_upper_kernel,
+        input_rest_kernel,
         out_shape=image,
-        in_specs=[IN_VMEM] * 6 + [pl.BlockSpec(memory_space=pl.ANY)],
+        in_specs=[IN_SMEM] + [IN_VMEM] * 6 + [pl.BlockSpec(memory_space=pl.ANY)],
         out_specs=pl.BlockSpec(memory_space=pl.ANY),
         scratch_shapes=[
             pltpu.VMEM((3 * REACH, chans, width), BF16),
             pltpu.VMEM((REACH, chans, width), BF16),
             pltpu.SemaphoreType.DMA(()),
         ],
-        input_output_aliases={6: 0},
-        compiler_params=PARAMS,
-    )(gz_above, gz_upper, gz_inner, gz_lower, g, back_taps, grad_rest)
+        input_output_aliases={7: 0},
+        compiler_params=PARAMS,
+    )(place, gz_second_halo, gz_first, gz_inner, gz_second, g, back_taps, grad_rest)
     mine, grad_input = lax.optimization_barrier((mine, grad_input))
     other = swap(mine, "core", 1)
     grad_w_in, grad_w_out_t, grad_kernel = pl.pallas_call(

time: 67.9 us -> 65.8 us (0.969)
  starting transfers between devices: 24.1 us -> 18.6 us
  waiting for transfers between devices: 10.6 us -> 14.4 us
  Pallas kernels: 27.8 us -> 30.1 us
  local copies, waits for them, and re-layouts: 3.18 us -> 1.21 us
    ppermute x4 -> x2, starting transfers between devices: 11.8 us -> 1.35 us  [second_swap(): lax.ppermute(value, 'space', pairs + [(high, low) for low, high in pairs])]
    ppermute x11 -> x13, waiting for transfers between devices: 5.17 us -> 14.4 us  [swap(): lax.ppermute(value, axis, [(source, source ^ mask) for source in range(co...]
    ppermute x4 -> x2, waiting for transfers between devices: 5.42 us -> 0.01 us  [second_swap(): lax.ppermute(value, 'space', pairs + [(high, low) for low, high in pairs])]
    ppermute x11 -> x13, starting transfers between devices: 12.4 us -> 17.2 us  [swap(): lax.ppermute(value, axis, [(source, source ^ mask) for source in range(co...]
    pallas_call x7 -> x8, Pallas kernels: 24.1 us -> 26.3 us  [the longest x1 6.51 us: on_device(): pl.pallas_call(first_kernel, out_shape=(narrow, narrow, *terms), in_specs...]
    unnamed x30 -> x24, local copies, waits for them, and re-layouts: 2.85 us -> 1.18 us
  transfers between devices with their start and end apart: 15 -> 15, of which waited for: 7 -> 8; matrix products, arithmetic and copies ran while one was open for 1% -> 0% of each run, Pallas kernels for 38% -> 43%
where the time goes in v3:
time: 65.8 us; the launch traced here: 65.5 us
  Pallas kernels  30.1 us (46%)
  starting transfers between devices  18.6 us (28%)
  waiting for transfers between devices  14.4 us (22%)
  local copies, waits for them, and re-layouts  1.21 us (2%)
  between operations  0.94 us (1%)
    ppermute x13, starting transfers between devices, swap(): lax.ppermute(value, axis, [(source, source ^ mask) for source in range(co...  17.2 us
    ppermute x13, waiting for transfers between devices, swap(): lax.ppermute(value, axis, [(source, source ^ mask) for source in range(co...  14.4 us
    pallas_call x1, Pallas kernels, on_device(): pl.pallas_call(first_kernel, out_shape=(narrow, narrow, *terms), in_specs...  6.51 us
    pallas_call x1, Pallas kernels, on_device(): pl.pallas_call(second_kernel, out_shape=(narrow, narrow, tall, *kept(REAC...  4.99 us
    pallas_call x1, Pallas kernels, on_device(): pl.pallas_call(input_kernel, out_shape=(image, image), in_specs=[IN_SMEM]...  4.45 us
    pallas_call x1, Pallas kernels, on_device(): pl.pallas_call(inner_kernel, out_shape=(middle, middle, *terms), in_specs...  4.02 us
    pallas_call x1, Pallas kernels, on_device(): pl.pallas_call(input_rest_kernel, out_shape=image, in_specs=[IN_SMEM] + [...  2.97 us
    pallas_call x1, Pallas kernels, on_device(): pl.pallas_call(prepare_kernel, out_shape=(spread, spread, across_lanes, h...  2.24 us
  transfers between devices with their start and end apart: 15, of which 8 were waited for; matrix products, arithmetic and copies ran while one was open for 0% of the time, Pallas kernels for 43%

profile of v3, /device:TPU:0, one launch (start us, length us, event | category | flops | bytes accessed | tf_op | source)
XLA Modules:
  0.0 65.5 jit_solution(4673533955110210830)
XLA Ops:
  0.8 1.1 %copy-done.1 = bf16[1,1,8,256,192]{3,4,2,1,0:T(8,128)(2,1)S(1)} copy-done((bf16[1,1,8,256,192]{3,4,2,1,0:T(8,128)(2,1)S(1)}, bf16[1,1,8,256,192]{3,4,2,1,0:T(8,128)(2,1)}, u32[]{:S(2)}) %copy-start.1) | copy-done | bytes 786456
  2.5 3.0 %collective-permute-start = (bf16[3,192,256]{2,1,0:T(8,128)(2,1)S(1)}, bf16[3,192,256]{2,1,0:T(8,128)(2,1)S(1)}, u32[]{:S(2)}, u32[]{:S(2)}) collective-permute-start(bf16[3,192,256]{2,1,0:T(8,128)(2,1)S(1)} %shard_map.146), channel_id=1, source_target_pairs={{0,1},{1,0},{2,3},{3,2},{4,5},{5,4},{6,7},{7,6},{8,9},{9,8},{10,11... | collective-permute-start | bytes 884744 | tf_op jit(solution)/shard_map/ppermute | solution.py:340
  6.2 2.2 %shard_map.148 = (bf16[12,112,224]{2,1,0:T(8,128)(2,1)S(1)}, bf16[12,112,224]{2,1,0:T(8,128)(2,1)S(1)}, f32[5,192,128]{2,1,0:T(8,128)S(1)}, f32[768,128]{1,0:T(8...) custom-call(f32[7,7,192]{2,1,0:T(8,128)S(1)} %copy-done.5, bf16[192,768]{1,0:T(8,128)(2,1)S(1)} %copy-done.3, ...), custom_call_target="tpu_custom_call" | custom-call | tf_op jit(solution)/shard_map/pallas_call | solution.py:408
  8.5 0.7 %collective-permute-start.1 = (bf16[3,192,256]{2,1,0:T(8,128)(2,1)S(1)}, bf16[3,192,256]{2,1,0:T(8,128)(2,1)S(1)}, u32[]{:S(2)}, u32[]{:S(2)}) collective-permute-start(bf16[3,192,256]{2,1,0:T(8,128)(2,1)S(1)} %shard_map.147), channel_id=1, source_target_pairs={{1,2},{3,4},{5,6},{2,1},{4,3},{6,5},{9,10},{11,12},{13,14},{10,9},... | collective-permute-start | bytes 884744 | tf_op jit(solution)/shard_map/ppermute | solution.py:381
  9.2 4.0 %shard_map.149 = (bf16[2,192,256]{2,1,0:T(8,128)(2,1)S(1)}, bf16[2,192,256]{2,1,0:T(8,128)(2,1)S(1)}, f32[192,768]{1,0:T(8,128)S(1)}, f32[192,768]{1,0:T(8,128)S(1)}, f32[12,8,112]{2,1,0:T(8,128)S(1)}) custom-call(bf16[8,192,256]{2,1,0:T(8,128)(2,1)S(1)} %bitcast.44, bf16[8,192,256]{2,1,0:T(8,128)(2,1)S(1)} %bitcast.37, ...), custom_call_target="tpu_custom_call" | custom-call | tf_op jit(solution)/shard_map/pallas_call | solution.py:418
  13.2 5.0 %collective-permute-done.halo_ref = bf16[3,192,256]{2,1,0:T(8,128)(2,1)S(1)} collective-permute-done((bf16[3,192,256]{2,1,0:T(8,128)(2,1)S(1)}, bf16[3,192,256]{2,1,0:T(8,128)(2,1)S(1)}, u32[]{:S(2)}, u32[]{:S(2)}) %collective-permute-start) | collective-permute-done | bytes 294944 | tf_op jit(solution)/shard_map/ppermute | solution.py:340
  18.2 6.5 %shard_map.150 = (bf16[3,192,256]{2,1,0:T(8,128)(2,1)S(1)}, bf16[3,192,256]{2,1,0:T(8,128)(2,1)S(1)}, f32[192,768]{1,0:T(8,128)S(1)}, f32[192,768]{1,0:T(8,128)S(1)}, f32[12,8,112]{2,1,0:T(8,128)S(1)}) custom-call(s32[3]{0:T(128)S(1)} %add_convert_fusion.2.refs_0_.place_ref, bf16[8,192,256]{2,1,0:T(8,128)(2,1)S(1)} %bitcast.45, ...), custom_call_target="tpu_custom_call" | custom-call | tf_op jit(solution)/shard_map/pallas_call | solution.py:429
  24.7 2.5 %collective-permute-start.2 = (bf16[3,192,256]{2,1,0:T(8,128)(2,1)S(1)}, bf16[3,192,256]{2,1,0:T(8,128)(2,1)S(1)}, u32[]{:S(2)}, u32[]{:S(2)}) collective-permute-start(bf16[3,192,256]{2,1,0:T(8,128)(2,1)S(1)} %get-tuple-element.65.gz_first_ref), channel_id=1, source_target_pairs={{0,1},{1,0},{2,3},{3,2},{4,5},{5,4},{6,7},{7,6},{8,9},{9,8},{10,11... | collective-permute-start | bytes 884744 | tf_op jit(solution)/shard_map/ppermute | solution.py:340
  27.2 5.0 %shard_map.151 = (bf16[3,192,256]{2,1,0:T(8,128)(2,1)S(1)}, bf16[3,192,256]{2,1,0:T(8,128)(2,1)S(1)}, bf16[9,192,256]{2,1,0:T(8,128)(2,1)S(1)}, bf16[3,192,256]{...) custom-call(s32[3]{0:T(128)S(1)} %add_convert_fusion.2.refs_0_.place, ...), custom_call_target="tpu_custom_call" | custom-call | tf_op jit(solution)/shard_map/pallas_call | solution.py:438
  32.2 2.1 %shard_map.152 = (bf16[1216,128]{1,0:T(8,128)(2,1)S(1)}, bf16[1216,128]{1,0:T(8,128)(2,1)S(1)}) custom-call(s32[3]{0:T(128)S(1)} %add_convert_fusion.2.refs_0_.place_ref, bf16[9,192,256]{2,1,0:T(8,128)(2,1)S(1)} %get-tuple-element.68.refs_1_, bf16[3,192,256]{2,1,0:T(8,128)(2,1)S(1)} %get-tuple-element.67.refs_2_.gz_second_ref, ...), custom_call_target="tpu_custom_call" | custom-call | tf_op jit(solution)/shard_map/pallas_call | solution.py:446
  34.4 1.6 %collective-permute-done.3 = bf16[1216,128]{1,0:T(8,128)(2,1)S(1)} collective-permute-done((bf16[1216,128]{1,0:T(8,128)(2,1)S(1)}, bf16[1216,128]{1,0:T(8,128)(2,1)S(1)}, u32[]{:S(2)}, u32[]{:S(2)}) %collective-permute-start.3) | collective-permute-done | bytes 311328 | tf_op jit(solution)/shard_map/ppermute | solution.py:340
  36.1 1.0 %collective-permute-start.6 = (bf16[304,128]{1,0:T(8,128)(2,1)S(1)}, bf16[304,128]{1,0:T(8,128)(2,1)S(1)}, u32[]{:S(2)}, u32[]{:S(2)}) collective-permute-start(bf16[304,128]{1,0:T(8,128)(2,1)S(1)} %get-tuple-element.96), channel_id=1, source_target_pairs={{0,17},{1,16},{2,19},{3,18},{4,21},{5,20},{6,23},{7,22},{16,1},{17... | collective-permute-start | bytes 233480 | tf_op jit(solution)/shard_map/ppermute | solution.py:340
  37.8 1.9 %collective-permute-start.4 = (bf16[304,128]{1,0:T(8,128)(2,1)S(1)}, bf16[304,128]{1,0:T(8,128)(2,1)S(1)}, u32[]{:S(2)}, u32[]{:S(2)}) collective-permute-start(bf16[304,128]{1,0:T(8,128)(2,1)S(1)} %get-tuple-element.95), channel_id=1, source_target_pairs={{0,1},{1,0},{2,3},{3,2},{4,5},{5,4},{6,7},{7,6},{16,17},{17,16},{1... | collective-permute-start | bytes 233480 | tf_op jit(solution)/shard_map/ppermute | solution.py:340
  39.7 2.3 %collective-permute-done.6 = bf16[304,128]{1,0:T(8,128)(2,1)S(1)} collective-permute-done((bf16[304,128]{1,0:T(8,128)(2,1)S(1)}, bf16[304,128]{1,0:T(8,128)(2,1)S(1)}, u32[]{:S(2)}, u32[]{:S(2)}) %collective-permute-start.6) | collective-permute-done | bytes 77856 | tf_op jit(solution)/shard_map/ppermute | solution.py:340
  42.0 1.1 %collective-permute-done.4 = bf16[304,128]{1,0:T(8,128)(2,1)S(1)} collective-permute-done((bf16[304,128]{1,0:T(8,128)(2,1)S(1)}, bf16[304,128]{1,0:T(8,128)(2,1)S(1)}, u32[]{:S(2)}, u32[]{:S(2)}) %collective-permute-start.4) | collective-permute-done | bytes 77856 | tf_op jit(solution)/shard_map/ppermute | solution.py:340
  43.3 3.0 %collective-permute-start.8 = (bf16[304,128]{1,0:T(8,128)(2,1)S(1)}, bf16[304,128]{1,0:T(8,128)(2,1)S(1)}, u32[]{:S(2)}, u32[]{:S(2)}) collective-permute-start(bf16[304,128]{1,0:T(8,128)(2,1)S(1)} %fusion.1), channel_id=1, source_target_pairs={{0,4},{1,5},{2,6},{3,7},{4,0},{5,1},{6,2},{7,3},{8,12},{9,13},{10,... | collective-permute-start | bytes 233480 | tf_op jit(solution)/shard_map/ppermute | solution.py:340
  46.3 1.3 %collective-permute-start.7 = (bf16[304,128]{1,0:T(8,128)(2,1)S(1)}, bf16[304,128]{1,0:T(8,128)(2,1)S(1)}, u32[]{:S(2)}, u32[]{:S(2)}) collective-permute-start(bf16[304,128]{1,0:T(8,128)(2,1)S(1)} %fusion.1), channel_id=1, source_target_pairs={{0,2},{1,3},{2,0},{3,1},{4,6},{5,7},{6,4},{7,5},{8,10},{9,11},{10,... | collective-permute-start | bytes 233480 | tf_op jit(solution)/shard_map/ppermute | solution.py:340
  47.7 0.7 %collective-permute-start.13 = (bf16[3,192,256]{2,1,0:T(8,128)(2,1)S(1)}, bf16[3,192,256]{2,1,0:T(8,128)(2,1)S(1)}, u32[]{:S(2)}, u32[]{:S(2)}) collective-permute-start(bf16[3,192,256]{2,1,0:T(8,128)(2,1)S(1)} %get-tuple-element.67.refs_2_.gz_second_ref), channel_id=1, source_target_pairs={{1,2},{3,4},{5,6},{2,1},{4,3},{6,5},{9,10},{11,12},{13,14},{10,9},... | collective-permute-start | bytes 884744 | tf_op jit(solution)/shard_map/ppermute | solution.py:381
  48.3 4.5 %shard_map.153 = (bf16[8,192,256]{2,1,0:T(8,128)(2,1)}, bf16[8,192,256]{2,1,0:T(8,128)(2,1)}) custom-call(s32[3]{0:T(128)S(1)} %add_convert_fusion.2.refs_0_.place_ref, bf16[3,192,256]{2,1,0:T(8,128)(2,1)S(1)} %get-tuple-element.61.out_first_ref, bf16[2,192,256]{2,1,0:T(8,128)(2,1)S(1)} %get-tuple-element.62.out_inner_ref, ...), custom_call_target="tpu_custom_call" | custom-call | tf_op jit(solution)/shard_map/pallas_call | solution.py:465
  52.8 1.6 %collective-permute-done.8 = bf16[304,128]{1,0:T(8,128)(2,1)S(1)} collective-permute-done((bf16[304,128]{1,0:T(8,128)(2,1)S(1)}, bf16[304,128]{1,0:T(8,128)(2,1)S(1)}, u32[]{:S(2)}, u32[]{:S(2)}) %collective-permute-start.8) | collective-permute-done | bytes 77856 | tf_op jit(solution)/shard_map/ppermute | solution.py:340
  54.4 2.8 %collective-permute-start.12 = (bf16[304,128]{1,0:T(8,128)(2,1)S(1)}, bf16[304,128]{1,0:T(8,128)(2,1)S(1)}, u32[]{:S(2)}, u32[]{:S(2)}) collective-permute-start(bf16[304,128]{1,0:T(8,128)(2,1)S(1)} %add_convert_fusion.1), channel_id=1, source_target_pairs={{0,17},{1,16},{2,19},{3,18},{4,21},{5,20},{6,23},{7,22},{16,1},{17... | collective-permute-start | bytes 233480 | tf_op jit(solution)/shard_map/ppermute | solution.py:340
  58.0 3.0 %shard_map.154 = bf16[8,192,256]{2,1,0:T(8,128)(2,1)} custom-call(s32[3]{0:T(128)S(1)} %add_convert_fusion.2.refs_0_.place_ref, bf16[3,192,256]{2,1,0:T(8,128)(2,1)S(1)} %collective-permute-done.13.halo_ref, bf16[3,192,256]{2,1,0:T(8,128)(2,1)S(1)} %get-tuple-element.65.gz_first_ref, ...), custom_call_target="tpu_custom_call", output_to_operand_aliasing={{}: (7, {})} | custom-call | tf_op jit(solution)/shard_map/pallas_call | solution.py:480
  62.3 1.6 %collective-permute-done.14.other_ref = bf16[4,304,128]{2,1,0:T(8,128)(2,1)S(1)} collective-permute-done((bf16[4,304,128]{2,1,0:T(8,128)(2,1)S(1)}, bf16[4,304,128]{2,1,0:T(8,128)(2,1)S(1)}, u32[]{:S(2)}, u32[]{:S(2)}) %collective-permute-start.14) | collective-permute-done | bytes 311328 | tf_op jit(solution)/shard_map/ppermute | solution.py:340
  63.9 1.7 %shard_map.155 = (f32[192,768]{1,0:T(8,128)}, f32[192,768]{1,0:T(8,128)}, f32[7,7,192]{2,1,0:T(8,128)}) custom-call(s32[3]{0:T(128)S(1)} %add_convert_fusion.2.refs_0_.place_ref, bf16[4,304,128]{2,1,0:T(8,128)(2,1)S(1)} %pad_maximum_fusion.mine_ref, bf16[4,304,128]{2,1,0:T(8,128)(2,1)S(1)} %collective-permute-done.14.other_ref), custom_call_target="tpu_custom_call" | custom-call | tf_op jit(solution)/shard_map/pallas_call | solution.py:495
  (46 shorter events, 4.3 us)
Async XLA Ops:
  0.6 5.5 %copy-start.5 = (f32[7,7,192]{2,1,0:T(8,128)S(1)}, f32[7,7,192]{2,1,0:T(8,128)}, u32[]{:S(2)}) copy-start(f32[7,7,192]{2,1,0:T(8,128)} %kernel_ref.1) | copy-start | bytes 112900
  0.6 5.5 %copy-start.6 = (f32[768]{0:T(1024)S(1)}, f32[768]{0:T(1024)}, u32[]{:S(2)}) copy-start(f32[768]{0:T(1024)} %param.17) | copy-start | bytes 9220
  0.7 5.5 %copy-start.7 = (f32[192]{0:T(256)S(1)}, f32[192]{0:T(256)}, u32[]{:S(2)}) copy-start(f32[192]{0:T(256)} %param.13) | copy-start | bytes 2308
  0.7 5.5 %copy-start.8 = (f32[192]{0:T(256)S(1)}, f32[192]{0:T(256)}, u32[]{:S(2)}) copy-start(f32[192]{0:T(256)} %param.14) | copy-start | bytes 2308
  0.7 5.5 %copy-start.9 = (f32[192]{0:T(256)S(1)}, f32[192]{0:T(256)}, u32[]{:S(2)}) copy-start(f32[192]{0:T(256)} %param.15) | copy-start | bytes 2308
  0.7 5.5 %copy-start.10 = (f32[192]{0:T(256)S(1)}, f32[192]{0:T(256)}, u32[]{:S(2)}) copy-start(f32[192]{0:T(256)} %param.19) | copy-start | bytes 2308
  1.9 4.3 %copy-start.11 = (f32[192]{0:T(256)S(1)}, f32[192]{0:T(256)}, u32[]{:S(2)}) copy-start(f32[192]{0:T(256)} %param.20) | copy-start | bytes 2308
  1.9 7.2 %copy-start = (bf16[1,1,8,256,192]{3,4,2,1,0:T(8,128)(2,1)S(1)}, bf16[1,1,8,256,192]{3,4,2,1,0:T(8,128)(2,1)}, u32[]{:S(2)}) copy-start(bf16[1,1,8,256,192]{3,4,2,1,0:T(8,128)(2,1)} %param.21) | copy-start | bytes 2359300
  1.9 7.2 %copy-start.2 = (bf16[1,1,8,256,192]{3,4,2,1,0:T(8,128)(2,1)S(1)}, bf16[1,1,8,256,192]{3,4,2,1,0:T(8,128)(2,1)}, u32[]{:S(2)}) copy-start(bf16[1,1,8,256,192]{3,4,2,1,0:T(8,128)(2,1)} %param.11) | copy-start | bytes 2359300
  2.5 15.7 %collective-permute-start = (bf16[3,192,256]{2,1,0:T(8,128)(2,1)S(1)}, bf16[3,192,256]{2,1,0:T(8,128)(2,1)S(1)}, u32[]{:S(2)}, u32[]{:S(2)}) collective-permute-start(bf16[3,192,256]{2,1,0:T(8,128)(2,1)S(1)} %shard_map.146), channel_id=1, source_target_pairs={{0,1},{1,0},{2,3},{3,2},{4,5},{5,4},{6,7},{7,6},{8,9},{9,8},{10,11... | collective-permute-start | bytes 884744 | tf_op jit(solution)/shard_map/ppermute | solution.py:340
  8.5 18.7 %collective-permute-start.1 = (bf16[3,192,256]{2,1,0:T(8,128)(2,1)S(1)}, bf16[3,192,256]{2,1,0:T(8,128)(2,1)S(1)}, u32[]{:S(2)}, u32[]{:S(2)}) collective-permute-start(bf16[3,192,256]{2,1,0:T(8,128)(2,1)S(1)} %shard_map.147), channel_id=1, source_target_pairs={{1,2},{3,4},{5,6},{2,1},{4,3},{6,5},{9,10},{11,12},{13,14},{10,9},... | collective-permute-start | bytes 884744 | tf_op jit(solution)/shard_map/ppermute | solution.py:381
  24.7 9.6 %collective-permute-start.2 = (bf16[3,192,256]{2,1,0:T(8,128)(2,1)S(1)}, bf16[3,192,256]{2,1,0:T(8,128)(2,1)S(1)}, u32[]{:S(2)}, u32[]{:S(2)}) collective-permute-start(bf16[3,192,256]{2,1,0:T(8,128)(2,1)S(1)} %get-tuple-element.65.gz_first_ref), channel_id=1, source_target_pairs={{0,1},{1,0},{2,3},{3,2},{4,5},{5,4},{6,7},{7,6},{8,9},{9,8},{10,11... | collective-permute-start | bytes 884744 | tf_op jit(solution)/shard_map/ppermute | solution.py:340
  34.3 1.7 %collective-permute-start.3 = (bf16[1216,128]{1,0:T(8,128)(2,1)S(1)}, bf16[1216,128]{1,0:T(8,128)(2,1)S(1)}, u32[]{:S(2)}, u32[]{:S(2)}) collective-permute-start(bf16[1216,128]{1,0:T(8,128)(2,1)S(1)} %get-tuple-element.82), channel_id=1, source_target_pairs={{0,8},{8,0},{1,9},{9,1},{2,10},{10,2},{3,11},{11,3},{4,12},{12,4},... | collective-permute-start | bytes 933896 | tf_op jit(solution)/shard_map/ppermute | solution.py:340
  36.1 5.9 %collective-permute-start.6 = (bf16[304,128]{1,0:T(8,128)(2,1)S(1)}, bf16[304,128]{1,0:T(8,128)(2,1)S(1)}, u32[]{:S(2)}, u32[]{:S(2)}) collective-permute-start(bf16[304,128]{1,0:T(8,128)(2,1)S(1)} %get-tuple-element.96), channel_id=1, source_target_pairs={{0,17},{1,16},{2,19},{3,18},{4,21},{5,20},{6,23},{7,22},{16,1},{17... | collective-permute-start | bytes 233480 | tf_op jit(solution)/shard_map/ppermute | solution.py:340
  37.2 4.9 %collective-permute-start.5 = (bf16[304,128]{1,0:T(8,128)(2,1)S(1)}, bf16[304,128]{1,0:T(8,128)(2,1)S(1)}, u32[]{:S(2)}, u32[]{:S(2)}) collective-permute-start(bf16[304,128]{1,0:T(8,128)(2,1)S(1)} %get-tuple-element.97), channel_id=1, source_target_pairs={{0,16},{1,17},{2,18},{3,19},{4,20},{5,21},{6,22},{7,23},{16,0},{17... | collective-permute-start | bytes 233480 | tf_op jit(solution)/shard_map/ppermute | solution.py:340
  37.8 5.4 %collective-permute-start.4 = (bf16[304,128]{1,0:T(8,128)(2,1)S(1)}, bf16[304,128]{1,0:T(8,128)(2,1)S(1)}, u32[]{:S(2)}, u32[]{:S(2)}) collective-permute-start(bf16[304,128]{1,0:T(8,128)(2,1)S(1)} %get-tuple-element.95), channel_id=1, source_target_pairs={{0,1},{1,0},{2,3},{3,2},{4,5},{5,4},{6,7},{7,6},{16,17},{17,16},{1... | collective-permute-start | bytes 233480 | tf_op jit(solution)/shard_map/ppermute | solution.py:340
  43.2 9.6 %collective-permute-start.9 = (bf16[304,128]{1,0:T(8,128)(2,1)S(1)}, bf16[304,128]{1,0:T(8,128)(2,1)S(1)}, u32[]{:S(2)}, u32[]{:S(2)}) collective-permute-start(bf16[304,128]{1,0:T(8,128)(2,1)S(1)} %fusion.1), channel_id=1, source_target_pairs={{0,6},{1,7},{2,4},{3,5},{4,2},{5,3},{6,0},{7,1},{8,14},{9,15},{10,... | collective-permute-start | bytes 233480 | tf_op jit(solution)/shard_map/ppermute | solution.py:340
  43.3 11.1 %collective-permute-start.8 = (bf16[304,128]{1,0:T(8,128)(2,1)S(1)}, bf16[304,128]{1,0:T(8,128)(2,1)S(1)}, u32[]{:S(2)}, u32[]{:S(2)}) collective-permute-start(bf16[304,128]{1,0:T(8,128)(2,1)S(1)} %fusion.1), channel_id=1, source_target_pairs={{0,4},{1,5},{2,6},{3,7},{4,0},{5,1},{6,2},{7,3},{8,12},{9,13},{10,... | collective-permute-start | bytes 233480 | tf_op jit(solution)/shard_map/ppermute | solution.py:340
  46.3 8.0 %collective-permute-start.7 = (bf16[304,128]{1,0:T(8,128)(2,1)S(1)}, bf16[304,128]{1,0:T(8,128)(2,1)S(1)}, u32[]{:S(2)}, u32[]{:S(2)}) collective-permute-start(bf16[304,128]{1,0:T(8,128)(2,1)S(1)} %fusion.1), channel_id=1, source_target_pairs={{0,2},{1,3},{2,0},{3,1},{4,6},{5,7},{6,4},{7,5},{8,10},{9,11},{10,... | collective-permute-start | bytes 233480 | tf_op jit(solution)/shard_map/ppermute | solution.py:340
  47.7 10.3 %collective-permute-start.13 = (bf16[3,192,256]{2,1,0:T(8,128)(2,1)S(1)}, bf16[3,192,256]{2,1,0:T(8,128)(2,1)S(1)}, u32[]{:S(2)}, u32[]{:S(2)}) collective-permute-start(bf16[3,192,256]{2,1,0:T(8,128)(2,1)S(1)} %get-tuple-element.67.refs_2_.gz_second_ref), channel_id=1, source_target_pairs={{1,2},{3,4},{5,6},{2,1},{4,3},{6,5},{9,10},{11,12},{13,14},{10,9},... | collective-permute-start | bytes 884744 | tf_op jit(solution)/shard_map/ppermute | solution.py:381
  54.4 6.5 %collective-permute-start.12 = (bf16[304,128]{1,0:T(8,128)(2,1)S(1)}, bf16[304,128]{1,0:T(8,128)(2,1)S(1)}, u32[]{:S(2)}, u32[]{:S(2)}) collective-permute-start(bf16[304,128]{1,0:T(8,128)(2,1)S(1)} %add_convert_fusion.1), channel_id=1, source_target_pairs={{0,17},{1,16},{2,19},{3,18},{4,21},{5,20},{6,23},{7,22},{16,1},{17... | collective-permute-start | bytes 233480 | tf_op jit(solution)/shard_map/ppermute | solution.py:340
  57.2 4.4 %collective-permute-start.11 = (bf16[304,128]{1,0:T(8,128)(2,1)S(1)}, bf16[304,128]{1,0:T(8,128)(2,1)S(1)}, u32[]{:S(2)}, u32[]{:S(2)}) collective-permute-start(bf16[304,128]{1,0:T(8,128)(2,1)S(1)} %add_convert_fusion.1), channel_id=1, source_target_pairs={{0,16},{1,17},{2,18},{3,19},{4,20},{5,21},{6,22},{7,23},{16,0},{17... | collective-permute-start | bytes 233480 | tf_op jit(solution)/shard_map/ppermute | solution.py:340
  57.8 4.4 %collective-permute-start.10 = (bf16[304,128]{1,0:T(8,128)(2,1)S(1)}, bf16[304,128]{1,0:T(8,128)(2,1)S(1)}, u32[]{:S(2)}, u32[]{:S(2)}) collective-permute-start(bf16[304,128]{1,0:T(8,128)(2,1)S(1)} %add_convert_fusion.1), channel_id=1, source_target_pairs={{0,1},{1,0},{2,3},{3,2},{4,5},{5,4},{6,7},{7,6},{16,17},{17,16},{1... | collective-permute-start | bytes 233480 | tf_op jit(solution)/shard_map/ppermute | solution.py:340
  62.2 1.7 %collective-permute-start.14 = (bf16[4,304,128]{2,1,0:T(8,128)(2,1)S(1)}, bf16[4,304,128]{2,1,0:T(8,128)(2,1)S(1)}, u32[]{:S(2)}, u32[]{:S(2)}) collective-permute-start(bf16[4,304,128]{2,1,0:T(8,128)(2,1)S(1)} %pad_maximum_fusion.mine_ref), channel_id=1, source_target_pairs={{0,8},{8,0},{1,9},{9,1},{2,10},{10,2},{3,11},{11,3},{4,12},{12,4},... | collective-permute-start | bytes 933896 | tf_op jit(solution)/shard_map/ppermute | solution.py:340
  (3 other events, 9.7 us)

commit v4 on v3

--- a/solution.py
+++ b/solution.py
@@ -38,6 +38,10 @@
             total = part if total is None else total + part
         pieces.append(total)
     return jnp.concatenate(pieces, axis=0)
+
+
+def is_low():
+    return 1 - lax.axis_index("space") % 2
 
 
 def spread_taps(kernel_ref, taps_ref, flipped):
@@ -102,7 +106,7 @@
         one_row(row, tall_ref, g_ref, taps_ref, weights, out_ref, gz_ref, kept)
         return carry
 
-    lax.fori_loop(0, out_ref.shape[0], step, 0)
+    lax.fori_loop(0, out_ref.shape[0], step, 0, unroll=True)
 
 
 NT = (((1,), (1,)), ((), ()))
@@ -190,13 +194,13 @@
 
 
 def first_kernel(
-    place_ref, x_ref, halo_ref, g_ref, taps_ref, vec_ref, bin_ref, win_ref, wint_ref, wout_ref, woutt_ref,
+    x_ref, halo_ref, g_ref, taps_ref, vec_ref, bin_ref, win_ref, wint_ref, wout_ref, woutt_ref,
     dwin_in_ref, dwout_in_ref, dtaps_in_ref,
     out_ref, gz_ref, dwin_ref, dwout_ref, dtaps_ref,
     tall_ref, *kept,
 ):
     hidden_units = win_ref.shape[1]
-    low = place_ref[2]
+    low = is_low()
     with_halo(x_ref, halo_ref, tall_ref, low)
     weights = (vec_ref, bin_ref, win_ref, wint_ref, wout_ref, woutt_ref)
     rows = g_ref.at[pl.ds((x_ref.shape[0] - REACH) * low, REACH)]
@@ -210,10 +214,10 @@
 
 
 def second_kernel(
-    place_ref, x_ref, halo_ref, g_ref, taps_ref, vec_ref, bin_ref, win_ref, wint_ref, wout_ref, woutt_ref,
+    x_ref, halo_ref, g_ref, taps_ref, vec_ref, bin_ref, win_ref, wint_ref, wout_ref, woutt_ref,
     out_ref, gz_ref, tall_ref, *kept,
 ):
-    low = 1 - place_ref[2]
+    low = 1 - is_low()
     with_halo(x_ref, halo_ref, tall_ref, low)
     weights = (vec_ref, bin_ref, win_ref, wint_ref, wout_ref, woutt_ref)
     rows = g_ref.at[pl.ds((x_ref.shape[0] - REACH) * low, REACH)]
@@ -221,7 +225,7 @@
 
 
 def terms_kernel(
-    core_ref, tall_ref, gz_ref, normed_ref, act_ref, gout_ref, gh_ref, dwin_ref, dwout_ref, dtaps_ref,
+    tall_ref, gz_ref, normed_ref, act_ref, gout_ref, gh_ref, dwin_ref, dwout_ref, dtaps_ref,
     keep_ref, send_ref, halves_ref, *, scale,
 ):
     chans, hidden_units = dwin_ref.shape
@@ -247,17 +251,17 @@
         both = jnp.concatenate([both, jnp.zeros((16, 128 - span), F32)], axis=1)
         half, place = divmod(pair, groups // 4)
         halves_ref[half, at + place * 16 : at + (place + 1) * 16, :] = both.astype(BF16)
-    core = core_ref[0]
+    core = lax.axis_index("core")
     keep_ref[...] = halves_ref[core]
     send_ref[...] = halves_ref[1 - core]
 
 
 def input_kernel(
-    place_ref, out_first_ref, out_inner_ref, out_second_ref, gz_first_ref, gz_inner_ref, gz_second_ref,
+    out_first_ref, out_inner_ref, out_second_ref, gz_first_ref, gz_inner_ref, gz_second_ref,
     halo_ref, g_ref, taps_ref,
     out_ref, grad_ref, tall_ref,
 ):
-    low = place_ref[2]
+    low = is_low()
     rows = g_ref.shape[0]
     inner = rows - 2 * REACH
     tall_ref[pl.ds(rows * (1 - low), REACH)] = gz_second_ref[...]
@@ -277,10 +281,10 @@
 
 
 def input_rest_kernel(
-    place_ref, halo_ref, gz_first_ref, gz_inner_ref, gz_second_ref, g_ref, taps_ref, rest_ref,
+    halo_ref, gz_first_ref, gz_inner_ref, gz_second_ref, g_ref, taps_ref, rest_ref,
     grad_ref, tall_ref, part_ref, sem,
 ):
-    low = 1 - place_ref[2]
+    low = 1 - is_low()
     rows = g_ref.shape[0]
     inner = rows - 2 * REACH
     near = REACH - inner
@@ -300,8 +304,9 @@
     copy.wait()
 
 
-def final_kernel(place_ref, mine_ref, other_ref, win_ref, woutt_ref, taps_ref, all_ref):
-    core, quarter = place_ref[0], place_ref[1]
+def final_kernel(mine_ref, other_ref, win_ref, woutt_ref, taps_ref, all_ref):
+    core = lax.axis_index("core")
+    quarter = 2 * lax.axis_index("x") + lax.axis_index("space") % 2
     chans, hidden_units = win_ref.shape
     size = mine_ref.shape[1]
     for turn in range(4):
@@ -324,15 +329,14 @@
                 taps_ref[tap, :, group * GROUP : (group + 1) * GROUP] = piece[:TAPS, tap * GROUP : (tap + 1) * GROUP]
 
 
-def edge_kernel(place_ref, x_ref, edge_ref, *, first):
-    low = place_ref[2] if first else 1 - place_ref[2]
+def edge_kernel(x_ref, edge_ref, *, first):
+    low = is_low() if first else 1 - is_low()
     edge_ref[...] = x_ref[pl.ds((x_ref.shape[0] - REACH) * low, REACH)]
 
 
 PARAMS = pltpu.CompilerParams(vmem_limit_bytes=20 * 1024 * 1024)
 SMALL = pltpu.CompilerParams(vmem_limit_bytes=8 * 1024 * 1024)
 IN_VMEM = pl.BlockSpec(memory_space=pltpu.VMEM)
-IN_SMEM = pl.BlockSpec(memory_space=pltpu.SMEM)
 
 
 def swap(value, axis, mask):
@@ -350,12 +354,9 @@
 def on_device(
     features, dw_kernel, dw_bias, ln_gain, ln_bias, w_in, b_in, w_out, b_out, layer_scale, cotangent
 ):
-    core = lax.axis_index("core").astype(jnp.uint32)
     quarter = (2 * lax.axis_index("x") + lax.axis_index("space") % 2).astype(jnp.uint32)
     turns = [quarter ^ turn for turn in range(4)]
-    even = (1 - lax.axis_index("space") % 2).astype(jnp.uint32)
-    place = jnp.stack([core, quarter, even]).astype(jnp.int32)
-    features, place, *turns = lax.optimization_barrier((features, place, *turns))
+    features, *turns = lax.optimization_barrier((features, *turns))
     x = jnp.swapaxes(features[0, 0], 1, 2)
     g = jnp.swapaxes(cotangent[0, 0], 1, 2)
     rows, chans, width = x.shape
@@ -368,10 +369,10 @@
         return pl.pallas_call(
             lambda *refs: edge_kernel(*refs, first=first),
             out_shape=narrow,
-            in_specs=[IN_SMEM, IN_VMEM],
+            in_specs=[IN_VMEM],
             out_specs=IN_VMEM,
             compiler_params=SMALL,
-        )(place, x)
+        )(x)
 
     def first_swap(value):
         return swap(value, "space", 1)
@@ -413,8 +414,6 @@
         compiler_params=SMALL,
     )(dw_kernel, w_in, w_out.T, b_in.reshape(-1, 128), *[vector[None] for vector in vectors])
     weights = (vectors, bias, w_in, w_in_t, w_out_turned, w_out.T)
-    second_edge, taps = lax.optimization_barrier((edge(False), taps))
-    second_halo = second_swap(second_edge)
     out_inner, gz_inner, *inner_terms = pl.pallas_call(
         inner_kernel,
         out_shape=(middle, middle, *terms),
@@ -423,34 +422,36 @@
         scratch_shapes=scratch(kept(inner)),
         compiler_params=PARAMS,
     )(x, g, taps, *weights)
+    second_edge, out_inner = lax.optimization_barrier((edge(False), out_inner))
+    second_halo = second_swap(second_edge)
     half_rows = hidden_units // 128 * chans + groups // 2 * 8
     half_rows = (half_rows + 63) // 64 * 64
     half = jax.ShapeDtypeStruct((half_rows, 128), BF16)
     out_first, gz_first, *first_terms = pl.pallas_call(
         first_kernel,
         out_shape=(narrow, narrow, *terms),
-        in_specs=[IN_SMEM] + [IN_VMEM] * 13,
+        in_specs=[IN_VMEM] * 13,
         out_specs=(IN_VMEM,) * 5,
         scratch_shapes=scratch((tall, *kept(REACH))),
         compiler_params=PARAMS,
-    )(place, x, first_halo, g, taps, *weights, *inner_terms)
+    )(x, first_halo, g, taps, *weights, *inner_terms)
     gz_first_halo = first_swap(gz_first)
     out_second, gz_second, *second_kept = pl.pallas_call(
         second_kernel,
         out_shape=(narrow, narrow, tall, *kept(REACH)),
-        in_specs=[IN_SMEM] + [IN_VMEM] * 10,
+        in_specs=[IN_VMEM] * 10,
         out_specs=(IN_VMEM,) * 7,
         compiler_params=PARAMS,
-    )(place, x, second_halo, g, taps, *weights)
+    )(x, second_halo, g, taps, *weights)
     gz_second_halo = second_swap(gz_second)
     keep, send = pl.pallas_call(
         lambda *refs: terms_kernel(*refs, scale=scale),
         out_shape=(half, half),
-        in_specs=[IN_SMEM] + [IN_VMEM] * 9,
+        in_specs=[IN_VMEM] * 9,
         out_specs=(IN_VMEM,) * 2,
         scratch_shapes=[pltpu.VMEM((2, half_rows, 128), BF16)],
         compiler_params=PARAMS,
-    )(place, second_kept[0], gz_second, *second_kept[1:], *first_terms)
+    )(second_kept[0], gz_second, *second_kept[1:], *first_terms)
     keep, send, gz_first_halo = lax.optimization_barrier((keep, send, gz_first_halo))
 
     summed = added(keep, swap(send, "core", 1)).reshape(4, half_rows // 4, 128)
@@ -465,11 +466,11 @@
     out, grad_rest = pl.pallas_call(
         input_kernel,
         out_shape=(image, image),
-        in_specs=[IN_SMEM] + [IN_VMEM] * 9,
+        in_specs=[IN_VMEM] * 9,
         out_specs=(IN_VMEM, IN_VMEM),
         scratch_shapes=[pltpu.VMEM((rows + REACH, chans, width), BF16)],
         compiler_params=PARAMS,
-    )(place, out_first, out_inner, out_second, gz_first, gz_inner, gz_second, gz_first_halo, g, back_taps)
+    )(out_first, out_inner, out_second, gz_first, gz_inner, gz_second, gz_first_halo, g, back_taps)
     bit = 2
     while bit < strips:
         masks = (bit, 2 * bit, 3 * bit) if 2 * bit < strips else (bit,)
@@ -480,26 +481,26 @@
     grad_input = pl.pallas_call(
         input_rest_kernel,
         out_shape=image,
-        in_specs=[IN_SMEM] + [IN_VMEM] * 6 + [pl.BlockSpec(memory_space=pl.ANY)],
+        in_specs=[IN_VMEM] * 6 + [pl.BlockSpec(memory_space=pl.ANY)],
         out_specs=pl.BlockSpec(memory_space=pl.ANY),
         scratch_shapes=[
             pltpu.VMEM((3 * REACH, chans, width), BF16),
             pltpu.VMEM((REACH, chans, width), BF16),
             pltpu.SemaphoreType.DMA(()),
         ],
-        input_output_aliases={7: 0},
-        compiler_params=PARAMS,
-    )(place, gz_second_halo, gz_first, gz_inner, gz_second, g, back_taps, grad_rest)
+        input_output_aliases={6: 0},
+        compiler_params=PARAMS,
+    )(gz_second_halo, gz_first, gz_inner, gz_second, g, back_taps, grad_rest)
     mine, grad_input = lax.optimization_barrier((mine, grad_input))
     other = swap(mine, "core", 1)
     grad_w_in, grad_w_out_t, grad_kernel = pl.pallas_call(
         final_kernel,
         out_shape=(matrix, matrix, jax.ShapeDtypeStruct((TAPS, TAPS, chans), F32)),
-        in_specs=[IN_SMEM, IN_VMEM, IN_VMEM],
+        in_specs=[IN_VMEM, IN_VMEM],
         out_specs=(IN_VMEM,) * 3,
         scratch_shapes=[pltpu.VMEM((2, half_rows, 128), BF16)],
         compiler_params=PARAMS,
-    )(place, mine, other)
+    )(mine, other)
     block_output = jnp.swapaxes(out, 1, 2)[None, None]
     grad_image = jnp.swapaxes(grad_input, 1, 2)[None, None]
     return (block_output, grad_image, grad_w_in, grad_w_out_t.T, grad_kernel)

time: 65.8 us -> 60.4 us (0.918)
  Pallas kernels: 30.1 us -> 24.2 us
  waiting for transfers between devices: 14.4 us -> 11.9 us
  starting transfers between devices: 18.6 us -> 20.6 us
  local copies, waits for them, and re-layouts: 1.21 us -> 2.03 us
    ppermute x13, waiting for transfers between devices: 14.4 us -> 11.9 us  [swap(): lax.ppermute(value, axis, [(source, source ^ mask) for source in range(co...]
    ppermute x13, starting transfers between devices: 17.2 us -> 19.1 us  [swap(): lax.ppermute(value, axis, [(source, source ^ mask) for source in range(co...]
    pallas_call x1, Pallas kernels: 6.51 us -> 5.27 us  [on_device(): pl.pallas_call(first_kernel, out_shape=(narrow, narrow, *terms), in_specs...]
    pallas_call x2, Pallas kernels: 1.13 us -> 0.05 us  [edge(): pl.pallas_call(lambda *refs: edge_kernel(*refs, first=first), out_shape=n...]
    pallas_call x2, Pallas kernels: 7.42 us -> 6.36 us  [the longest x1 3.93 us: on_device(): pl.pallas_call(input_kernel, out_shape=(image, image), in_specs=[IN_VMEM]...]
    pallas_call x1, Pallas kernels: 4.99 us -> 4.03 us  [on_device(): pl.pallas_call(second_kernel, out_shape=(narrow, narrow, tall, *kept(REAC...]
    unnamed x24, local copies, waits for them, and re-layouts: 1.18 us -> 2 us
  transfers between devices with their start and end apart: 15 -> 15, of which waited for: 8 -> 9; matrix products, arithmetic and copies ran while one was open for 0% -> 0% of each run, Pallas kernels for 43% -> 39%
where the time goes in v4:
time: 60.4 us; the launch traced here: 59.9 us
  Pallas kernels  24.2 us (40%)
  starting transfers between devices  20.6 us (34%)
  waiting for transfers between devices  11.9 us (20%)
  local copies, waits for them, and re-layouts  2.03 us (3%)
  between operations  0.92 us (2%)
    ppermute x13, starting transfers between devices, swap(): lax.ppermute(value, axis, [(source, source ^ mask) for source in range(co...  19.1 us
    ppermute x13, waiting for transfers between devices, swap(): lax.ppermute(value, axis, [(source, source ^ mask) for source in range(co...  11.9 us
    pallas_call x1, Pallas kernels, on_device(): pl.pallas_call(first_kernel, out_shape=(narrow, narrow, *terms), in_specs...  5.27 us
    pallas_call x1, Pallas kernels, on_device(): pl.pallas_call(second_kernel, out_shape=(narrow, narrow, tall, *kept(REAC...  4.03 us
    pallas_call x1, Pallas kernels, on_device(): pl.pallas_call(input_kernel, out_shape=(image, image), in_specs=[IN_VMEM]...  3.93 us
    pallas_call x1, Pallas kernels, on_device(): pl.pallas_call(inner_kernel, out_shape=(middle, middle, *terms), in_specs...  3.52 us
    pallas_call x1, Pallas kernels, on_device(): pl.pallas_call(input_rest_kernel, out_shape=image, in_specs=[IN_VMEM] * 6...  2.44 us
    pallas_call x1, Pallas kernels, on_device(): pl.pallas_call(prepare_kernel, out_shape=(spread, spread, across_lanes, h...  2.24 us
  transfers between devices with their start and end apart: 15, of which 9 were waited for; matrix products, arithmetic and copies ran while one was open for 0% of the time, Pallas kernels for 39%

profile of v4, /device:TPU:0, one launch (start us, length us, event | category | flops | bytes accessed | tf_op | source)
XLA Modules:
  0.0 59.9 jit_solution(4230870948763924535)
XLA Ops:
  0.7 1.1 %copy-done = bf16[1,1,8,256,192]{3,4,2,1,0:T(8,128)(2,1)S(1)} copy-done((bf16[1,1,8,256,192]{3,4,2,1,0:T(8,128)(2,1)S(1)}, bf16[1,1,8,256,192]{3,4,2,1,0:T(8,128)(2,1)}, u32[]{:S(2)}) %copy-start) | copy-done | bytes 786456
  1.9 3.0 %collective-permute-start = (bf16[3,192,256]{2,1,0:T(8,128)(2,1)S(1)}, bf16[3,192,256]{2,1,0:T(8,128)(2,1)S(1)}, u32[]{:S(2)}, u32[]{:S(2)}) collective-permute-start(bf16[3,192,256]{2,1,0:T(8,128)(2,1)S(1)} %shard_map.146), channel_id=1, source_target_pairs={{0,1},{1,0},{2,3},{3,2},{4,5},{5,4},{6,7},{7,6},{8,9},{9,8},{10,11... | collective-permute-start | bytes 884744 | tf_op jit(solution)/shard_map/ppermute | solution.py:344
  5.1 0.8 %copy-done.5 = f32[7,7,192]{2,1,0:T(8,128)S(1)} copy-done((f32[7,7,192]{2,1,0:T(8,128)S(1)}, f32[7,7,192]{2,1,0:T(8,128)}, u32[]{:S(2)}) %copy-start.5) | copy-done | bytes 37656
  5.9 2.2 %shard_map.147 = (bf16[12,112,224]{2,1,0:T(8,128)(2,1)S(1)}, bf16[12,112,224]{2,1,0:T(8,128)(2,1)S(1)}, f32[5,192,128]{2,1,0:T(8,128)S(1)}, f32[768,128]{1,0:T(8...) custom-call(f32[7,7,192]{2,1,0:T(8,128)S(1)} %copy-done.5, bf16[192,768]{1,0:T(8,128)(2,1)S(1)} %copy-done.3, ...), custom_call_target="tpu_custom_call" | custom-call | tf_op jit(solution)/shard_map/pallas_call | solution.py:409
  8.1 3.5 %shard_map.148 = (bf16[2,192,256]{2,1,0:T(8,128)(2,1)S(1)}, bf16[2,192,256]{2,1,0:T(8,128)(2,1)S(1)}, f32[192,768]{1,0:T(8,128)S(1)}, f32[192,768]{1,0:T(8,128)S(1)}, f32[12,8,112]{2,1,0:T(8,128)S(1)}) custom-call(bf16[8,192,256]{2,1,0:T(8,128)(2,1)S(1)} %bitcast.36, bf16[8,192,256]{2,1,0:T(8,128)(2,1)S(1)} %bitcast.39, ...), custom_call_target="tpu_custom_call" | custom-call | tf_op jit(solution)/shard_map/pallas_call | solution.py:417
  11.7 0.9 %collective-permute-start.1 = (bf16[3,192,256]{2,1,0:T(8,128)(2,1)S(1)}, bf16[3,192,256]{2,1,0:T(8,128)(2,1)S(1)}, u32[]{:S(2)}, u32[]{:S(2)}) collective-permute-start(bf16[3,192,256]{2,1,0:T(8,128)(2,1)S(1)} %shard_map.150), channel_id=1, source_target_pairs={{1,2},{3,4},{5,6},{2,1},{4,3},{6,5},{9,10},{11,12},{13,14},{10,9},... | collective-permute-start | bytes 884744 | tf_op jit(solution)/shard_map/ppermute | solution.py:382
  12.5 5.3 %shard_map.149 = (bf16[3,192,256]{2,1,0:T(8,128)(2,1)S(1)}, bf16[3,192,256]{2,1,0:T(8,128)(2,1)S(1)}, f32[192,768]{1,0:T(8,128)S(1)}, f32[192,768]{1,0:T(8,128)S(1)}, f32[12,8,112]{2,1,0:T(8,128)S(1)}) custom-call(bf16[8,192,256]{2,1,0:T(8,128)(2,1)S(1)} %bitcast.37, bf16[3,192,256]{2,1,0:T(8,128)(2,1)S(1)} %collective-permute-done.halo_ref, ...), custom_call_target="tpu_custom_call" | custom-call | tf_op jit(solution)/shard_map/pallas_call | solution.py:430
  17.8 4.3 %collective-permute-start.2 = (bf16[3,192,256]{2,1,0:T(8,128)(2,1)S(1)}, bf16[3,192,256]{2,1,0:T(8,128)(2,1)S(1)}, u32[]{:S(2)}, u32[]{:S(2)}) collective-permute-start(bf16[3,192,256]{2,1,0:T(8,128)(2,1)S(1)} %get-tuple-element.63.gz_first_ref), channel_id=1, source_target_pairs={{0,1},{1,0},{2,3},{3,2},{4,5},{5,4},{6,7},{7,6},{8,9},{9,8},{10,11... | collective-permute-start | bytes 884744 | tf_op jit(solution)/shard_map/ppermute | solution.py:344
  22.2 4.0 %shard_map.151 = (bf16[3,192,256]{2,1,0:T(8,128)(2,1)S(1)}, bf16[3,192,256]{2,1,0:T(8,128)(2,1)S(1)}, bf16[9,192,256]{2,1,0:T(8,128)(2,1)S(1)}, bf16[3,192,256]{...) custom-call(bf16[8,192,256]{2,1,0:T(8,128)(2,1)S(1)} %bitcast.38, ...), custom_call_target="tpu_custom_call" | custom-call | tf_op jit(solution)/shard_map/pallas_call | solution.py:439
  26.2 1.6 %shard_map.152 = (bf16[1216,128]{1,0:T(8,128)(2,1)S(1)}, bf16[1216,128]{1,0:T(8,128)(2,1)S(1)}) custom-call(bf16[9,192,256]{2,1,0:T(8,128)(2,1)S(1)} %get-tuple-element.66.refs_0_, bf16[3,192,256]{2,1,0:T(8,128)(2,1)S(1)} %get-tuple-element.65.refs_1_.gz_second_ref, bf16[3,192,256]{2,1,0:T(8,128)(2,1)S(1)} %get-tuple-element.67.refs_2_, ...), custom_call_target="tpu_custom_call" | custom-call | tf_op jit(solution)/shard_map/pallas_call | solution.py:447
  27.8 0.8 %collective-permute-done.2.halo_ref = bf16[3,192,256]{2,1,0:T(8,128)(2,1)S(1)} collective-permute-done((bf16[3,192,256]{2,1,0:T(8,128)(2,1)S(1)}, bf16[3,192,256]{2,1,0:T(8,128)(2,1)S(1)}, u32[]{:S(2)}, u32[]{:S(2)}) %collective-permute-start.2) | collective-permute-done | bytes 294944 | tf_op jit(solution)/shard_map/ppermute | solution.py:344
  28.6 1.6 %collective-permute-done.3 = bf16[1216,128]{1,0:T(8,128)(2,1)S(1)} collective-permute-done((bf16[1216,128]{1,0:T(8,128)(2,1)S(1)}, bf16[1216,128]{1,0:T(8,128)(2,1)S(1)}, u32[]{:S(2)}, u32[]{:S(2)}) %collective-permute-start.3) | collective-permute-done | bytes 311328 | tf_op jit(solution)/shard_map/ppermute | solution.py:344
  30.3 2.7 %collective-permute-start.6 = (bf16[304,128]{1,0:T(8,128)(2,1)S(1)}, bf16[304,128]{1,0:T(8,128)(2,1)S(1)}, u32[]{:S(2)}, u32[]{:S(2)}) collective-permute-start(bf16[304,128]{1,0:T(8,128)(2,1)S(1)} %get-tuple-element.94), channel_id=1, source_target_pairs={{0,17},{1,16},{2,19},{3,18},{4,21},{5,20},{6,23},{7,22},{16,1},{17... | collective-permute-start | bytes 233480 | tf_op jit(solution)/shard_map/ppermute | solution.py:344
  33.9 2.4 %collective-permute-done.6 = bf16[304,128]{1,0:T(8,128)(2,1)S(1)} collective-permute-done((bf16[304,128]{1,0:T(8,128)(2,1)S(1)}, bf16[304,128]{1,0:T(8,128)(2,1)S(1)}, u32[]{:S(2)}, u32[]{:S(2)}) %collective-permute-start.6) | collective-permute-done | bytes 77856 | tf_op jit(solution)/shard_map/ppermute | solution.py:344
  36.3 1.3 %collective-permute-done.5 = bf16[304,128]{1,0:T(8,128)(2,1)S(1)} collective-permute-done((bf16[304,128]{1,0:T(8,128)(2,1)S(1)}, bf16[304,128]{1,0:T(8,128)(2,1)S(1)}, u32[]{:S(2)}, u32[]{:S(2)}) %collective-permute-start.5) | collective-permute-done | bytes 77856 | tf_op jit(solution)/shard_map/ppermute | solution.py:344
  38.1 3.7 %collective-permute-start.9 = (bf16[304,128]{1,0:T(8,128)(2,1)S(1)}, bf16[304,128]{1,0:T(8,128)(2,1)S(1)}, u32[]{:S(2)}, u32[]{:S(2)}) collective-permute-start(bf16[304,128]{1,0:T(8,128)(2,1)S(1)} %fusion.1), channel_id=1, source_target_pairs={{0,6},{1,7},{2,4},{3,5},{4,2},{5,3},{6,0},{7,1},{8,14},{9,15},{10,... | collective-permute-start | bytes 233480 | tf_op jit(solution)/shard_map/ppermute | solution.py:344
  41.7 0.8 %collective-permute-start.7 = (bf16[304,128]{1,0:T(8,128)(2,1)S(1)}, bf16[304,128]{1,0:T(8,128)(2,1)S(1)}, u32[]{:S(2)}, u32[]{:S(2)}) collective-permute-start(bf16[304,128]{1,0:T(8,128)(2,1)S(1)} %fusion.1), channel_id=1, source_target_pairs={{0,2},{1,3},{2,0},{3,1},{4,6},{5,7},{6,4},{7,5},{8,10},{9,11},{10,... | collective-permute-start | bytes 233480 | tf_op jit(solution)/shard_map/ppermute | solution.py:344
  43.2 3.9 %shard_map.153 = (bf16[8,192,256]{2,1,0:T(8,128)(2,1)}, bf16[8,192,256]{2,1,0:T(8,128)(2,1)}) custom-call(bf16[3,192,256]{2,1,0:T(8,128)(2,1)S(1)} %get-tuple-element.58.out_first_ref, bf16[2,192,256]{2,1,0:T(8,128)(2,1)S(1)} %get-tuple-element.60.out_inner_ref, bf16[3,192,256]{2,1,0:T(8,128)(2,1)S(1)} %get-tuple-element.62.out_second_ref, ...), custom_call_target="tpu_custom_call" | custom-call | tf_op jit(solution)/shard_map/pallas_call | solution.py:466
  47.1 2.0 %collective-permute-done.8 = bf16[304,128]{1,0:T(8,128)(2,1)S(1)} collective-permute-done((bf16[304,128]{1,0:T(8,128)(2,1)S(1)}, bf16[304,128]{1,0:T(8,128)(2,1)S(1)}, u32[]{:S(2)}, u32[]{:S(2)}) %collective-permute-start.8) | collective-permute-done | bytes 77856 | tf_op jit(solution)/shard_map/ppermute | solution.py:344
  49.1 3.0 %collective-permute-start.12 = (bf16[304,128]{1,0:T(8,128)(2,1)S(1)}, bf16[304,128]{1,0:T(8,128)(2,1)S(1)}, u32[]{:S(2)}, u32[]{:S(2)}) collective-permute-start(bf16[304,128]{1,0:T(8,128)(2,1)S(1)} %add_convert_fusion.1), channel_id=1, source_target_pairs={{0,17},{1,16},{2,19},{3,18},{4,21},{5,20},{6,23},{7,22},{16,1},{17... | collective-permute-start | bytes 233480 | tf_op jit(solution)/shard_map/ppermute | solution.py:344
  52.8 2.4 %shard_map.154 = bf16[8,192,256]{2,1,0:T(8,128)(2,1)} custom-call(bf16[3,192,256]{2,1,0:T(8,128)(2,1)S(1)} %collective-permute-done.13.halo_ref, bf16[3,192,256]{2,1,0:T(8,128)(2,1)S(1)} %get-tuple-element.63.gz_first_ref, bf16[2,192,256]{2,1,0:T(8,128)(2,1)S(1)} %get-tuple-element.64.gz_inner_ref, ...), custom_call_target="tpu_custom_call", output_to_operand_aliasing={{}: (6, {})} | custom-call | tf_op jit(solution)/shard_map/pallas_call | solution.py:481
  55.2 1.3 %collective-permute-done.11 = bf16[304,128]{1,0:T(8,128)(2,1)S(1)} collective-permute-done((bf16[304,128]{1,0:T(8,128)(2,1)S(1)}, bf16[304,128]{1,0:T(8,128)(2,1)S(1)}, u32[]{:S(2)}, u32[]{:S(2)}) %collective-permute-start.11) | collective-permute-done | bytes 77856 | tf_op jit(solution)/shard_map/ppermute | solution.py:344
  57.2 1.6 %collective-permute-done.14.other_ref = bf16[4,304,128]{2,1,0:T(8,128)(2,1)S(1)} collective-permute-done((bf16[4,304,128]{2,1,0:T(8,128)(2,1)S(1)}, bf16[4,304,128]{2,1,0:T(8,128)(2,1)S(1)}, u32[]{:S(2)}, u32[]{:S(2)}) %collective-permute-start.14) | collective-permute-done | bytes 311328 | tf_op jit(solution)/shard_map/ppermute | solution.py:344
  58.8 1.1 %shard_map.155 = (f32[192,768]{1,0:T(8,128)}, f32[192,768]{1,0:T(8,128)}, f32[7,7,192]{2,1,0:T(8,128)}) custom-call(bf16[4,304,128]{2,1,0:T(8,128)(2,1)S(1)} %pad_maximum_fusion.mine_ref, bf16[4,304,128]{2,1,0:T(8,128)(2,1)S(1)} %collective-permute-done.14.other_ref), custom_call_target="tpu_custom_call" | custom-call | tf_op jit(solution)/shard_map/pallas_call | solution.py:496
  (45 shorter events, 3.5 us)
Async XLA Ops:
  0.6 4.3 %copy-start.6 = (f32[768]{0:T(1024)S(1)}, f32[768]{0:T(1024)}, u32[]{:S(2)}) copy-start(f32[768]{0:T(1024)} %param.17) | copy-start | bytes 9220
  0.6 4.3 %copy-start.7 = (f32[192]{0:T(256)S(1)}, f32[192]{0:T(256)}, u32[]{:S(2)}) copy-start(f32[192]{0:T(256)} %param.13) | copy-start | bytes 2308
  0.7 4.3 %copy-start.8 = (f32[192]{0:T(256)S(1)}, f32[192]{0:T(256)}, u32[]{:S(2)}) copy-start(f32[192]{0:T(256)} %param.14) | copy-start | bytes 2308
  0.7 4.3 %copy-start.9 = (f32[192]{0:T(256)S(1)}, f32[192]{0:T(256)}, u32[]{:S(2)}) copy-start(f32[192]{0:T(256)} %param.15) | copy-start | bytes 2308
  0.7 4.3 %copy-start.10 = (f32[192]{0:T(256)S(1)}, f32[192]{0:T(256)}, u32[]{:S(2)}) copy-start(f32[192]{0:T(256)} %param.19) | copy-start | bytes 2308
  0.7 4.3 %copy-start.11 = (f32[192]{0:T(256)S(1)}, f32[192]{0:T(256)}, u32[]{:S(2)}) copy-start(f32[192]{0:T(256)} %param.20) | copy-start | bytes 2308
  1.9 3.2 %copy-start.4 = (bf16[768,192]{0,1:T(8,128)(2,1)S(1)}, bf16[768,192]{0,1:T(8,128)(2,1)}, u32[]{:S(2)}) copy-start(bf16[768,192]{0,1:T(8,128)(2,1)} %param.18) | copy-start | bytes 884740
  1.9 6.3 %copy-start.1 = (bf16[1,1,8,256,192]{3,4,2,1,0:T(8,128)(2,1)S(1)}, bf16[1,1,8,256,192]{3,4,2,1,0:T(8,128)(2,1)}, u32[]{:S(2)}) copy-start(bf16[1,1,8,256,192]{3,4,2,1,0:T(8,128)(2,1)} %param.11) | copy-start | bytes 2359300
  1.9 6.3 %copy-start.2 = (bf16[1,1,8,256,192]{3,4,2,1,0:T(8,128)(2,1)S(1)}, bf16[1,1,8,256,192]{3,4,2,1,0:T(8,128)(2,1)}, u32[]{:S(2)}) copy-start(bf16[1,1,8,256,192]{3,4,2,1,0:T(8,128)(2,1)} %param.21) | copy-start | bytes 2359300
  1.9 10.6 %collective-permute-start = (bf16[3,192,256]{2,1,0:T(8,128)(2,1)S(1)}, bf16[3,192,256]{2,1,0:T(8,128)(2,1)S(1)}, u32[]{:S(2)}, u32[]{:S(2)}) collective-permute-start(bf16[3,192,256]{2,1,0:T(8,128)(2,1)S(1)} %shard_map.146), channel_id=1, source_target_pairs={{0,1},{1,0},{2,3},{3,2},{4,5},{5,4},{6,7},{7,6},{8,9},{9,8},{10,11... | collective-permute-start | bytes 884744 | tf_op jit(solution)/shard_map/ppermute | solution.py:344
  11.7 10.5 %collective-permute-start.1 = (bf16[3,192,256]{2,1,0:T(8,128)(2,1)S(1)}, bf16[3,192,256]{2,1,0:T(8,128)(2,1)S(1)}, u32[]{:S(2)}, u32[]{:S(2)}) collective-permute-start(bf16[3,192,256]{2,1,0:T(8,128)(2,1)S(1)} %shard_map.150), channel_id=1, source_target_pairs={{1,2},{3,4},{5,6},{2,1},{4,3},{6,5},{9,10},{11,12},{13,14},{10,9},... | collective-permute-start | bytes 884744 | tf_op jit(solution)/shard_map/ppermute | solution.py:382
  17.8 10.8 %collective-permute-start.2 = (bf16[3,192,256]{2,1,0:T(8,128)(2,1)S(1)}, bf16[3,192,256]{2,1,0:T(8,128)(2,1)S(1)}, u32[]{:S(2)}, u32[]{:S(2)}) collective-permute-start(bf16[3,192,256]{2,1,0:T(8,128)(2,1)S(1)} %get-tuple-element.63.gz_first_ref), channel_id=1, source_target_pairs={{0,1},{1,0},{2,3},{3,2},{4,5},{5,4},{6,7},{7,6},{8,9},{9,8},{10,11... | collective-permute-start | bytes 884744 | tf_op jit(solution)/shard_map/ppermute | solution.py:344
  28.6 1.6 %collective-permute-start.3 = (bf16[1216,128]{1,0:T(8,128)(2,1)S(1)}, bf16[1216,128]{1,0:T(8,128)(2,1)S(1)}, u32[]{:S(2)}, u32[]{:S(2)}) collective-permute-start(bf16[1216,128]{1,0:T(8,128)(2,1)S(1)} %get-tuple-element.80), channel_id=1, source_target_pairs={{0,8},{8,0},{1,9},{9,1},{2,10},{10,2},{3,11},{11,3},{4,12},{12,4},... | collective-permute-start | bytes 933896 | tf_op jit(solution)/shard_map/ppermute | solution.py:344
  30.3 6.0 %collective-permute-start.6 = (bf16[304,128]{1,0:T(8,128)(2,1)S(1)}, bf16[304,128]{1,0:T(8,128)(2,1)S(1)}, u32[]{:S(2)}, u32[]{:S(2)}) collective-permute-start(bf16[304,128]{1,0:T(8,128)(2,1)S(1)} %get-tuple-element.94), channel_id=1, source_target_pairs={{0,17},{1,16},{2,19},{3,18},{4,21},{5,20},{6,23},{7,22},{16,1},{17... | collective-permute-start | bytes 233480 | tf_op jit(solution)/shard_map/ppermute | solution.py:344
  33.1 4.6 %collective-permute-start.5 = (bf16[304,128]{1,0:T(8,128)(2,1)S(1)}, bf16[304,128]{1,0:T(8,128)(2,1)S(1)}, u32[]{:S(2)}, u32[]{:S(2)}) collective-permute-start(bf16[304,128]{1,0:T(8,128)(2,1)S(1)} %get-tuple-element.95), channel_id=1, source_target_pairs={{0,16},{1,17},{2,18},{3,19},{4,20},{5,21},{6,22},{7,23},{16,0},{17... | collective-permute-start | bytes 233480 | tf_op jit(solution)/shard_map/ppermute | solution.py:344
  33.6 4.4 %collective-permute-start.4 = (bf16[304,128]{1,0:T(8,128)(2,1)S(1)}, bf16[304,128]{1,0:T(8,128)(2,1)S(1)}, u32[]{:S(2)}, u32[]{:S(2)}) collective-permute-start(bf16[304,128]{1,0:T(8,128)(2,1)S(1)} %get-tuple-element.93), channel_id=1, source_target_pairs={{0,1},{1,0},{2,3},{3,2},{4,5},{5,4},{6,7},{7,6},{16,17},{17,16},{1... | collective-permute-start | bytes 233480 | tf_op jit(solution)/shard_map/ppermute | solution.py:344
  38.1 9.1 %collective-permute-start.9 = (bf16[304,128]{1,0:T(8,128)(2,1)S(1)}, bf16[304,128]{1,0:T(8,128)(2,1)S(1)}, u32[]{:S(2)}, u32[]{:S(2)}) collective-permute-start(bf16[304,128]{1,0:T(8,128)(2,1)S(1)} %fusion.1), channel_id=1, source_target_pairs={{0,6},{1,7},{2,4},{3,5},{4,2},{5,3},{6,0},{7,1},{8,14},{9,15},{10,... | collective-permute-start | bytes 233480 | tf_op jit(solution)/shard_map/ppermute | solution.py:344
  41.7 7.4 %collective-permute-start.8 = (bf16[304,128]{1,0:T(8,128)(2,1)S(1)}, bf16[304,128]{1,0:T(8,128)(2,1)S(1)}, u32[]{:S(2)}, u32[]{:S(2)}) collective-permute-start(bf16[304,128]{1,0:T(8,128)(2,1)S(1)} %fusion.1), channel_id=1, source_target_pairs={{0,4},{1,5},{2,6},{3,7},{4,0},{5,1},{6,2},{7,3},{8,12},{9,13},{10,... | collective-permute-start | bytes 233480 | tf_op jit(solution)/shard_map/ppermute | solution.py:344
  41.7 7.4 %collective-permute-start.7 = (bf16[304,128]{1,0:T(8,128)(2,1)S(1)}, bf16[304,128]{1,0:T(8,128)(2,1)S(1)}, u32[]{:S(2)}, u32[]{:S(2)}) collective-permute-start(bf16[304,128]{1,0:T(8,128)(2,1)S(1)} %fusion.1), channel_id=1, source_target_pairs={{0,2},{1,3},{2,0},{3,1},{4,6},{5,7},{6,4},{7,5},{8,10},{9,11},{10,... | collective-permute-start | bytes 233480 | tf_op jit(solution)/shard_map/ppermute | solution.py:344
  42.5 10.2 %collective-permute-start.13 = (bf16[3,192,256]{2,1,0:T(8,128)(2,1)S(1)}, bf16[3,192,256]{2,1,0:T(8,128)(2,1)S(1)}, u32[]{:S(2)}, u32[]{:S(2)}) collective-permute-start(bf16[3,192,256]{2,1,0:T(8,128)(2,1)S(1)} %get-tuple-element.65.refs_1_.gz_second_ref), channel_id=1, source_target_pairs={{1,2},{3,4},{5,6},{2,1},{4,3},{6,5},{9,10},{11,12},{13,14},{10,9},... | collective-permute-start | bytes 884744 | tf_op jit(solution)/shard_map/ppermute | solution.py:382
  49.1 6.1 %collective-permute-start.12 = (bf16[304,128]{1,0:T(8,128)(2,1)S(1)}, bf16[304,128]{1,0:T(8,128)(2,1)S(1)}, u32[]{:S(2)}, u32[]{:S(2)}) collective-permute-start(bf16[304,128]{1,0:T(8,128)(2,1)S(1)} %add_convert_fusion.1), channel_id=1, source_target_pairs={{0,17},{1,16},{2,19},{3,18},{4,21},{5,20},{6,23},{7,22},{16,1},{17... | collective-permute-start | bytes 233480 | tf_op jit(solution)/shard_map/ppermute | solution.py:344
  52.1 4.4 %collective-permute-start.11 = (bf16[304,128]{1,0:T(8,128)(2,1)S(1)}, bf16[304,128]{1,0:T(8,128)(2,1)S(1)}, u32[]{:S(2)}, u32[]{:S(2)}) collective-permute-start(bf16[304,128]{1,0:T(8,128)(2,1)S(1)} %add_convert_fusion.1), channel_id=1, source_target_pairs={{0,16},{1,17},{2,18},{3,19},{4,20},{5,21},{6,22},{7,23},{16,0},{17... | collective-permute-start | bytes 233480 | tf_op jit(solution)/shard_map/ppermute | solution.py:344
  52.6 4.4 %collective-permute-start.10 = (bf16[304,128]{1,0:T(8,128)(2,1)S(1)}, bf16[304,128]{1,0:T(8,128)(2,1)S(1)}, u32[]{:S(2)}, u32[]{:S(2)}) collective-permute-start(bf16[304,128]{1,0:T(8,128)(2,1)S(1)} %add_convert_fusion.1), channel_id=1, source_target_pairs={{0,1},{1,0},{2,3},{3,2},{4,5},{5,4},{6,7},{7,6},{16,17},{17,16},{1... | collective-permute-start | bytes 233480 | tf_op jit(solution)/shard_map/ppermute | solution.py:344
  57.1 1.7 %collective-permute-start.14 = (bf16[4,304,128]{2,1,0:T(8,128)(2,1)S(1)}, bf16[4,304,128]{2,1,0:T(8,128)(2,1)S(1)}, u32[]{:S(2)}, u32[]{:S(2)}) collective-permute-start(bf16[4,304,128]{2,1,0:T(8,128)(2,1)S(1)} %pad_maximum_fusion.mine_ref), channel_id=1, source_target_pairs={{0,8},{8,0},{1,9},{9,1},{2,10},{10,2},{3,11},{11,3},{4,12},{12,4},... | collective-permute-start | bytes 933896 | tf_op jit(solution)/shard_map/ppermute | solution.py:344
  (3 other events, 5.1 us)

commit v5 on v4

--- a/solution.py
+++ b/solution.py
@@ -150,10 +150,9 @@
 def prepare_kernel(
     kernel_ref, win_ref, woutt_ref, bin_in_ref, *refs
 ):
-    count = len(refs) - 6
-    vectors, (taps_ref, back_ref, vec_ref, bin_ref, wint_ref, wout_ref) = refs[:count], refs[count:]
+    count = len(refs) - 5
+    vectors, (taps_ref, vec_ref, bin_ref, wint_ref, wout_ref) = refs[:count], refs[count:]
     spread_taps(kernel_ref, taps_ref, False)
-    spread_taps(kernel_ref, back_ref, True)
     for source, target in ((win_ref, wint_ref), (woutt_ref, wout_ref)):
         target[...] = source[...].T
     chans = vec_ref.shape[1]
@@ -258,9 +257,10 @@
 
 def input_kernel(
     out_first_ref, out_inner_ref, out_second_ref, gz_first_ref, gz_inner_ref, gz_second_ref,
-    halo_ref, g_ref, taps_ref,
-    out_ref, grad_ref, tall_ref,
-):
+    halo_ref, g_ref, kernel_ref,
+    out_ref, grad_ref, taps_ref, tall_ref,
+):
+    spread_taps(kernel_ref, taps_ref, True)
     low = is_low()
     rows = g_ref.shape[0]
     inner = rows - 2 * REACH
@@ -406,11 +406,11 @@
     across_lanes = jax.ShapeDtypeStruct((len(vectors), chans, 128), F32)
     hidden_lanes = jax.ShapeDtypeStruct((hidden_units, 128), F32)
     turned = jax.ShapeDtypeStruct((hidden_units, chans), BF16)
-    taps, back_taps, vectors, bias, w_in_t, w_out_turned = pl.pallas_call(
+    taps, vectors, bias, w_in_t, w_out_turned = pl.pallas_call(
         prepare_kernel,
-        out_shape=(spread, spread, across_lanes, hidden_lanes, turned, turned),
+        out_shape=(spread, across_lanes, hidden_lanes, turned, turned),
         in_specs=[IN_VMEM] * (4 + len(vectors)),
-        out_specs=(IN_VMEM,) * 6,
+        out_specs=(IN_VMEM,) * 5,
         compiler_params=SMALL,
     )(dw_kernel, w_in, w_out.T, b_in.reshape(-1, 128), *[vector[None] for vector in vectors])
     weights = (vectors, bias, w_in, w_in_t, w_out_turned, w_out.T)
@@ -463,14 +463,14 @@
         return swap(value, ("x", "space"), (turn >> 1) * strips | (turn & 1))
 
     own = added(at(0), *[partner(at(turn), turn) for turn in (1, 2, 3)])
-    out, grad_rest = pl.pallas_call(
+    out, grad_rest, back_taps = pl.pallas_call(
         input_kernel,
-        out_shape=(image, image),
+        out_shape=(image, image, spread),
         in_specs=[IN_VMEM] * 9,
-        out_specs=(IN_VMEM, IN_VMEM),
+        out_specs=(IN_VMEM,) * 3,
         scratch_shapes=[pltpu.VMEM((rows + REACH, chans, width), BF16)],
         compiler_params=PARAMS,
-    )(out_first, out_inner, out_second, gz_first, gz_inner, gz_second, gz_first_halo, g, back_taps)
+    )(out_first, out_inner, out_second, gz_first, gz_inner, gz_second, gz_first_halo, g, dw_kernel)
     bit = 2
     while bit < strips:
         masks = (bit, 2 * bit, 3 * bit) if 2 * bit < strips else (bit,)

time: 60.4 us -> 59.3 us (0.982)
  Pallas kernels: 24.2 us -> 23.5 us
    pallas_call x2, Pallas kernels: 6.17 us -> 5.4 us  [the longest x1 4.2 us: on_device(): pl.pallas_call(input_kernel, out_shape=(image, image, spread), in_specs=[...]
  transfers between devices with their start and end apart: 15 -> 15, of which waited for: 9 -> 10; matrix products, arithmetic and copies ran while one was open for 0% -> 0% of each run, Pallas kernels for 39% -> 38%
where the time goes in v5:
time: 59.3 us; the launch traced here: 59.1 us
  Pallas kernels  23.5 us (40%)
  starting transfers between devices  20.4 us (34%)
  waiting for transfers between devices  12.1 us (20%)
  local copies, waits for them, and re-layouts  2.03 us (3%)
  between operations  0.91 us (2%)
    ppermute x13, starting transfers between devices, swap(): lax.ppermute(value, axis, [(source, source ^ mask) for source in range(co...  18.9 us
    ppermute x13, waiting for transfers between devices, swap(): lax.ppermute(value, axis, [(source, source ^ mask) for source in range(co...  12 us
    pallas_call x1, Pallas kernels, on_device(): pl.pallas_call(first_kernel, out_shape=(narrow, narrow, *terms), in_specs...  5.26 us
    pallas_call x1, Pallas kernels, on_device(): pl.pallas_call(input_kernel, out_shape=(image, image, spread), in_specs=[...  4.2 us
    pallas_call x1, Pallas kernels, on_device(): pl.pallas_call(second_kernel, out_shape=(narrow, narrow, tall, *kept(REAC...  4.03 us
    pallas_call x1, Pallas kernels, on_device(): pl.pallas_call(inner_kernel, out_shape=(middle, middle, *terms), in_specs...  3.52 us
    pallas_call x1, Pallas kernels, on_device(): pl.pallas_call(input_rest_kernel, out_shape=image, in_specs=[IN_VMEM] * 6...  2.44 us
    unnamed x24, local copies, waits for them, and re-layouts  2 us
  transfers between devices with their start and end apart: 15, of which 10 were waited for; matrix products, arithmetic and copies ran while one was open for 0% of the time, Pallas kernels for 38%

profile of v5, /device:TPU:0, one launch (start us, length us, event | category | flops | bytes accessed | tf_op | source)
XLA Modules:
  0.0 59.1 jit_solution(10589512855978004830)
XLA Ops:
  0.7 1.1 %copy-done = bf16[1,1,8,256,192]{3,4,2,1,0:T(8,128)(2,1)S(1)} copy-done((bf16[1,1,8,256,192]{3,4,2,1,0:T(8,128)(2,1)S(1)}, bf16[1,1,8,256,192]{3,4,2,1,0:T(8,128)(2,1)}, u32[]{:S(2)}) %copy-start) | copy-done | bytes 786456
  1.9 3.0 %collective-permute-start = (bf16[3,192,256]{2,1,0:T(8,128)(2,1)S(1)}, bf16[3,192,256]{2,1,0:T(8,128)(2,1)S(1)}, u32[]{:S(2)}, u32[]{:S(2)}) collective-permute-start(bf16[3,192,256]{2,1,0:T(8,128)(2,1)S(1)} %shard_map.146), channel_id=1, source_target_pairs={{0,1},{1,0},{2,3},{3,2},{4,5},{5,4},{6,7},{7,6},{8,9},{9,8},{10,11... | collective-permute-start | bytes 884744 | tf_op jit(solution)/shard_map/ppermute | solution.py:344
  5.1 0.8 %copy-done.5 = f32[7,7,192]{2,1,0:T(8,128)S(1)} copy-done((f32[7,7,192]{2,1,0:T(8,128)S(1)}, f32[7,7,192]{2,1,0:T(8,128)}, u32[]{:S(2)}) %copy-start.5) | copy-done | bytes 37656
  5.9 1.2 %shard_map.147 = (bf16[12,112,224]{2,1,0:T(8,128)(2,1)S(1)}, f32[5,192,128]{2,1,0:T(8,128)S(1)}, f32[768,128]{1,0:T(8,128)S(1)}, bf16[768,192]{1,0:T(8,128)(2,1)S(1)}, bf16[768,192]{1,0:T(8,128)(2,1)S(1)}) custom-call(f32[7,7,192]{2,1,0:T(8,128)S(1)} %copy-done.5, bf16[192,768]{1,0:T(8,128)(2,1)S(1)} %copy-done.3, bf16[192,768]{1,0:T(8,128)(2,1)S(1)} %bitcast.44, ...), custom_call_target="tpu_custom_call" | custom-call | tf_op jit(solution)/shard_map/pallas_call | solution.py:409
  7.1 3.5 %shard_map.148 = (bf16[2,192,256]{2,1,0:T(8,128)(2,1)S(1)}, bf16[2,192,256]{2,1,0:T(8,128)(2,1)S(1)}, f32[192,768]{1,0:T(8,128)S(1)}, f32[192,768]{1,0:T(8,128)S(1)}, f32[12,8,112]{2,1,0:T(8,128)S(1)}) custom-call(bf16[8,192,256]{2,1,0:T(8,128)(2,1)S(1)} %bitcast.36, bf16[8,192,256]{2,1,0:T(8,128)(2,1)S(1)} %bitcast.39, ...), custom_call_target="tpu_custom_call" | custom-call | tf_op jit(solution)/shard_map/pallas_call | solution.py:417
  10.6 0.9 %collective-permute-start.1 = (bf16[3,192,256]{2,1,0:T(8,128)(2,1)S(1)}, bf16[3,192,256]{2,1,0:T(8,128)(2,1)S(1)}, u32[]{:S(2)}, u32[]{:S(2)}) collective-permute-start(bf16[3,192,256]{2,1,0:T(8,128)(2,1)S(1)} %shard_map.150), channel_id=1, source_target_pairs={{1,2},{3,4},{5,6},{2,1},{4,3},{6,5},{9,10},{11,12},{13,14},{10,9},... | collective-permute-start | bytes 884744 | tf_op jit(solution)/shard_map/ppermute | solution.py:382
  12.0 5.3 %shard_map.149 = (bf16[3,192,256]{2,1,0:T(8,128)(2,1)S(1)}, bf16[3,192,256]{2,1,0:T(8,128)(2,1)S(1)}, f32[192,768]{1,0:T(8,128)S(1)}, f32[192,768]{1,0:T(8,128)S(1)}, f32[12,8,112]{2,1,0:T(8,128)S(1)}) custom-call(bf16[8,192,256]{2,1,0:T(8,128)(2,1)S(1)} %bitcast.37, bf16[3,192,256]{2,1,0:T(8,128)(2,1)S(1)} %collective-permute-done.halo_ref, ...), custom_call_target="tpu_custom_call" | custom-call | tf_op jit(solution)/shard_map/pallas_call | solution.py:430
  17.2 3.9 %collective-permute-start.2 = (bf16[3,192,256]{2,1,0:T(8,128)(2,1)S(1)}, bf16[3,192,256]{2,1,0:T(8,128)(2,1)S(1)}, u32[]{:S(2)}, u32[]{:S(2)}) collective-permute-start(bf16[3,192,256]{2,1,0:T(8,128)(2,1)S(1)} %get-tuple-element.63.gz_first_ref), channel_id=1, source_target_pairs={{0,1},{1,0},{2,3},{3,2},{4,5},{5,4},{6,7},{7,6},{8,9},{9,8},{10,11... | collective-permute-start | bytes 884744 | tf_op jit(solution)/shard_map/ppermute | solution.py:344
  21.1 4.0 %shard_map.151 = (bf16[3,192,256]{2,1,0:T(8,128)(2,1)S(1)}, bf16[3,192,256]{2,1,0:T(8,128)(2,1)S(1)}, bf16[9,192,256]{2,1,0:T(8,128)(2,1)S(1)}, bf16[3,192,256]{...) custom-call(bf16[8,192,256]{2,1,0:T(8,128)(2,1)S(1)} %bitcast.38, ...), custom_call_target="tpu_custom_call" | custom-call | tf_op jit(solution)/shard_map/pallas_call | solution.py:439
  25.2 1.6 %shard_map.152 = (bf16[1216,128]{1,0:T(8,128)(2,1)S(1)}, bf16[1216,128]{1,0:T(8,128)(2,1)S(1)}) custom-call(bf16[9,192,256]{2,1,0:T(8,128)(2,1)S(1)} %get-tuple-element.66.refs_0_, bf16[3,192,256]{2,1,0:T(8,128)(2,1)S(1)} %get-tuple-element.65.refs_1_.gz_second_ref, bf16[3,192,256]{2,1,0:T(8,128)(2,1)S(1)} %get-tuple-element.67.refs_2_, ...), custom_call_target="tpu_custom_call" | custom-call | tf_op jit(solution)/shard_map/pallas_call | solution.py:447
  26.8 0.8 %collective-permute-done.2.halo_ref = bf16[3,192,256]{2,1,0:T(8,128)(2,1)S(1)} collective-permute-done((bf16[3,192,256]{2,1,0:T(8,128)(2,1)S(1)}, bf16[3,192,256]{2,1,0:T(8,128)(2,1)S(1)}, u32[]{:S(2)}, u32[]{:S(2)}) %collective-permute-start.2) | collective-permute-done | bytes 294944 | tf_op jit(solution)/shard_map/ppermute | solution.py:344
  27.6 1.6 %collective-permute-done.3 = bf16[1216,128]{1,0:T(8,128)(2,1)S(1)} collective-permute-done((bf16[1216,128]{1,0:T(8,128)(2,1)S(1)}, bf16[1216,128]{1,0:T(8,128)(2,1)S(1)}, u32[]{:S(2)}, u32[]{:S(2)}) %collective-permute-start.3) | collective-permute-done | bytes 311328 | tf_op jit(solution)/shard_map/ppermute | solution.py:344
  29.3 2.7 %collective-permute-start.6 = (bf16[304,128]{1,0:T(8,128)(2,1)S(1)}, bf16[304,128]{1,0:T(8,128)(2,1)S(1)}, u32[]{:S(2)}, u32[]{:S(2)}) collective-permute-start(bf16[304,128]{1,0:T(8,128)(2,1)S(1)} %get-tuple-element.94), channel_id=1, source_target_pairs={{0,17},{1,16},{2,19},{3,18},{4,21},{5,20},{6,23},{7,22},{16,1},{17... | collective-permute-start | bytes 233480 | tf_op jit(solution)/shard_map/ppermute | solution.py:344
  32.9 2.3 %collective-permute-done.6 = bf16[304,128]{1,0:T(8,128)(2,1)S(1)} collective-permute-done((bf16[304,128]{1,0:T(8,128)(2,1)S(1)}, bf16[304,128]{1,0:T(8,128)(2,1)S(1)}, u32[]{:S(2)}, u32[]{:S(2)}) %collective-permute-start.6) | collective-permute-done | bytes 77856 | tf_op jit(solution)/shard_map/ppermute | solution.py:344
  35.2 1.4 %collective-permute-done.5 = bf16[304,128]{1,0:T(8,128)(2,1)S(1)} collective-permute-done((bf16[304,128]{1,0:T(8,128)(2,1)S(1)}, bf16[304,128]{1,0:T(8,128)(2,1)S(1)}, u32[]{:S(2)}, u32[]{:S(2)}) %collective-permute-start.5) | collective-permute-done | bytes 77856 | tf_op jit(solution)/shard_map/ppermute | solution.py:344
  37.0 3.7 %collective-permute-start.9 = (bf16[304,128]{1,0:T(8,128)(2,1)S(1)}, bf16[304,128]{1,0:T(8,128)(2,1)S(1)}, u32[]{:S(2)}, u32[]{:S(2)}) collective-permute-start(bf16[304,128]{1,0:T(8,128)(2,1)S(1)} %fusion.1), channel_id=1, source_target_pairs={{0,6},{1,7},{2,4},{3,5},{4,2},{5,3},{6,0},{7,1},{8,14},{9,15},{10,... | collective-permute-start | bytes 233480 | tf_op jit(solution)/shard_map/ppermute | solution.py:344
  40.7 0.8 %collective-permute-start.7 = (bf16[304,128]{1,0:T(8,128)(2,1)S(1)}, bf16[304,128]{1,0:T(8,128)(2,1)S(1)}, u32[]{:S(2)}, u32[]{:S(2)}) collective-permute-start(bf16[304,128]{1,0:T(8,128)(2,1)S(1)} %fusion.1), channel_id=1, source_target_pairs={{0,2},{1,3},{2,0},{3,1},{4,6},{5,7},{6,4},{7,5},{8,10},{9,11},{10,... | collective-permute-start | bytes 233480 | tf_op jit(solution)/shard_map/ppermute | solution.py:344
  42.2 4.2 %shard_map.153 = (bf16[8,192,256]{2,1,0:T(8,128)(2,1)}, bf16[8,192,256]{2,1,0:T(8,128)(2,1)}, bf16[12,112,224]{2,1,0:T(8,128)(2,1)S(1)}) custom-call(bf16[3,192,256]{2,1,0:T(8,128)(2,1)S(1)} %get-tuple-element.58.out_first_ref, bf16[2,192,256]{2,1,0:T(8,128)(2,1)S(1)} %get-tuple-element.60.out_inner_ref, ...), custom_call_target="tpu_custom_call" | custom-call | tf_op jit(solution)/shard_map/pallas_call | solution.py:466
  46.4 1.7 %collective-permute-done.8 = bf16[304,128]{1,0:T(8,128)(2,1)S(1)} collective-permute-done((bf16[304,128]{1,0:T(8,128)(2,1)S(1)}, bf16[304,128]{1,0:T(8,128)(2,1)S(1)}, u32[]{:S(2)}, u32[]{:S(2)}) %collective-permute-start.8) | collective-permute-done | bytes 77856 | tf_op jit(solution)/shard_map/ppermute | solution.py:344
  48.1 3.3 %collective-permute-start.12 = (bf16[304,128]{1,0:T(8,128)(2,1)S(1)}, bf16[304,128]{1,0:T(8,128)(2,1)S(1)}, u32[]{:S(2)}, u32[]{:S(2)}) collective-permute-start(bf16[304,128]{1,0:T(8,128)(2,1)S(1)} %add_convert_fusion.1), channel_id=1, source_target_pairs={{0,17},{1,16},{2,19},{3,18},{4,21},{5,20},{6,23},{7,22},{16,1},{17... | collective-permute-start | bytes 233480 | tf_op jit(solution)/shard_map/ppermute | solution.py:344
  52.0 2.4 %shard_map.154 = bf16[8,192,256]{2,1,0:T(8,128)(2,1)} custom-call(bf16[3,192,256]{2,1,0:T(8,128)(2,1)S(1)} %collective-permute-done.13.halo_ref, bf16[3,192,256]{2,1,0:T(8,128)(2,1)S(1)} %get-tuple-element.63.gz_first_ref, bf16[2,192,256]{2,1,0:T(8,128)(2,1)S(1)} %get-tuple-element.64.gz_inner_ref, ...), custom_call_target="tpu_custom_call", output_to_operand_aliasing={{}: (6, {})} | custom-call | tf_op jit(solution)/shard_map/pallas_call | solution.py:481
  54.5 1.3 %collective-permute-done.11 = bf16[304,128]{1,0:T(8,128)(2,1)S(1)} collective-permute-done((bf16[304,128]{1,0:T(8,128)(2,1)S(1)}, bf16[304,128]{1,0:T(8,128)(2,1)S(1)}, u32[]{:S(2)}, u32[]{:S(2)}) %collective-permute-start.11) | collective-permute-done | bytes 77856 | tf_op jit(solution)/shard_map/ppermute | solution.py:344
  56.4 1.6 %collective-permute-done.14.other_ref = bf16[4,304,128]{2,1,0:T(8,128)(2,1)S(1)} collective-permute-done((bf16[4,304,128]{2,1,0:T(8,128)(2,1)S(1)}, bf16[4,304,128]{2,1,0:T(8,128)(2,1)S(1)}, u32[]{:S(2)}, u32[]{:S(2)}) %collective-permute-start.14) | collective-permute-done | bytes 311328 | tf_op jit(solution)/shard_map/ppermute | solution.py:344
  58.0 1.1 %shard_map.155 = (f32[192,768]{1,0:T(8,128)}, f32[192,768]{1,0:T(8,128)}, f32[7,7,192]{2,1,0:T(8,128)}) custom-call(bf16[4,304,128]{2,1,0:T(8,128)(2,1)S(1)} %pad_maximum_fusion.mine_ref, bf16[4,304,128]{2,1,0:T(8,128)(2,1)S(1)} %collective-permute-done.14.other_ref), custom_call_target="tpu_custom_call" | custom-call | tf_op jit(solution)/shard_map/pallas_call | solution.py:496
  (45 shorter events, 3.9 us)
Async XLA Ops:
  0.6 4.3 %copy-start.6 = (f32[768]{0:T(1024)S(1)}, f32[768]{0:T(1024)}, u32[]{:S(2)}) copy-start(f32[768]{0:T(1024)} %param.17) | copy-start | bytes 9220
  0.6 4.3 %copy-start.7 = (f32[192]{0:T(256)S(1)}, f32[192]{0:T(256)}, u32[]{:S(2)}) copy-start(f32[192]{0:T(256)} %param.13) | copy-start | bytes 2308
  0.7 4.3 %copy-start.8 = (f32[192]{0:T(256)S(1)}, f32[192]{0:T(256)}, u32[]{:S(2)}) copy-start(f32[192]{0:T(256)} %param.14) | copy-start | bytes 2308
  0.7 4.3 %copy-start.9 = (f32[192]{0:T(256)S(1)}, f32[192]{0:T(256)}, u32[]{:S(2)}) copy-start(f32[192]{0:T(256)} %param.15) | copy-start | bytes 2308
  0.7 4.3 %copy-start.10 = (f32[192]{0:T(256)S(1)}, f32[192]{0:T(256)}, u32[]{:S(2)}) copy-start(f32[192]{0:T(256)} %param.19) | copy-start | bytes 2308
  0.7 4.3 %copy-start.11 = (f32[192]{0:T(256)S(1)}, f32[192]{0:T(256)}, u32[]{:S(2)}) copy-start(f32[192]{0:T(256)} %param.20) | copy-start | bytes 2308
  1.9 3.2 %copy-start.4 = (bf16[768,192]{0,1:T(8,128)(2,1)S(1)}, bf16[768,192]{0,1:T(8,128)(2,1)}, u32[]{:S(2)}) copy-start(bf16[768,192]{0,1:T(8,128)(2,1)} %param.18) | copy-start | bytes 884740
  1.9 5.2 %copy-start.1 = (bf16[1,1,8,256,192]{3,4,2,1,0:T(8,128)(2,1)S(1)}, bf16[1,1,8,256,192]{3,4,2,1,0:T(8,128)(2,1)}, u32[]{:S(2)}) copy-start(bf16[1,1,8,256,192]{3,4,2,1,0:T(8,128)(2,1)} %param.11) | copy-start | bytes 2359300
  1.9 5.2 %copy-start.2 = (bf16[1,1,8,256,192]{3,4,2,1,0:T(8,128)(2,1)S(1)}, bf16[1,1,8,256,192]{3,4,2,1,0:T(8,128)(2,1)}, u32[]{:S(2)}) copy-start(bf16[1,1,8,256,192]{3,4,2,1,0:T(8,128)(2,1)} %param.21) | copy-start | bytes 2359300
  1.9 10.0 %collective-permute-start = (bf16[3,192,256]{2,1,0:T(8,128)(2,1)S(1)}, bf16[3,192,256]{2,1,0:T(8,128)(2,1)S(1)}, u32[]{:S(2)}, u32[]{:S(2)}) collective-permute-start(bf16[3,192,256]{2,1,0:T(8,128)(2,1)S(1)} %shard_map.146), channel_id=1, source_target_pairs={{0,1},{1,0},{2,3},{3,2},{4,5},{5,4},{6,7},{7,6},{8,9},{9,8},{10,11... | collective-permute-start | bytes 884744 | tf_op jit(solution)/shard_map/ppermute | solution.py:344
  10.6 10.5 %collective-permute-start.1 = (bf16[3,192,256]{2,1,0:T(8,128)(2,1)S(1)}, bf16[3,192,256]{2,1,0:T(8,128)(2,1)S(1)}, u32[]{:S(2)}, u32[]{:S(2)}) collective-permute-start(bf16[3,192,256]{2,1,0:T(8,128)(2,1)S(1)} %shard_map.150), channel_id=1, source_target_pairs={{1,2},{3,4},{5,6},{2,1},{4,3},{6,5},{9,10},{11,12},{13,14},{10,9},... | collective-permute-start | bytes 884744 | tf_op jit(solution)/shard_map/ppermute | solution.py:382
  17.2 10.4 %collective-permute-start.2 = (bf16[3,192,256]{2,1,0:T(8,128)(2,1)S(1)}, bf16[3,192,256]{2,1,0:T(8,128)(2,1)S(1)}, u32[]{:S(2)}, u32[]{:S(2)}) collective-permute-start(bf16[3,192,256]{2,1,0:T(8,128)(2,1)S(1)} %get-tuple-element.63.gz_first_ref), channel_id=1, source_target_pairs={{0,1},{1,0},{2,3},{3,2},{4,5},{5,4},{6,7},{7,6},{8,9},{9,8},{10,11... | collective-permute-start | bytes 884744 | tf_op jit(solution)/shard_map/ppermute | solution.py:344
  27.6 1.6 %collective-permute-start.3 = (bf16[1216,128]{1,0:T(8,128)(2,1)S(1)}, bf16[1216,128]{1,0:T(8,128)(2,1)S(1)}, u32[]{:S(2)}, u32[]{:S(2)}) collective-permute-start(bf16[1216,128]{1,0:T(8,128)(2,1)S(1)} %get-tuple-element.79), channel_id=1, source_target_pairs={{0,8},{8,0},{1,9},{9,1},{2,10},{10,2},{3,11},{11,3},{4,12},{12,4},... | collective-permute-start | bytes 933896 | tf_op jit(solution)/shard_map/ppermute | solution.py:344
  29.3 5.9 %collective-permute-start.6 = (bf16[304,128]{1,0:T(8,128)(2,1)S(1)}, bf16[304,128]{1,0:T(8,128)(2,1)S(1)}, u32[]{:S(2)}, u32[]{:S(2)}) collective-permute-start(bf16[304,128]{1,0:T(8,128)(2,1)S(1)} %get-tuple-element.94), channel_id=1, source_target_pairs={{0,17},{1,16},{2,19},{3,18},{4,21},{5,20},{6,23},{7,22},{16,1},{17... | collective-permute-start | bytes 233480 | tf_op jit(solution)/shard_map/ppermute | solution.py:344
  32.0 4.6 %collective-permute-start.5 = (bf16[304,128]{1,0:T(8,128)(2,1)S(1)}, bf16[304,128]{1,0:T(8,128)(2,1)S(1)}, u32[]{:S(2)}, u32[]{:S(2)}) collective-permute-start(bf16[304,128]{1,0:T(8,128)(2,1)S(1)} %get-tuple-element.95), channel_id=1, source_target_pairs={{0,16},{1,17},{2,18},{3,19},{4,20},{5,21},{6,22},{7,23},{16,0},{17... | collective-permute-start | bytes 233480 | tf_op jit(solution)/shard_map/ppermute | solution.py:344
  32.6 4.4 %collective-permute-start.4 = (bf16[304,128]{1,0:T(8,128)(2,1)S(1)}, bf16[304,128]{1,0:T(8,128)(2,1)S(1)}, u32[]{:S(2)}, u32[]{:S(2)}) collective-permute-start(bf16[304,128]{1,0:T(8,128)(2,1)S(1)} %get-tuple-element.93), channel_id=1, source_target_pairs={{0,1},{1,0},{2,3},{3,2},{4,5},{5,4},{6,7},{7,6},{16,17},{17,16},{1... | collective-permute-start | bytes 233480 | tf_op jit(solution)/shard_map/ppermute | solution.py:344
  37.0 9.3 %collective-permute-start.9 = (bf16[304,128]{1,0:T(8,128)(2,1)S(1)}, bf16[304,128]{1,0:T(8,128)(2,1)S(1)}, u32[]{:S(2)}, u32[]{:S(2)}) collective-permute-start(bf16[304,128]{1,0:T(8,128)(2,1)S(1)} %fusion.1), channel_id=1, source_target_pairs={{0,6},{1,7},{2,4},{3,5},{4,2},{5,3},{6,0},{7,1},{8,14},{9,15},{10,... | collective-permute-start | bytes 233480 | tf_op jit(solution)/shard_map/ppermute | solution.py:344
  40.7 7.4 %collective-permute-start.8 = (bf16[304,128]{1,0:T(8,128)(2,1)S(1)}, bf16[304,128]{1,0:T(8,128)(2,1)S(1)}, u32[]{:S(2)}, u32[]{:S(2)}) collective-permute-start(bf16[304,128]{1,0:T(8,128)(2,1)S(1)} %fusion.1), channel_id=1, source_target_pairs={{0,4},{1,5},{2,6},{3,7},{4,0},{5,1},{6,2},{7,3},{8,12},{9,13},{10,... | collective-permute-start | bytes 233480 | tf_op jit(solution)/shard_map/ppermute | solution.py:344
  40.7 7.4 %collective-permute-start.7 = (bf16[304,128]{1,0:T(8,128)(2,1)S(1)}, bf16[304,128]{1,0:T(8,128)(2,1)S(1)}, u32[]{:S(2)}, u32[]{:S(2)}) collective-permute-start(bf16[304,128]{1,0:T(8,128)(2,1)S(1)} %fusion.1), channel_id=1, source_target_pairs={{0,2},{1,3},{2,0},{3,1},{4,6},{5,7},{6,4},{7,5},{8,10},{9,11},{10,... | collective-permute-start | bytes 233480 | tf_op jit(solution)/shard_map/ppermute | solution.py:344
  41.5 10.5 %collective-permute-start.13 = (bf16[3,192,256]{2,1,0:T(8,128)(2,1)S(1)}, bf16[3,192,256]{2,1,0:T(8,128)(2,1)S(1)}, u32[]{:S(2)}, u32[]{:S(2)}) collective-permute-start(bf16[3,192,256]{2,1,0:T(8,128)(2,1)S(1)} %get-tuple-element.65.refs_1_.gz_second_ref), channel_id=1, source_target_pairs={{1,2},{3,4},{5,6},{2,1},{4,3},{6,5},{9,10},{11,12},{13,14},{10,9},... | collective-permute-start | bytes 884744 | tf_op jit(solution)/shard_map/ppermute | solution.py:382
  48.1 6.4 %collective-permute-start.12 = (bf16[304,128]{1,0:T(8,128)(2,1)S(1)}, bf16[304,128]{1,0:T(8,128)(2,1)S(1)}, u32[]{:S(2)}, u32[]{:S(2)}) collective-permute-start(bf16[304,128]{1,0:T(8,128)(2,1)S(1)} %add_convert_fusion.1), channel_id=1, source_target_pairs={{0,17},{1,16},{2,19},{3,18},{4,21},{5,20},{6,23},{7,22},{16,1},{17... | collective-permute-start | bytes 233480 | tf_op jit(solution)/shard_map/ppermute | solution.py:344
  51.3 4.4 %collective-permute-start.11 = (bf16[304,128]{1,0:T(8,128)(2,1)S(1)}, bf16[304,128]{1,0:T(8,128)(2,1)S(1)}, u32[]{:S(2)}, u32[]{:S(2)}) collective-permute-start(bf16[304,128]{1,0:T(8,128)(2,1)S(1)} %add_convert_fusion.1), channel_id=1, source_target_pairs={{0,16},{1,17},{2,18},{3,19},{4,20},{5,21},{6,22},{7,23},{16,0},{17... | collective-permute-start | bytes 233480 | tf_op jit(solution)/shard_map/ppermute | solution.py:344
  51.9 4.4 %collective-permute-start.10 = (bf16[304,128]{1,0:T(8,128)(2,1)S(1)}, bf16[304,128]{1,0:T(8,128)(2,1)S(1)}, u32[]{:S(2)}, u32[]{:S(2)}) collective-permute-start(bf16[304,128]{1,0:T(8,128)(2,1)S(1)} %add_convert_fusion.1), channel_id=1, source_target_pairs={{0,1},{1,0},{2,3},{3,2},{4,5},{5,4},{6,7},{7,6},{16,17},{17,16},{1... | collective-permute-start | bytes 233480 | tf_op jit(solution)/shard_map/ppermute | solution.py:344
  56.3 1.7 %collective-permute-start.14 = (bf16[4,304,128]{2,1,0:T(8,128)(2,1)S(1)}, bf16[4,304,128]{2,1,0:T(8,128)(2,1)S(1)}, u32[]{:S(2)}, u32[]{:S(2)}) collective-permute-start(bf16[4,304,128]{2,1,0:T(8,128)(2,1)S(1)} %pad_maximum_fusion.mine_ref), channel_id=1, source_target_pairs={{0,8},{8,0},{1,9},{9,1},{2,10},{10,2},{3,11},{11,3},{4,12},{12,4},... | collective-permute-start | bytes 933896 | tf_op jit(solution)/shard_map/ppermute | solution.py:344
  (3 other events, 5.1 us)

commit v6 on v5

--- a/solution.py
+++ b/solution.py
@@ -277,7 +277,7 @@
         grad_ref[at] = (g_ref[at].astype(F32) + conv_row(tall_ref, taps_ref, row)).astype(BF16)
         return carry
 
-    lax.fori_loop(0, rows - REACH, step, 0)
+    lax.fori_loop(0, rows - REACH, step, 0, unroll=True)
 
 
 def input_rest_kernel(
@@ -298,7 +298,7 @@
         part_ref[row] = (g_ref[first + row].astype(F32) + conv_row(tall_ref, taps_ref, row)).astype(BF16)
         return carry
 
-    lax.fori_loop(0, REACH, step, 0)
+    lax.fori_loop(0, REACH, step, 0, unroll=True)
     copy = pltpu.make_async_copy(part_ref, grad_ref.at[pl.ds(first, REACH)], sem)
     copy.start()
     copy.wait()

time: 59.3 us -> 59 us (level)
  Pallas kernels: 23.5 us -> 22.4 us
  waiting for transfers between devices: 12.1 us -> 12.8 us
    ppermute x13, waiting for transfers between devices: 12 us -> 12.8 us  [swap(): lax.ppermute(value, axis, [(source, source ^ mask) for source in range(co...]
  transfers between devices with their start and end apart: 15 -> 15, of which waited for: 10 -> 10; matrix products, arithmetic and copies ran while one was open for 0% -> 0% of each run, Pallas kernels for 38% -> 36%
where the time goes in v6:
time: 59 us; the launch traced here: 58.8 us
  Pallas kernels  22.4 us (38%)
  starting transfers between devices  20.3 us (34%)
  waiting for transfers between devices  12.8 us (22%)
  local copies, waits for them, and re-layouts  2.03 us (3%)
  between operations  0.91 us (2%)
    ppermute x13, starting transfers between devices, swap(): lax.ppermute(value, axis, [(source, source ^ mask) for source in range(co...  18.6 us
    ppermute x13, waiting for transfers between devices, swap(): lax.ppermute(value, axis, [(source, source ^ mask) for source in range(co...  12.8 us
    pallas_call x1, Pallas kernels, on_device(): pl.pallas_call(first_kernel, out_shape=(narrow, narrow, *terms), in_specs...  5.26 us
    pallas_call x1, Pallas kernels, on_device(): pl.pallas_call(second_kernel, out_shape=(narrow, narrow, tall, *kept(REAC...  4.03 us
    pallas_call x1, Pallas kernels, on_device(): pl.pallas_call(input_kernel, out_shape=(image, image, spread), in_specs=[...  3.63 us
    pallas_call x1, Pallas kernels, on_device(): pl.pallas_call(inner_kernel, out_shape=(middle, middle, *terms), in_specs...  3.52 us
    unnamed x24, local copies, waits for them, and re-layouts  2 us
    pallas_call x1, Pallas kernels, on_device(): pl.pallas_call(input_rest_kernel, out_shape=image, in_specs=[IN_VMEM] * 6...  2 us
  transfers between devices with their start and end apart: 15, of which 10 were waited for; matrix products, arithmetic and copies ran while one was open for 0% of the time, Pallas kernels for 36%

profile of v6, /device:TPU:0, one launch (start us, length us, event | category | flops | bytes accessed | tf_op | source)
XLA Modules:
  0.0 58.8 jit_solution(17765811067658349785)
XLA Ops:
  0.7 1.1 %copy-done = bf16[1,1,8,256,192]{3,4,2,1,0:T(8,128)(2,1)S(1)} copy-done((bf16[1,1,8,256,192]{3,4,2,1,0:T(8,128)(2,1)S(1)}, bf16[1,1,8,256,192]{3,4,2,1,0:T(8,128)(2,1)}, u32[]{:S(2)}) %copy-start) | copy-done | bytes 786456
  1.9 3.0 %collective-permute-start = (bf16[3,192,256]{2,1,0:T(8,128)(2,1)S(1)}, bf16[3,192,256]{2,1,0:T(8,128)(2,1)S(1)}, u32[]{:S(2)}, u32[]{:S(2)}) collective-permute-start(bf16[3,192,256]{2,1,0:T(8,128)(2,1)S(1)} %shard_map.146), channel_id=1, source_target_pairs={{0,1},{1,0},{2,3},{3,2},{4,5},{5,4},{6,7},{7,6},{8,9},{9,8},{10,11... | collective-permute-start | bytes 884744 | tf_op jit(solution)/shard_map/ppermute | solution.py:344
  5.1 0.8 %copy-done.5 = f32[7,7,192]{2,1,0:T(8,128)S(1)} copy-done((f32[7,7,192]{2,1,0:T(8,128)S(1)}, f32[7,7,192]{2,1,0:T(8,128)}, u32[]{:S(2)}) %copy-start.5) | copy-done | bytes 37656
  5.9 1.2 %shard_map.147 = (bf16[12,112,224]{2,1,0:T(8,128)(2,1)S(1)}, f32[5,192,128]{2,1,0:T(8,128)S(1)}, f32[768,128]{1,0:T(8,128)S(1)}, bf16[768,192]{1,0:T(8,128)(2,1)S(1)}, bf16[768,192]{1,0:T(8,128)(2,1)S(1)}) custom-call(f32[7,7,192]{2,1,0:T(8,128)S(1)} %copy-done.5, bf16[192,768]{1,0:T(8,128)(2,1)S(1)} %copy-done.3, bf16[192,768]{1,0:T(8,128)(2,1)S(1)} %bitcast.44, ...), custom_call_target="tpu_custom_call" | custom-call | tf_op jit(solution)/shard_map/pallas_call | solution.py:409
  7.1 3.5 %shard_map.148 = (bf16[2,192,256]{2,1,0:T(8,128)(2,1)S(1)}, bf16[2,192,256]{2,1,0:T(8,128)(2,1)S(1)}, f32[192,768]{1,0:T(8,128)S(1)}, f32[192,768]{1,0:T(8,128)S(1)}, f32[12,8,112]{2,1,0:T(8,128)S(1)}) custom-call(bf16[8,192,256]{2,1,0:T(8,128)(2,1)S(1)} %bitcast.36, bf16[8,192,256]{2,1,0:T(8,128)(2,1)S(1)} %bitcast.39, ...), custom_call_target="tpu_custom_call" | custom-call | tf_op jit(solution)/shard_map/pallas_call | solution.py:417
  10.6 0.9 %collective-permute-start.1 = (bf16[3,192,256]{2,1,0:T(8,128)(2,1)S(1)}, bf16[3,192,256]{2,1,0:T(8,128)(2,1)S(1)}, u32[]{:S(2)}, u32[]{:S(2)}) collective-permute-start(bf16[3,192,256]{2,1,0:T(8,128)(2,1)S(1)} %shard_map.150), channel_id=1, source_target_pairs={{1,2},{3,4},{5,6},{2,1},{4,3},{6,5},{9,10},{11,12},{13,14},{10,9},... | collective-permute-start | bytes 884744 | tf_op jit(solution)/shard_map/ppermute | solution.py:382
  12.0 5.3 %shard_map.149 = (bf16[3,192,256]{2,1,0:T(8,128)(2,1)S(1)}, bf16[3,192,256]{2,1,0:T(8,128)(2,1)S(1)}, f32[192,768]{1,0:T(8,128)S(1)}, f32[192,768]{1,0:T(8,128)S(1)}, f32[12,8,112]{2,1,0:T(8,128)S(1)}) custom-call(bf16[8,192,256]{2,1,0:T(8,128)(2,1)S(1)} %bitcast.37, bf16[3,192,256]{2,1,0:T(8,128)(2,1)S(1)} %collective-permute-done.halo_ref, ...), custom_call_target="tpu_custom_call" | custom-call | tf_op jit(solution)/shard_map/pallas_call | solution.py:430
  17.2 3.9 %collective-permute-start.2 = (bf16[3,192,256]{2,1,0:T(8,128)(2,1)S(1)}, bf16[3,192,256]{2,1,0:T(8,128)(2,1)S(1)}, u32[]{:S(2)}, u32[]{:S(2)}) collective-permute-start(bf16[3,192,256]{2,1,0:T(8,128)(2,1)S(1)} %get-tuple-element.63.gz_first_ref), channel_id=1, source_target_pairs={{0,1},{1,0},{2,3},{3,2},{4,5},{5,4},{6,7},{7,6},{8,9},{9,8},{10,11... | collective-permute-start | bytes 884744 | tf_op jit(solution)/shard_map/ppermute | solution.py:344
  21.1 4.0 %shard_map.151 = (bf16[3,192,256]{2,1,0:T(8,128)(2,1)S(1)}, bf16[3,192,256]{2,1,0:T(8,128)(2,1)S(1)}, bf16[9,192,256]{2,1,0:T(8,128)(2,1)S(1)}, bf16[3,192,256]{...) custom-call(bf16[8,192,256]{2,1,0:T(8,128)(2,1)S(1)} %bitcast.38, ...), custom_call_target="tpu_custom_call" | custom-call | tf_op jit(solution)/shard_map/pallas_call | solution.py:439
  25.2 1.6 %shard_map.152 = (bf16[1216,128]{1,0:T(8,128)(2,1)S(1)}, bf16[1216,128]{1,0:T(8,128)(2,1)S(1)}) custom-call(bf16[9,192,256]{2,1,0:T(8,128)(2,1)S(1)} %get-tuple-element.66.refs_0_, bf16[3,192,256]{2,1,0:T(8,128)(2,1)S(1)} %get-tuple-element.65.refs_1_.gz_second_ref, bf16[3,192,256]{2,1,0:T(8,128)(2,1)S(1)} %get-tuple-element.67.refs_2_, ...), custom_call_target="tpu_custom_call" | custom-call | tf_op jit(solution)/shard_map/pallas_call | solution.py:447
  27.6 1.6 %collective-permute-done.3 = bf16[1216,128]{1,0:T(8,128)(2,1)S(1)} collective-permute-done((bf16[1216,128]{1,0:T(8,128)(2,1)S(1)}, bf16[1216,128]{1,0:T(8,128)(2,1)S(1)}, u32[]{:S(2)}, u32[]{:S(2)}) %collective-permute-start.3) | collective-permute-done | bytes 311328 | tf_op jit(solution)/shard_map/ppermute | solution.py:344
  29.3 2.7 %collective-permute-start.6 = (bf16[304,128]{1,0:T(8,128)(2,1)S(1)}, bf16[304,128]{1,0:T(8,128)(2,1)S(1)}, u32[]{:S(2)}, u32[]{:S(2)}) collective-permute-start(bf16[304,128]{1,0:T(8,128)(2,1)S(1)} %get-tuple-element.94), channel_id=1, source_target_pairs={{0,17},{1,16},{2,19},{3,18},{4,21},{5,20},{6,23},{7,22},{16,1},{17... | collective-permute-start | bytes 233480 | tf_op jit(solution)/shard_map/ppermute | solution.py:344
  32.9 2.3 %collective-permute-done.6 = bf16[304,128]{1,0:T(8,128)(2,1)S(1)} collective-permute-done((bf16[304,128]{1,0:T(8,128)(2,1)S(1)}, bf16[304,128]{1,0:T(8,128)(2,1)S(1)}, u32[]{:S(2)}, u32[]{:S(2)}) %collective-permute-start.6) | collective-permute-done | bytes 77856 | tf_op jit(solution)/shard_map/ppermute | solution.py:344
  35.2 1.4 %collective-permute-done.5 = bf16[304,128]{1,0:T(8,128)(2,1)S(1)} collective-permute-done((bf16[304,128]{1,0:T(8,128)(2,1)S(1)}, bf16[304,128]{1,0:T(8,128)(2,1)S(1)}, u32[]{:S(2)}, u32[]{:S(2)}) %collective-permute-start.5) | collective-permute-done | bytes 77856 | tf_op jit(solution)/shard_map/ppermute | solution.py:344
  37.0 3.7 %collective-permute-start.9 = (bf16[304,128]{1,0:T(8,128)(2,1)S(1)}, bf16[304,128]{1,0:T(8,128)(2,1)S(1)}, u32[]{:S(2)}, u32[]{:S(2)}) collective-permute-start(bf16[304,128]{1,0:T(8,128)(2,1)S(1)} %fusion.1), channel_id=1, source_target_pairs={{0,6},{1,7},{2,4},{3,5},{4,2},{5,3},{6,0},{7,1},{8,14},{9,15},{10,... | collective-permute-start | bytes 233480 | tf_op jit(solution)/shard_map/ppermute | solution.py:344
  40.7 0.8 %collective-permute-start.7 = (bf16[304,128]{1,0:T(8,128)(2,1)S(1)}, bf16[304,128]{1,0:T(8,128)(2,1)S(1)}, u32[]{:S(2)}, u32[]{:S(2)}) collective-permute-start(bf16[304,128]{1,0:T(8,128)(2,1)S(1)} %fusion.1), channel_id=1, source_target_pairs={{0,2},{1,3},{2,0},{3,1},{4,6},{5,7},{6,4},{7,5},{8,10},{9,11},{10,... | collective-permute-start | bytes 233480 | tf_op jit(solution)/shard_map/ppermute | solution.py:344
  41.5 0.9 %collective-permute-start.13 = (bf16[3,192,256]{2,1,0:T(8,128)(2,1)S(1)}, bf16[3,192,256]{2,1,0:T(8,128)(2,1)S(1)}, u32[]{:S(2)}, u32[]{:S(2)}) collective-permute-start(bf16[3,192,256]{2,1,0:T(8,128)(2,1)S(1)} %get-tuple-element.65.refs_1_.gz_second_ref), channel_id=1, source_target_pairs={{1,2},{3,4},{5,6},{2,1},{4,3},{6,5},{9,10},{11,12},{13,14},{10,9},... | collective-permute-start | bytes 884744 | tf_op jit(solution)/shard_map/ppermute | solution.py:382
  42.4 3.6 %shard_map.153 = (bf16[8,192,256]{2,1,0:T(8,128)(2,1)}, bf16[8,192,256]{2,1,0:T(8,128)(2,1)}, bf16[12,112,224]{2,1,0:T(8,128)(2,1)S(1)}) custom-call(bf16[3,192,256]{2,1,0:T(8,128)(2,1)S(1)} %get-tuple-element.58.out_first_ref, bf16[2,192,256]{2,1,0:T(8,128)(2,1)S(1)} %get-tuple-element.60.out_inner_ref, ...), custom_call_target="tpu_custom_call" | custom-call | tf_op jit(solution)/shard_map/pallas_call | solution.py:466
  46.0 2.0 %collective-permute-done.8 = bf16[304,128]{1,0:T(8,128)(2,1)S(1)} collective-permute-done((bf16[304,128]{1,0:T(8,128)(2,1)S(1)}, bf16[304,128]{1,0:T(8,128)(2,1)S(1)}, u32[]{:S(2)}, u32[]{:S(2)}) %collective-permute-start.8) | collective-permute-done | bytes 77856 | tf_op jit(solution)/shard_map/ppermute | solution.py:344
  48.1 2.9 %collective-permute-start.12 = (bf16[304,128]{1,0:T(8,128)(2,1)S(1)}, bf16[304,128]{1,0:T(8,128)(2,1)S(1)}, u32[]{:S(2)}, u32[]{:S(2)}) collective-permute-start(bf16[304,128]{1,0:T(8,128)(2,1)S(1)} %add_convert_fusion.1), channel_id=1, source_target_pairs={{0,17},{1,16},{2,19},{3,18},{4,21},{5,20},{6,23},{7,22},{16,1},{17... | collective-permute-start | bytes 233480 | tf_op jit(solution)/shard_map/ppermute | solution.py:344
  51.6 2.0 %shard_map.154 = bf16[8,192,256]{2,1,0:T(8,128)(2,1)} custom-call(bf16[3,192,256]{2,1,0:T(8,128)(2,1)S(1)} %collective-permute-done.13.halo_ref, bf16[3,192,256]{2,1,0:T(8,128)(2,1)S(1)} %get-tuple-element.63.gz_first_ref, bf16[2,192,256]{2,1,0:T(8,128)(2,1)S(1)} %get-tuple-element.64.gz_inner_ref, ...), custom_call_target="tpu_custom_call", output_to_operand_aliasing={{}: (6, {})} | custom-call | tf_op jit(solution)/shard_map/pallas_call | solution.py:481
  53.7 1.7 %collective-permute-done.11 = bf16[304,128]{1,0:T(8,128)(2,1)S(1)} collective-permute-done((bf16[304,128]{1,0:T(8,128)(2,1)S(1)}, bf16[304,128]{1,0:T(8,128)(2,1)S(1)}, u32[]{:S(2)}, u32[]{:S(2)}) %collective-permute-start.11) | collective-permute-done | bytes 77856 | tf_op jit(solution)/shard_map/ppermute | solution.py:344
  56.0 1.6 %collective-permute-done.14.other_ref = bf16[4,304,128]{2,1,0:T(8,128)(2,1)S(1)} collective-permute-done((bf16[4,304,128]{2,1,0:T(8,128)(2,1)S(1)}, bf16[4,304,128]{2,1,0:T(8,128)(2,1)S(1)}, u32[]{:S(2)}, u32[]{:S(2)}) %collective-permute-start.14) | collective-permute-done | bytes 311328 | tf_op jit(solution)/shard_map/ppermute | solution.py:344
  57.6 1.1 %shard_map.155 = (f32[192,768]{1,0:T(8,128)}, f32[192,768]{1,0:T(8,128)}, f32[7,7,192]{2,1,0:T(8,128)}) custom-call(bf16[4,304,128]{2,1,0:T(8,128)(2,1)S(1)} %pad_maximum_fusion.mine_ref, bf16[4,304,128]{2,1,0:T(8,128)(2,1)S(1)} %collective-permute-done.14.other_ref), custom_call_target="tpu_custom_call" | custom-call | tf_op jit(solution)/shard_map/pallas_call | solution.py:496
  (45 shorter events, 4.0 us)
Async XLA Ops:
  0.6 4.3 %copy-start.6 = (f32[768]{0:T(1024)S(1)}, f32[768]{0:T(1024)}, u32[]{:S(2)}) copy-start(f32[768]{0:T(1024)} %param.17) | copy-start | bytes 9220
  0.6 4.3 %copy-start.7 = (f32[192]{0:T(256)S(1)}, f32[192]{0:T(256)}, u32[]{:S(2)}) copy-start(f32[192]{0:T(256)} %param.13) | copy-start | bytes 2308
  0.7 4.3 %copy-start.8 = (f32[192]{0:T(256)S(1)}, f32[192]{0:T(256)}, u32[]{:S(2)}) copy-start(f32[192]{0:T(256)} %param.14) | copy-start | bytes 2308
  0.7 4.3 %copy-start.9 = (f32[192]{0:T(256)S(1)}, f32[192]{0:T(256)}, u32[]{:S(2)}) copy-start(f32[192]{0:T(256)} %param.15) | copy-start | bytes 2308
  0.7 4.3 %copy-start.10 = (f32[192]{0:T(256)S(1)}, f32[192]{0:T(256)}, u32[]{:S(2)}) copy-start(f32[192]{0:T(256)} %param.19) | copy-start | bytes 2308
  0.7 4.3 %copy-start.11 = (f32[192]{0:T(256)S(1)}, f32[192]{0:T(256)}, u32[]{:S(2)}) copy-start(f32[192]{0:T(256)} %param.20) | copy-start | bytes 2308
  1.9 3.2 %copy-start.4 = (bf16[768,192]{0,1:T(8,128)(2,1)S(1)}, bf16[768,192]{0,1:T(8,128)(2,1)}, u32[]{:S(2)}) copy-start(bf16[768,192]{0,1:T(8,128)(2,1)} %param.18) | copy-start | bytes 884740
  1.9 5.2 %copy-start.1 = (bf16[1,1,8,256,192]{3,4,2,1,0:T(8,128)(2,1)S(1)}, bf16[1,1,8,256,192]{3,4,2,1,0:T(8,128)(2,1)}, u32[]{:S(2)}) copy-start(bf16[1,1,8,256,192]{3,4,2,1,0:T(8,128)(2,1)} %param.11) | copy-start | bytes 2359300
  1.9 5.2 %copy-start.2 = (bf16[1,1,8,256,192]{3,4,2,1,0:T(8,128)(2,1)S(1)}, bf16[1,1,8,256,192]{3,4,2,1,0:T(8,128)(2,1)}, u32[]{:S(2)}) copy-start(bf16[1,1,8,256,192]{3,4,2,1,0:T(8,128)(2,1)} %param.21) | copy-start | bytes 2359300
  1.9 10.0 %collective-permute-start = (bf16[3,192,256]{2,1,0:T(8,128)(2,1)S(1)}, bf16[3,192,256]{2,1,0:T(8,128)(2,1)S(1)}, u32[]{:S(2)}, u32[]{:S(2)}) collective-permute-start(bf16[3,192,256]{2,1,0:T(8,128)(2,1)S(1)} %shard_map.146), channel_id=1, source_target_pairs={{0,1},{1,0},{2,3},{3,2},{4,5},{5,4},{6,7},{7,6},{8,9},{9,8},{10,11... | collective-permute-start | bytes 884744 | tf_op jit(solution)/shard_map/ppermute | solution.py:344
  10.6 10.5 %collective-permute-start.1 = (bf16[3,192,256]{2,1,0:T(8,128)(2,1)S(1)}, bf16[3,192,256]{2,1,0:T(8,128)(2,1)S(1)}, u32[]{:S(2)}, u32[]{:S(2)}) collective-permute-start(bf16[3,192,256]{2,1,0:T(8,128)(2,1)S(1)} %shard_map.150), channel_id=1, source_target_pairs={{1,2},{3,4},{5,6},{2,1},{4,3},{6,5},{9,10},{11,12},{13,14},{10,9},... | collective-permute-start | bytes 884744 | tf_op jit(solution)/shard_map/ppermute | solution.py:382
  17.2 10.4 %collective-permute-start.2 = (bf16[3,192,256]{2,1,0:T(8,128)(2,1)S(1)}, bf16[3,192,256]{2,1,0:T(8,128)(2,1)S(1)}, u32[]{:S(2)}, u32[]{:S(2)}) collective-permute-start(bf16[3,192,256]{2,1,0:T(8,128)(2,1)S(1)} %get-tuple-element.63.gz_first_ref), channel_id=1, source_target_pairs={{0,1},{1,0},{2,3},{3,2},{4,5},{5,4},{6,7},{7,6},{8,9},{9,8},{10,11... | collective-permute-start | bytes 884744 | tf_op jit(solution)/shard_map/ppermute | solution.py:344
  27.6 1.6 %collective-permute-start.3 = (bf16[1216,128]{1,0:T(8,128)(2,1)S(1)}, bf16[1216,128]{1,0:T(8,128)(2,1)S(1)}, u32[]{:S(2)}, u32[]{:S(2)}) collective-permute-start(bf16[1216,128]{1,0:T(8,128)(2,1)S(1)} %get-tuple-element.79), channel_id=1, source_target_pairs={{0,8},{8,0},{1,9},{9,1},{2,10},{10,2},{3,11},{11,3},{4,12},{12,4},... | collective-permute-start | bytes 933896 | tf_op jit(solution)/shard_map/ppermute | solution.py:344
  29.3 5.9 %collective-permute-start.6 = (bf16[304,128]{1,0:T(8,128)(2,1)S(1)}, bf16[304,128]{1,0:T(8,128)(2,1)S(1)}, u32[]{:S(2)}, u32[]{:S(2)}) collective-permute-start(bf16[304,128]{1,0:T(8,128)(2,1)S(1)} %get-tuple-element.94), channel_id=1, source_target_pairs={{0,17},{1,16},{2,19},{3,18},{4,21},{5,20},{6,23},{7,22},{16,1},{17... | collective-permute-start | bytes 233480 | tf_op jit(solution)/shard_map/ppermute | solution.py:344
  32.0 4.6 %collective-permute-start.5 = (bf16[304,128]{1,0:T(8,128)(2,1)S(1)}, bf16[304,128]{1,0:T(8,128)(2,1)S(1)}, u32[]{:S(2)}, u32[]{:S(2)}) collective-permute-start(bf16[304,128]{1,0:T(8,128)(2,1)S(1)} %get-tuple-element.95), channel_id=1, source_target_pairs={{0,16},{1,17},{2,18},{3,19},{4,20},{5,21},{6,22},{7,23},{16,0},{17... | collective-permute-start | bytes 233480 | tf_op jit(solution)/shard_map/ppermute | solution.py:344
  32.6 4.4 %collective-permute-start.4 = (bf16[304,128]{1,0:T(8,128)(2,1)S(1)}, bf16[304,128]{1,0:T(8,128)(2,1)S(1)}, u32[]{:S(2)}, u32[]{:S(2)}) collective-permute-start(bf16[304,128]{1,0:T(8,128)(2,1)S(1)} %get-tuple-element.93), channel_id=1, source_target_pairs={{0,1},{1,0},{2,3},{3,2},{4,5},{5,4},{6,7},{7,6},{16,17},{17,16},{1... | collective-permute-start | bytes 233480 | tf_op jit(solution)/shard_map/ppermute | solution.py:344
  37.0 9.0 %collective-permute-start.9 = (bf16[304,128]{1,0:T(8,128)(2,1)S(1)}, bf16[304,128]{1,0:T(8,128)(2,1)S(1)}, u32[]{:S(2)}, u32[]{:S(2)}) collective-permute-start(bf16[304,128]{1,0:T(8,128)(2,1)S(1)} %fusion.1), channel_id=1, source_target_pairs={{0,6},{1,7},{2,4},{3,5},{4,2},{5,3},{6,0},{7,1},{8,14},{9,15},{10,... | collective-permute-start | bytes 233480 | tf_op jit(solution)/shard_map/ppermute | solution.py:344
  40.7 7.4 %collective-permute-start.8 = (bf16[304,128]{1,0:T(8,128)(2,1)S(1)}, bf16[304,128]{1,0:T(8,128)(2,1)S(1)}, u32[]{:S(2)}, u32[]{:S(2)}) collective-permute-start(bf16[304,128]{1,0:T(8,128)(2,1)S(1)} %fusion.1), channel_id=1, source_target_pairs={{0,4},{1,5},{2,6},{3,7},{4,0},{5,1},{6,2},{7,3},{8,12},{9,13},{10,... | collective-permute-start | bytes 233480 | tf_op jit(solution)/shard_map/ppermute | solution.py:344
  40.7 7.4 %collective-permute-start.7 = (bf16[304,128]{1,0:T(8,128)(2,1)S(1)}, bf16[304,128]{1,0:T(8,128)(2,1)S(1)}, u32[]{:S(2)}, u32[]{:S(2)}) collective-permute-start(bf16[304,128]{1,0:T(8,128)(2,1)S(1)} %fusion.1), channel_id=1, source_target_pairs={{0,2},{1,3},{2,0},{3,1},{4,6},{5,7},{6,4},{7,5},{8,10},{9,11},{10,... | collective-permute-start | bytes 233480 | tf_op jit(solution)/shard_map/ppermute | solution.py:344
  41.5 10.2 %collective-permute-start.13 = (bf16[3,192,256]{2,1,0:T(8,128)(2,1)S(1)}, bf16[3,192,256]{2,1,0:T(8,128)(2,1)S(1)}, u32[]{:S(2)}, u32[]{:S(2)}) collective-permute-start(bf16[3,192,256]{2,1,0:T(8,128)(2,1)S(1)} %get-tuple-element.65.refs_1_.gz_second_ref), channel_id=1, source_target_pairs={{1,2},{3,4},{5,6},{2,1},{4,3},{6,5},{9,10},{11,12},{13,14},{10,9},... | collective-permute-start | bytes 884744 | tf_op jit(solution)/shard_map/ppermute | solution.py:382
  48.1 5.6 %collective-permute-start.12 = (bf16[304,128]{1,0:T(8,128)(2,1)S(1)}, bf16[304,128]{1,0:T(8,128)(2,1)S(1)}, u32[]{:S(2)}, u32[]{:S(2)}) collective-permute-start(bf16[304,128]{1,0:T(8,128)(2,1)S(1)} %add_convert_fusion.1), channel_id=1, source_target_pairs={{0,17},{1,16},{2,19},{3,18},{4,21},{5,20},{6,23},{7,22},{16,1},{17... | collective-permute-start | bytes 233480 | tf_op jit(solution)/shard_map/ppermute | solution.py:344
  51.0 4.4 %collective-permute-start.11 = (bf16[304,128]{1,0:T(8,128)(2,1)S(1)}, bf16[304,128]{1,0:T(8,128)(2,1)S(1)}, u32[]{:S(2)}, u32[]{:S(2)}) collective-permute-start(bf16[304,128]{1,0:T(8,128)(2,1)S(1)} %add_convert_fusion.1), channel_id=1, source_target_pairs={{0,16},{1,17},{2,18},{3,19},{4,20},{5,21},{6,22},{7,23},{16,0},{17... | collective-permute-start | bytes 233480 | tf_op jit(solution)/shard_map/ppermute | solution.py:344
  51.5 4.4 %collective-permute-start.10 = (bf16[304,128]{1,0:T(8,128)(2,1)S(1)}, bf16[304,128]{1,0:T(8,128)(2,1)S(1)}, u32[]{:S(2)}, u32[]{:S(2)}) collective-permute-start(bf16[304,128]{1,0:T(8,128)(2,1)S(1)} %add_convert_fusion.1), channel_id=1, source_target_pairs={{0,1},{1,0},{2,3},{3,2},{4,5},{5,4},{6,7},{7,6},{16,17},{17,16},{1... | collective-permute-start | bytes 233480 | tf_op jit(solution)/shard_map/ppermute | solution.py:344
  56.0 1.7 %collective-permute-start.14 = (bf16[4,304,128]{2,1,0:T(8,128)(2,1)S(1)}, bf16[4,304,128]{2,1,0:T(8,128)(2,1)S(1)}, u32[]{:S(2)}, u32[]{:S(2)}) collective-permute-start(bf16[4,304,128]{2,1,0:T(8,128)(2,1)S(1)} %pad_maximum_fusion.mine_ref), channel_id=1, source_target_pairs={{0,8},{8,0},{1,9},{9,1},{2,10},{10,2},{3,11},{11,3},{4,12},{12,4},... | collective-permute-start | bytes 933896 | tf_op jit(solution)/shard_map/ppermute | solution.py:344
  (3 other events, 5.1 us)
